TPU v7x, 32 devices: a whole 2x2x4 slice. The times are simulated.
32 devices in a mesh: fsdp: 8 (over z, y), rep: 4 (over x, core).
Axes of the slice: x: 2, y: 2, z: 4, core: 2. Of those that a mesh axis runs over, the one named last changes fastest.
Arguments:
- tokens: bfloat16 [32, 1024, 768], P(('fsdp', 'rep')), may hold values from -6 to 6
- cotangent: bfloat16 [32, 1024, 768], P(('fsdp', 'rep')), may hold values from -6 to 6
- seq_lengths: int32 [32], P(('fsdp', 'rep')), may hold values from 256 to 1024, as said below
- token_positions: int32 [32, 1024], P(('fsdp', 'rep')), may hold values from 0 to 2046, as said below
- first_query: bfloat16 [768, 768], P('fsdp'), may hold values from -0.21875 to 0.21875
- first_key: bfloat16 [768, 768], P('fsdp'), may hold values from -0.21875 to 0.21875
- first_value: bfloat16 [768, 768], P('fsdp'), may hold values from -0.21875 to 0.21875
- first_output: bfloat16 [768, 768], P('fsdp'), may hold values from -1.75 to 1.75
- first_gate: bfloat16 [768, 2048], P('fsdp'), may hold values from -0.21875 to 0.21875
- first_up: bfloat16 [768, 2048], P('fsdp'), may hold values from -0.21875 to 0.21875
- first_down: bfloat16 [2048, 768], P('fsdp'), may hold values from -0.125 to 0.125
- first_attngain: bfloat16 [768], P('fsdp'), may hold values from 0.099609375 to 1.8984375
- first_ffngain: bfloat16 [768], P('fsdp'), may hold values from 0.099609375 to 1.8984375
- second_query: bfloat16 [768, 768], P('fsdp'), may hold values from -0.21875 to 0.21875
- second_key: bfloat16 [768, 768], P('fsdp'), may hold values from -0.21875 to 0.21875
- second_value: bfloat16 [768, 768], P('fsdp'), may hold values from -0.21875 to 0.21875
- second_output: bfloat16 [768, 768], P('fsdp'), may hold values from -1.75 to 1.75
- second_gate: bfloat16 [768, 2048], P('fsdp'), may hold values from -0.21875 to 0.21875
- second_up: bfloat16 [768, 2048], P('fsdp'), may hold values from -0.21875 to 0.21875
- second_down: bfloat16 [2048, 768], P('fsdp'), may hold values from -0.125 to 0.125
- second_attngain: bfloat16 [768], P('fsdp'), may hold values from 0.099609375 to 1.8984375
- second_ffngain: bfloat16 [768], P('fsdp'), may hold values from 0.099609375 to 1.8984375
Outputs:
- first_hidden: float32 [32, 1024, 768], P(('fsdp', 'rep'))
- second_hidden: float32 [32, 1024, 768], P(('fsdp', 'rep'))
- input_grad: float32 [32, 1024, 768], P(('fsdp', 'rep'))
- first_query_grad: float32 [768, 768], P('fsdp')
- first_key_grad: float32 [768, 768], P('fsdp')
- first_value_grad: float32 [768, 768], P('fsdp')
- first_output_grad: float32 [768, 768], P('fsdp')
- first_gate_grad: float32 [768, 2048], P('fsdp')
- first_up_grad: float32 [768, 2048], P('fsdp')
- first_down_grad: float32 [2048, 768], P('fsdp')
- first_attngain_grad: float32 [768], P('fsdp')
- first_ffngain_grad: float32 [768], P('fsdp')
- second_query_grad: float32 [768, 768], P('fsdp')
- second_key_grad: float32 [768, 768], P('fsdp')
- second_value_grad: float32 [768, 768], P('fsdp')
- second_output_grad: float32 [768, 768], P('fsdp')
- second_gate_grad: float32 [768, 2048], P('fsdp')
- second_up_grad: float32 [768, 2048], P('fsdp')
- second_down_grad: float32 [2048, 768], P('fsdp')
- second_attngain_grad: float32 [768], P('fsdp')
- second_ffngain_grad: float32 [768], P('fsdp')
Inputs may be any that keep to these rules, and one draw needn't show every extreme that they name: `seq_lengths`: keys at or past a sequence's length are masked; some sequence is 1024 long and some 1024/4. `token_positions`: each sequence starts at 0 and rises by 1 or 2 from token to token.
All inputs are finite; a program needn't handle non-finite values.
Results may differ from a plain program's by a relative error of at most 0.034.
Values may be sent and summed in bfloat16 or wider, within the bound.
No kernel may reach another device: no remote copies, remote signals or barrier semaphores. Data moves between devices by JAX's collectives and lax.ppermute only.
A program may use at most 384 MiB of HBM per device.

v0:
```python
import math

import jax
import jax.numpy as jnp
from jax import lax
from jax.sharding import PartitionSpec as P

HEADS = 12
HEAD_DIM = 64


epsilon = 1e-06
masked_score = -1e30


def rms_forward(values, scales):
    scaler = lax.rsqrt(jnp.mean(values * values, axis=-1, keepdims=True) + epsilon)
    return (values * scaler * scales, scaler)


def rms_backward(values, scaler, scales, upstream):
    weighted = upstream * scales
    inward = scaler * weighted - values * scaler**3 * jnp.mean(
        weighted * values, axis=-1, keepdims=True
    )
    return (inward, jnp.sum(upstream * values * scaler, axis=0))


def rope_tables(positions):
    even_steps = jnp.arange(0, HEAD_DIM, 2).astype(jnp.float32)
    inverse = jnp.exp(even_steps * (-math.log(10000.0) / HEAD_DIM))
    angles = positions.astype(jnp.float32)[..., None] * inverse
    cosine = jnp.concatenate([jnp.cos(angles), jnp.cos(angles)], axis=-1)[:, None, :]
    sine_table = jnp.concatenate([jnp.sin(angles), jnp.sin(angles)], axis=-1)[:, None, :]
    return (cosine, sine_table)


def rotate(values, cosine, sine_table):
    middle = values.shape[-1] // 2
    turned = jnp.concatenate([-values[..., middle:], values[..., :middle]], axis=-1)
    return values * cosine + turned * sine_table


def rotate_back(upstream, cosine, sine_table):
    middle = upstream.shape[-1] // 2
    moved = upstream * sine_table
    return upstream * cosine + jnp.concatenate([moved[..., middle:], -moved[..., :middle]], axis=-1)


def scores_of(query_rows, key_rows, first_row, length_now):
    raw = jnp.einsum(
        "qhd,khd->hqk", query_rows, key_rows, preferred_element_type=jnp.float32
    ) * HEAD_DIM ** (-0.5)
    row_ids = first_row + jnp.arange(query_rows.shape[0])[:, None]
    col_ids = jnp.arange(key_rows.shape[0])[None, :]
    valid = (col_ids <= row_ids) & (col_ids < length_now)
    return jnp.where(valid[None], raw, masked_score)


def attend_forward(queries, key_rows, value_rows, lengths):
    seq_span = queries.shape[1]
    block_rows = min(512, seq_span)

    def one_sequence(sequence):
        query_seq, key_seq, value_seq, length_now = sequence
        outputs = []
        log_parts = []
        for first_row in range(0, seq_span, block_rows):
            end_row = first_row + block_rows
            scores = scores_of(
                query_seq[first_row:end_row], key_seq[:end_row], first_row, length_now
            )
            row_max = jnp.max(scores, axis=-1, keepdims=True)
            shifted = jnp.exp(scores - row_max)
            row_sum = jnp.sum(shifted, axis=-1, keepdims=True)
            soft_low = (shifted / row_sum).astype(jnp.bfloat16)
            outputs.append(
                jnp.einsum(
                    "hqk,khd->qhd",
                    soft_low,
                    value_seq[:end_row],
                    preferred_element_type=jnp.float32,
                )
            )
            log_parts.append((row_max + jnp.log(row_sum))[..., 0])
        return (jnp.concatenate(outputs, 0).astype(jnp.bfloat16), jnp.concatenate(log_parts, 1))

    return lax.map(one_sequence, (queries, key_rows, value_rows, lengths))


def attend_backward(queries, key_rows, value_rows, log_sums, upstream, lengths):
    seq_span = queries.shape[1]
    block_rows = min(512, seq_span)
    factor = HEAD_DIM ** (-0.5)

    def one_sequence(sequence):
        query_seq, key_seq, value_seq, log_seq, grad_seq, length_now = sequence
        key_grad = jnp.zeros(key_seq.shape, jnp.float32)
        value_grad = jnp.zeros(value_seq.shape, jnp.float32)
        query_grads = []
        for first_row in range(0, seq_span, block_rows):
            end_row = first_row + block_rows
            query_block = query_seq[first_row:end_row]
            grad_block = grad_seq[first_row:end_row]
            scores = scores_of(query_block, key_seq[:end_row], first_row, length_now)
            soft_block = jnp.exp(scores - log_seq[:, first_row:end_row, None])
            grad_soft = jnp.einsum(
                "qhd,khd->hqk", grad_block, value_seq[:end_row], preferred_element_type=jnp.float32
            )
            value_add = jnp.einsum(
                "hqk,qhd->khd",
                soft_block.astype(jnp.bfloat16),
                grad_block,
                preferred_element_type=jnp.float32,
            )
            row_dot = jnp.sum(soft_block * grad_soft, axis=-1, keepdims=True)
            grad_score = (soft_block * (grad_soft - row_dot)).astype(jnp.bfloat16)
            query_grads.append(
                jnp.einsum(
                    "hqk,khd->qhd",
                    grad_score,
                    key_seq[:end_row],
                    preferred_element_type=jnp.float32,
                )
                * factor
            )
            key_add = (
                jnp.einsum(
                    "hqk,qhd->khd", grad_score, query_block, preferred_element_type=jnp.float32
                )
                * factor
            )
            padding = ((0, seq_span - end_row), (0, 0), (0, 0))
            key_grad = key_grad + jnp.pad(key_add, padding)
            value_grad = value_grad + jnp.pad(value_add, padding)
        return (jnp.concatenate(query_grads, 0), key_grad, value_grad)

    return lax.map(one_sequence, (queries, key_rows, value_rows, log_sums, upstream, lengths))


def attention_forward(inputs, weights, cosine, sine_table, lengths, shape_four):
    row_count = inputs.shape[0]
    heads_view = (row_count, HEADS, HEAD_DIM)
    queries = (
        rotate(
            jnp.dot(inputs, weights[0], preferred_element_type=jnp.float32).reshape(heads_view),
            cosine,
            sine_table,
        )
        .astype(jnp.bfloat16)
        .reshape(shape_four)
    )
    key_rows = (
        rotate(
            jnp.dot(inputs, weights[1], preferred_element_type=jnp.float32).reshape(heads_view),
            cosine,
            sine_table,
        )
        .astype(jnp.bfloat16)
        .reshape(shape_four)
    )
    value_rows = (
        jnp.dot(inputs, weights[2], preferred_element_type=jnp.float32)
        .astype(jnp.bfloat16)
        .reshape(shape_four)
    )
    mixed, log_sums = attend_forward(queries, key_rows, value_rows, lengths)
    mixed = mixed.reshape(row_count, -1)
    branch = jnp.dot(mixed, weights[3], preferred_element_type=jnp.float32)
    return (branch, (inputs, queries, key_rows, value_rows, mixed, log_sums))


def attention_backward(upstream, saved, weights, cosine, sine_table, lengths):
    inputs, queries, key_rows, value_rows, mixed, log_sums = saved
    row_count = inputs.shape[0]
    heads_view = (row_count, HEADS, HEAD_DIM)
    up_low = upstream.astype(jnp.bfloat16)
    output_grad = jnp.einsum("td,te->de", mixed, up_low, preferred_element_type=jnp.float32)
    mixed_grad = (
        jnp.einsum("te,de->td", up_low, weights[3], preferred_element_type=jnp.float32)
        .astype(jnp.bfloat16)
        .reshape(queries.shape)
    )
    query_rot, key_rot, value_back = attend_backward(
        queries, key_rows, value_rows, log_sums, mixed_grad, lengths
    )
    query_back = (
        rotate_back(query_rot.reshape(heads_view), cosine, sine_table)
        .reshape(row_count, -1)
        .astype(jnp.bfloat16)
    )
    key_back = (
        rotate_back(key_rot.reshape(heads_view), cosine, sine_table)
        .reshape(row_count, -1)
        .astype(jnp.bfloat16)
    )
    value_low = value_back.reshape(row_count, -1).astype(jnp.bfloat16)
    query_grad = jnp.einsum("td,te->de", inputs, query_back, preferred_element_type=jnp.float32)
    key_grad = jnp.einsum("td,te->de", inputs, key_back, preferred_element_type=jnp.float32)
    value_grad = jnp.einsum("td,te->de", inputs, value_low, preferred_element_type=jnp.float32)
    inward = jnp.einsum("te,de->td", query_back, weights[0], preferred_element_type=jnp.float32)
    inward = inward + jnp.einsum(
        "te,de->td", key_back, weights[1], preferred_element_type=jnp.float32
    )
    inward = inward + jnp.einsum(
        "te,de->td", value_low, weights[2], preferred_element_type=jnp.float32
    )
    return (inward, (query_grad, key_grad, value_grad, output_grad))


def feed_forward(inputs, weights):
    gated = jnp.dot(inputs, weights[4], preferred_element_type=jnp.float32)
    upward = jnp.dot(inputs, weights[5], preferred_element_type=jnp.float32)
    hidden = (jax.nn.silu(gated) * upward).astype(jnp.bfloat16)
    return (
        jnp.dot(hidden, weights[6], preferred_element_type=jnp.float32),
        (inputs, gated, upward, hidden),
    )


def feed_backward(upstream, saved, weights):
    inputs, gated, upward, hidden = saved
    up_low = upstream.astype(jnp.bfloat16)
    down_grad = jnp.einsum("tf,td->fd", hidden, up_low, preferred_element_type=jnp.float32)
    hidden_grad = jnp.einsum("td,fd->tf", up_low, weights[6], preferred_element_type=jnp.float32)
    sigmoid_gate = jax.nn.sigmoid(gated)
    up_back = (hidden_grad * (gated * sigmoid_gate)).astype(jnp.bfloat16)
    gate_back = (hidden_grad * upward * sigmoid_gate * (1.0 + gated * (1.0 - sigmoid_gate))).astype(
        jnp.bfloat16
    )
    gate_grad = jnp.einsum("td,tf->df", inputs, gate_back, preferred_element_type=jnp.float32)
    up_grad = jnp.einsum("td,tf->df", inputs, up_back, preferred_element_type=jnp.float32)
    inward = jnp.einsum("tf,df->td", gate_back, weights[4], preferred_element_type=jnp.float32)
    inward = inward + jnp.einsum(
        "tf,df->td", up_back, weights[5], preferred_element_type=jnp.float32
    )
    return (inward, (gate_grad, up_grad, down_grad))


def collect(query_w, key_w, value_w, output_w, gate_w, up_w, down_w, attn_gain, ffn_gain):
    return (
        lax.all_gather(query_w, "fsdp", axis=0, tiled=True),
        lax.all_gather(key_w, "fsdp", axis=0, tiled=True),
        lax.all_gather(value_w, "fsdp", axis=0, tiled=True),
        lax.all_gather(output_w, "fsdp", axis=0, tiled=True),
        lax.all_gather(gate_w, "fsdp", axis=0, tiled=True),
        lax.all_gather(up_w, "fsdp", axis=0, tiled=True),
        lax.all_gather(down_w, "fsdp", axis=0, tiled=True),
        lax.all_gather(attn_gain, "fsdp", axis=0, tiled=True),
        lax.all_gather(ffn_gain, "fsdp", axis=0, tiled=True),
    )


def collect_again(query_w, key_w, value_w, output_w, gate_w, up_w, down_w, attn_gain, ffn_gain):
    return (
        lax.all_gather(query_w, "fsdp", axis=0, tiled=True),
        lax.all_gather(key_w, "fsdp", axis=0, tiled=True),
        lax.all_gather(value_w, "fsdp", axis=0, tiled=True),
        lax.all_gather(output_w, "fsdp", axis=0, tiled=True),
        lax.all_gather(gate_w, "fsdp", axis=0, tiled=True),
        lax.all_gather(up_w, "fsdp", axis=0, tiled=True),
        lax.all_gather(down_w, "fsdp", axis=0, tiled=True),
        lax.all_gather(attn_gain, "fsdp", axis=0, tiled=True),
        lax.all_gather(ffn_gain, "fsdp", axis=0, tiled=True),
    )


def reduce_grads(query_g, key_g, value_g, output_g, gate_g, up_g, down_g, attn_g, ffn_g):
    shares = (
        lax.psum_scatter(
            query_g.astype(jnp.bfloat16), "fsdp", scatter_dimension=0, tiled=True
        ).astype(jnp.float32),
        lax.psum_scatter(
            key_g.astype(jnp.bfloat16), "fsdp", scatter_dimension=0, tiled=True
        ).astype(jnp.float32),
        lax.psum_scatter(
            value_g.astype(jnp.bfloat16), "fsdp", scatter_dimension=0, tiled=True
        ).astype(jnp.float32),
        lax.psum_scatter(
            output_g.astype(jnp.bfloat16), "fsdp", scatter_dimension=0, tiled=True
        ).astype(jnp.float32),
        lax.psum_scatter(
            gate_g.astype(jnp.bfloat16), "fsdp", scatter_dimension=0, tiled=True
        ).astype(jnp.float32),
        lax.psum_scatter(up_g.astype(jnp.bfloat16), "fsdp", scatter_dimension=0, tiled=True).astype(
            jnp.float32
        ),
        lax.psum_scatter(
            down_g.astype(jnp.bfloat16), "fsdp", scatter_dimension=0, tiled=True
        ).astype(jnp.float32),
        lax.psum_scatter(
            attn_g.astype(jnp.bfloat16), "fsdp", scatter_dimension=0, tiled=True
        ).astype(jnp.float32),
        lax.psum_scatter(
            ffn_g.astype(jnp.bfloat16), "fsdp", scatter_dimension=0, tiled=True
        ).astype(jnp.float32),
    )
    query_s, key_s, value_s, output_s, gate_s, up_s, down_s, attn_s, ffn_s = shares
    return (
        lax.psum(query_s.astype(jnp.bfloat16), "rep").astype(jnp.float32),
        lax.psum(key_s.astype(jnp.bfloat16), "rep").astype(jnp.float32),
        lax.psum(value_s.astype(jnp.bfloat16), "rep").astype(jnp.float32),
        lax.psum(output_s.astype(jnp.bfloat16), "rep").astype(jnp.float32),
        lax.psum(gate_s.astype(jnp.bfloat16), "rep").astype(jnp.float32),
        lax.psum(up_s.astype(jnp.bfloat16), "rep").astype(jnp.float32),
        lax.psum(down_s.astype(jnp.bfloat16), "rep").astype(jnp.float32),
        lax.psum(attn_s.astype(jnp.bfloat16), "rep").astype(jnp.float32),
        lax.psum(ffn_s.astype(jnp.bfloat16), "rep").astype(jnp.float32),
    )


def body(
    tokens,
    cotangent,
    seq_lengths,
    token_positions,
    first_query,
    first_key,
    first_value,
    first_output,
    first_gate,
    first_up,
    first_down,
    first_attngain,
    first_ffngain,
    second_query,
    second_key,
    second_value,
    second_output,
    second_gate,
    second_up,
    second_down,
    second_attngain,
    second_ffngain,
):
    seqs_here, seq_span, width = tokens.shape
    row_count = seqs_here * seq_span
    shape_four = (seqs_here, seq_span, HEADS, HEAD_DIM)
    cosine, sine_table = rope_tables(token_positions.reshape(row_count))
    flat_tokens = tokens.reshape(row_count, width)
    weights_one = collect(
        first_query,
        first_key,
        first_value,
        first_output,
        first_gate,
        first_up,
        first_down,
        first_attngain,
        first_ffngain,
    )
    branch_one, attn_saved_one = attention_forward(
        flat_tokens, weights_one, cosine, sine_table, seq_lengths, shape_four
    )
    resid_one = flat_tokens.astype(jnp.float32) + branch_one
    normed, scaler_a = rms_forward(resid_one, weights_one[7].astype(jnp.float32))
    ffn_one, ffn_saved_one = feed_forward(normed.astype(jnp.bfloat16), weights_one)
    resid_two = normed + ffn_one
    first_out, scaler_b = rms_forward(resid_two, weights_one[8].astype(jnp.float32))
    weights_two = collect(
        second_query,
        second_key,
        second_value,
        second_output,
        second_gate,
        second_up,
        second_down,
        second_attngain,
        second_ffngain,
    )
    pre_attn, scaler_c = rms_forward(first_out, weights_two[7].astype(jnp.float32))
    branch_two, attn_saved_two = attention_forward(
        pre_attn.astype(jnp.bfloat16), weights_two, cosine, sine_table, seq_lengths, shape_four
    )
    resid_three = first_out + branch_two
    pre_ffn, scaler_d = rms_forward(resid_three, weights_two[8].astype(jnp.float32))
    ffn_two, ffn_saved_two = feed_forward(pre_ffn.astype(jnp.bfloat16), weights_two)
    second_out = resid_three + ffn_two
    back_two = collect_again(
        second_query,
        second_key,
        second_value,
        second_output,
        second_gate,
        second_up,
        second_down,
        second_attngain,
        second_ffngain,
    )
    upstream = cotangent.reshape(row_count, width).astype(jnp.float32)
    hidden_two, ffn_grads_two = feed_backward(upstream, ffn_saved_two, back_two)
    resid_back, ffn_gain_two = rms_backward(
        resid_three, scaler_d, back_two[8].astype(jnp.float32), hidden_two
    )
    resid_back = upstream + resid_back
    attn_in_two, attn_grads_two = attention_backward(
        resid_back, attn_saved_two, back_two, cosine, sine_table, seq_lengths
    )
    first_back, attn_gain_two = rms_backward(
        first_out, scaler_c, back_two[7].astype(jnp.float32), attn_in_two
    )
    first_back = resid_back + first_back
    grads_two = reduce_grads(
        attn_grads_two[0],
        attn_grads_two[1],
        attn_grads_two[2],
        attn_grads_two[3],
        ffn_grads_two[0],
        ffn_grads_two[1],
        ffn_grads_two[2],
        attn_gain_two,
        ffn_gain_two,
    )
    back_one = collect_again(
        first_query,
        first_key,
        first_value,
        first_output,
        first_gate,
        first_up,
        first_down,
        first_attngain,
        first_ffngain,
    )
    resid_two_back, ffn_gain_one = rms_backward(
        resid_two, scaler_b, back_one[8].astype(jnp.float32), first_back
    )
    hidden_one, ffn_grads_one = feed_backward(resid_two_back, ffn_saved_one, back_one)
    normed_back = resid_two_back + hidden_one
    resid_one_back, attn_gain_one = rms_backward(
        resid_one, scaler_a, back_one[7].astype(jnp.float32), normed_back
    )
    tokens_back, attn_grads_one = attention_backward(
        resid_one_back, attn_saved_one, back_one, cosine, sine_table, seq_lengths
    )
    input_grad = resid_one_back + tokens_back
    grads_one = reduce_grads(
        attn_grads_one[0],
        attn_grads_one[1],
        attn_grads_one[2],
        attn_grads_one[3],
        ffn_grads_one[0],
        ffn_grads_one[1],
        ffn_grads_one[2],
        attn_gain_one,
        ffn_gain_one,
    )
    return (
        first_out.reshape(tokens.shape),
        second_out.reshape(tokens.shape),
        input_grad.reshape(tokens.shape),
        grads_one[0],
        grads_one[1],
        grads_one[2],
        grads_one[3],
        grads_one[4],
        grads_one[5],
        grads_one[6],
        grads_one[7],
        grads_one[8],
        grads_two[0],
        grads_two[1],
        grads_two[2],
        grads_two[3],
        grads_two[4],
        grads_two[5],
        grads_two[6],
        grads_two[7],
        grads_two[8],
    )


def solution(mesh):
    placed = (
        P(("fsdp", "rep"), None, None),
        P(("fsdp", "rep"), None, None),
        P(("fsdp", "rep")),
        P(("fsdp", "rep"), None),
        P("fsdp", None),
        P("fsdp", None),
        P("fsdp", None),
        P("fsdp", None),
        P("fsdp", None),
        P("fsdp", None),
        P("fsdp", None),
        P("fsdp"),
        P("fsdp"),
        P("fsdp", None),
        P("fsdp", None),
        P("fsdp", None),
        P("fsdp", None),
        P("fsdp", None),
        P("fsdp", None),
        P("fsdp", None),
        P("fsdp"),
        P("fsdp"),
    )
    return jax.shard_map(
        body,
        mesh=mesh,
        in_specs=placed,
        out_specs=(
            P(("fsdp", "rep"), None, None),
            P(("fsdp", "rep"), None, None),
            P(("fsdp", "rep"), None, None),
            P("fsdp", None),
            P("fsdp", None),
            P("fsdp", None),
            P("fsdp", None),
            P("fsdp", None),
            P("fsdp", None),
            P("fsdp", None),
            P("fsdp"),
            P("fsdp"),
            P("fsdp", None),
            P("fsdp", None),
            P("fsdp", None),
            P("fsdp", None),
            P("fsdp", None),
            P("fsdp", None),
            P("fsdp", None),
            P("fsdp"),
            P("fsdp"),
        ),
        check_vma=False,
    )
```

profile of v0, /device:TPU:0, one launch (start us, length us, event | category | flops | bytes accessed | tf_op | source)
XLA Modules:
  0.0 2041.9 jit_solution(3337879552946595465)
XLA Ops:
  19.7 23.6 %all-reduce.13 = (bf16[768]{0:T(1024)(128)(2,1)S(1)}, bf16[768]{0:T(1024)(128)(2,1)S(1)}, bf16[768]{0:T(1024)(128)(2,1)S(1)}, bf16[768]{0:T(1024)(128)(2,1)S(1)}) all-reduce(bf16[768]{0:T(1024)(128)(2,1)S(1)} %dynamic-update-slice, bf16[768]{0:T(1024)(128)(2,1)S(1)} %dynamic-update-slice.2, ...), channel_id=1, replica_groups=mesh['fsdp'=8,'rep'=4] {'fsdp'}, use_global_device_ids=true, to_apply=%add.4 | all-reduce | flops 3072 | bytes 12288
  56.5 39.7 %all-gather.17.cloned.1.call-done = bf16[768,768]{1,0:T(8,128)(2,1)} async-done(((bf16[96,768]{1,0:T(8,128)(2,1)}), bf16[768,768]{1,0:T(8,128)(2,1)}) %all-gather.17.cloned.1.call-update) | async-done | bytes 1179664 | tf_op jit(solution)/shard_map/all_gather | solution.py:242
  98.6 39.7 %all-gather.15.cloned.1.call-done = bf16[768,768]{1,0:T(8,128)(2,1)} async-done(((bf16[96,768]{1,0:T(8,128)(2,1)}), bf16[768,768]{1,0:T(8,128)(2,1)}) %all-gather.15.cloned.1.call-update) | async-done | bytes 1179664 | tf_op jit(solution)/shard_map/all_gather | solution.py:244
  186.1 19.5 fusion.95
  210.8 30.6 %all-gather.23.cloned.1.call-done = bf16[768,2048]{1,0:T(8,128)(2,1)} async-done(((bf16[96,2048]{1,0:T(8,128)(2,1)}), bf16[768,2048]{1,0:T(8,128)(2,1)}) %all-gather.23.cloned.1.call-update) | async-done | bytes 3145744 | tf_op jit(solution)/shard_map/all_gather | solution.py:246
  249.1 53.4 %all-gather.25.cloned.1.call-done = bf16[768,2048]{1,0:T(8,128)(2,1)} async-done(((bf16[96,2048]{1,0:T(8,128)(2,1)}), bf16[768,2048]{1,0:T(8,128)(2,1)}) %all-gather.25.cloned.1.call-update) | async-done | bytes 3145744 | tf_op jit(solution)/shard_map/all_gather | solution.py:247
  313.3 50.6 %all-gather.27.cloned.1.call-done = bf16[2048,768]{1,0:T(8,128)(2,1)} async-done(((bf16[256,768]{1,0:T(8,128)(2,1)}), bf16[2048,768]{1,0:T(8,128)(2,1)}) %all-gather.27.cloned.1.call-update) | async-done | bytes 3145744 | tf_op jit(solution)/shard_map/all_gather | solution.py:248
  375.2 30.6 %all-gather.31.cloned.1.call-done = bf16[768,768]{1,0:T(8,128)(2,1)} async-done(((bf16[96,768]{1,0:T(8,128)(2,1)}), bf16[768,768]{1,0:T(8,128)(2,1)}) %all-gather.31.cloned.1.call-update) | async-done | bytes 1179664 | tf_op jit(solution)/shard_map/all_gather | solution.py:242
  412.5 35.3 %all-gather.33.cloned.1.call-done = bf16[768,768]{1,0:T(8,128)(2,1)} async-done(((bf16[96,768]{1,0:T(8,128)(2,1)}), bf16[768,768]{1,0:T(8,128)(2,1)}) %all-gather.33.cloned.1.call-update) | async-done | bytes 1179664 | tf_op jit(solution)/shard_map/all_gather | solution.py:243
  472.5 17.2 all-gather.29.cloned.1.call-done
  540.1 53.0 %all-gather.39.cloned.1.call-done = bf16[768,2048]{1,0:T(8,128)(2,1)} async-done(((bf16[96,2048]{1,0:T(8,128)(2,1)}), bf16[768,2048]{1,0:T(8,128)(2,1)}) %all-gather.39.cloned.1.call-update) | async-done | bytes 3145744 | tf_op jit(solution)/shard_map/all_gather | solution.py:247
  600.8 53.6 %all-gather.37.cloned.1.call-done = bf16[768,2048]{1,0:T(8,128)(2,1)} async-done(((bf16[96,2048]{1,0:T(8,128)(2,1)}), bf16[768,2048]{1,0:T(8,128)(2,1)}) %all-gather.37.cloned.1.call-update) | async-done | bytes 3145744 | tf_op jit(solution)/shard_map/all_gather | solution.py:246
  662.0 53.5 %all-gather.41.cloned.1.call-done = bf16[2048,768]{1,0:T(8,128)(2,1)} async-done(((bf16[256,768]{1,0:T(8,128)(2,1)}), bf16[2048,768]{1,0:T(8,128)(2,1)}) %all-gather.41.cloned.1.call-update) | async-done | bytes 3145744 | tf_op jit(solution)/shard_map/all_gather | solution.py:248
  769.7 21.8 %multiply_reduce_fusion.1 = (f32[12,512]{1,0:T(8,128)S(1)}, f32[12,512,1024]{2,1,0:T(8,128)}) fusion(f32[12,512]{1,0:T(8,128)S(1)} %log_add_fusion.2, f32[12,512,1024]{2,1,0:T(8,128)} %get-tuple-element.259, pred[512,1024]{1,0:T(8,128)(4,1)S(1)} %copy-done.8, bf16[512,12,64]{0,2,1:T(8,128)(2,1)S(1)} %bitcast.270, bf16[1024,12,64]{0,2,1:T(8,128)(2,1)S(1)} %bitcast.259), kind=kOutput, calls=%fused_computation.4 | convolution fusion | flops 836757504 | bytes 53264384 | tf_op jit(solution)/shard_map/while/body/eval_jaxpr/qhd,khd->hqk/dot_general | solution.py:107
  791.5 13.3 fusion.45
  804.8 17.0 multiply_convert_fusion.1
  906.7 21.6 %multiply_reduce_fusion = (f32[12,512]{1,0:T(8,128)S(1)}, f32[12,512,1024]{2,1,0:T(8,128)}) fusion(f32[12,512]{1,0:T(8,128)S(1)} %copy-done.80, f32[12,512,1024]{2,1,0:T(8,128)} %get-tuple-element.249, pred[512,1024]{1,0:T(8,128)(4,1)S(1)} %copy-done.10, bf16[512,12,64]{0,2,1:T(8,128)(2,1)S(1)} %bitcast.268, bf16[1024,12,64]{0,2,1:T(8,128)(2,1)S(1)} %bitcast.257), kind=kOutput, calls=%fused_computation.1 | convolution fusion | flops 836757504 | bytes 53264384 | tf_op jit(solution)/shard_map/while/body/eval_jaxpr/qhd,khd->hqk/dot_general | solution.py:107
  943.5 17.6 multiply_convert_fusion
  1074.5 64.6 %reduce-scatter.45.cloned.1.call-done = bf16[96,768]{1,0:T(8,128)(2,1)} async-done(((bf16[768,768]{1,0:T(8,128)(2,1)}), bf16[96,768]{1,0:T(8,128)(2,1)}) %reduce-scatter.45.cloned.1.call-update) | async-done | bytes 147472
  1140.8 64.5 %reduce-scatter.35.cloned.1.call-done = bf16[96,768]{1,0:T(8,128)(2,1)} async-done(((bf16[768,768]{1,0:T(8,128)(2,1)}), bf16[96,768]{1,0:T(8,128)(2,1)}) %reduce-scatter.35.cloned.1.call-update) | async-done | bytes 147472 | tf_op jit(solution)/shard_map/reduce_scatter | solution.py:279
  1205.3 66.4 %reduce-scatter.33.cloned.1.call-done = bf16[96,768]{1,0:T(8,128)(2,1)} async-done(((bf16[768,768]{1,0:T(8,128)(2,1)}), bf16[96,768]{1,0:T(8,128)(2,1)}) %reduce-scatter.33.cloned.1.call-update) | async-done | bytes 147472 | tf_op jit(solution)/shard_map/reduce_scatter | solution.py:276
  1271.7 66.3 %reduce-scatter.31.cloned.1.call-done = bf16[96,768]{1,0:T(8,128)(2,1)} async-done(((bf16[768,768]{1,0:T(8,128)(2,1)}), bf16[96,768]{1,0:T(8,128)(2,1)}) %reduce-scatter.31.cloned.1.call-update) | async-done | bytes 147472 | tf_op jit(solution)/shard_map/reduce_scatter | solution.py:273
  1338.1 66.5 %reduce-scatter.29.cloned.1.call-done = bf16[96,768]{1,0:T(8,128)(2,1)} async-done(((bf16[768,768]{1,0:T(8,128)(2,1)}), bf16[96,768]{1,0:T(8,128)(2,1)}) %reduce-scatter.29.cloned.1.call-update) | async-done | bytes 147472 | tf_op jit(solution)/shard_map/reduce_scatter | solution.py:270
  1404.6 66.5 %reduce-scatter.21.cloned.1.call-done = bf16[96,768]{1,0:T(8,128)(2,1)} async-done(((bf16[768,768]{1,0:T(8,128)(2,1)}), bf16[96,768]{1,0:T(8,128)(2,1)}) %reduce-scatter.21.cloned.1.call-update) | async-done | bytes 147472 | tf_op jit(solution)/shard_map/reduce_scatter | solution.py:279
  1471.0 76.9 %reduce-scatter.41.cloned.1.call-done = bf16[256,768]{1,0:T(8,128)(2,1)} async-done(((bf16[2048,768]{1,0:T(8,128)(2,1)}), bf16[256,768]{1,0:T(8,128)(2,1)}) %reduce-scatter.41.cloned.1.call-update) | async-done | bytes 393232 | tf_op jit(solution)/shard_map/reduce_scatter | solution.py:288
  1547.9 77.0 %reduce-scatter.37.cloned.1.call-done = bf16[96,2048]{1,0:T(8,128)(2,1)} async-done(((bf16[768,2048]{1,0:T(8,128)(2,1)}), bf16[96,2048]{1,0:T(8,128)(2,1)}) %reduce-scatter.37.cloned.1.call-update) | async-done | bytes 393232 | tf_op jit(solution)/shard_map/reduce_scatter | solution.py:282
  1624.9 77.2 %reduce-scatter.39.cloned.1.call-done = bf16[96,2048]{1,0:T(8,128)(2,1)} async-done(((bf16[768,2048]{1,0:T(8,128)(2,1)}), bf16[96,2048]{1,0:T(8,128)(2,1)}) %reduce-scatter.39.cloned.1.call-update) | async-done | bytes 393232 | tf_op jit(solution)/shard_map/reduce_scatter | solution.py:285
  1702.1 77.5 %reduce-scatter.23.cloned.1.call-done = bf16[96,2048]{1,0:T(8,128)(2,1)} async-done(((bf16[768,2048]{1,0:T(8,128)(2,1)}), bf16[96,2048]{1,0:T(8,128)(2,1)}) %reduce-scatter.23.cloned.1.call-update) | async-done | bytes 393232 | tf_op jit(solution)/shard_map/reduce_scatter | solution.py:282
  1779.6 76.8 %reduce-scatter.25.cloned.1.call-done = bf16[96,2048]{1,0:T(8,128)(2,1)} async-done(((bf16[768,2048]{1,0:T(8,128)(2,1)}), bf16[96,2048]{1,0:T(8,128)(2,1)}) %reduce-scatter.25.cloned.1.call-update) | async-done | bytes 393232 | tf_op jit(solution)/shard_map/reduce_scatter | solution.py:285
  1856.4 77.2 %reduce-scatter.27.cloned.1.call-done = bf16[256,768]{1,0:T(8,128)(2,1)} async-done(((bf16[2048,768]{1,0:T(8,128)(2,1)}), bf16[256,768]{1,0:T(8,128)(2,1)}) %reduce-scatter.27.cloned.1.call-update) | async-done | bytes 393232 | tf_op jit(solution)/shard_map/reduce_scatter | solution.py:288
  1950.0 19.8 all-reduce.12
  1989.1 27.6 %all-reduce.18.cloned.1.call-done = (bf16[96,768]{0,1:T(8,128)(2,1)}, bf16[96,768]{0,1:T(8,128)(2,1)}, bf16[96,768]{0,1:T(8,128)(2,1)}, bf16[96,768]{1,0:T(8,128...) async-done(((bf16[96,768]{0,1:T(8,128)(2,1)}, ...) | async-done | bytes 3538960 | tf_op jit(solution)/shard_map/psum | solution.py:300
  (488 shorter events, 527.6 us)
Async XLA Ops:
  7.3 46.9 %all-gather.19.cloned.1.call-start = ((), (), s32[]{:S(2)}) async-start(), calls=%async_computation.16 | async-start | bytes 1327104 | tf_op jit(solution)/shard_map/all_gather | solution.py:243
  8.0 88.2 %all-gather.17.cloned.1.call-start = ((), (), s32[]{:S(2)}) async-start(), calls=%async_computation.15 | async-start | bytes 1327104 | tf_op jit(solution)/shard_map/all_gather | solution.py:242
  8.7 129.5 %all-gather.15.cloned.1.call-start = ((), (), s32[]{:S(2)}) async-start(), calls=%async_computation.14 | async-start | bytes 1327104 | tf_op jit(solution)/shard_map/all_gather | solution.py:244
  9.5 196.2 %all-gather.21.cloned.1.call-start = ((), (), s32[]{:S(2)}) async-start(), calls=%async_computation.17 | async-start | bytes 1327104 | tf_op jit(solution)/shard_map/all_gather | solution.py:245
  10.0 231.4 %all-gather.23.cloned.1.call-start = ((), (), s32[]{:S(2)}) async-start(), calls=%async_computation.18 | async-start | bytes 3538944 | tf_op jit(solution)/shard_map/all_gather | solution.py:246
  10.6 291.9 %all-gather.25.cloned.1.call-start = ((), (), s32[]{:S(2)}) async-start(), calls=%async_computation.19 | async-start | bytes 3538944 | tf_op jit(solution)/shard_map/all_gather | solution.py:247
  11.2 352.6 %all-gather.27.cloned.1.call-start = ((), (), s32[]{:S(2)}) async-start(), calls=%async_computation.20 | async-start | bytes 3538944 | tf_op jit(solution)/shard_map/all_gather | solution.py:248
  12.0 393.8 %all-gather.31.cloned.1.call-start = ((), (), s32[]{:S(2)}) async-start(), calls=%async_computation.22 | async-start | bytes 1327104 | tf_op jit(solution)/shard_map/all_gather | solution.py:242
  12.7 435.1 %all-gather.33.cloned.1.call-start = ((), (), s32[]{:S(2)}) async-start(), calls=%async_computation.23 | async-start | bytes 1327104 | tf_op jit(solution)/shard_map/all_gather | solution.py:243
  13.5 476.2 %all-gather.29.cloned.1.call-start = ((), (), s32[]{:S(2)}) async-start(), calls=%async_computation.21 | async-start | bytes 1327104 | tf_op jit(solution)/shard_map/all_gather | solution.py:244
  14.0 520.4 %all-gather.35.cloned.1.call-start = ((), (), s32[]{:S(2)}) async-start(), calls=%async_computation.24 | async-start | bytes 1327104 | tf_op jit(solution)/shard_map/all_gather | solution.py:245
  14.8 578.3 %all-gather.39.cloned.1.call-start = ((), (), s32[]{:S(2)}) async-start(), calls=%async_computation.26 | async-start | bytes 3538944 | tf_op jit(solution)/shard_map/all_gather | solution.py:247
  15.4 639.0 %all-gather.37.cloned.1.call-start = ((), (), s32[]{:S(2)}) async-start(), calls=%async_computation.25 | async-start | bytes 3538944 | tf_op jit(solution)/shard_map/all_gather | solution.py:246
  16.1 699.4 %all-gather.41.cloned.1.call-start = ((), (), s32[]{:S(2)}) async-start(), calls=%async_computation.27 | async-start | bytes 3538944 | tf_op jit(solution)/shard_map/all_gather | solution.py:248
  16.7 1045.5 %reduce-scatter.47.cloned.1.call-start = ((), (), s32[]{:S(2)}) async-start(), calls=%async_computation.41 | async-start | bytes 1327104
  43.3 320.6 %copy-start.95 = (f32[768]{0:T(1024)}, f32[768]{0:T(1024)S(1)}, u32[]{:S(2)}) copy-start(f32[768]{0:T(1024)S(1)} %convert_element_type.366) | copy-start | bytes 9220
  43.3 491.2 %copy-start.83 = (f32[768]{0:T(1024)}, f32[768]{0:T(1024)S(1)}, u32[]{:S(2)}) copy-start(f32[768]{0:T(1024)S(1)} %convert_element_type.369) | copy-start | bytes 9220
  43.3 330.1 %copy-start.89 = (f32[768]{0:T(1024)}, f32[768]{0:T(1024)S(1)}, u32[]{:S(2)}) copy-start(f32[768]{0:T(1024)S(1)} %convert_element_type.370) | copy-start | bytes 9220
  943.5 129.3 %reduce-scatter.43.cloned.1.call-start = ((), (), s32[]{:S(2)}) async-start(), calls=%async_computation.39 | async-start | bytes 1327104
  983.0 156.1 %reduce-scatter.45.cloned.1.call-start = ((), (), s32[]{:S(2)}) async-start(), calls=%async_computation.40 | async-start | bytes 1327104
  989.8 215.6 %reduce-scatter.35.cloned.1.call-start = ((), (), s32[]{:S(2)}) async-start(), calls=%async_computation.35 | async-start | bytes 1327104 | tf_op jit(solution)/shard_map/reduce_scatter | solution.py:279
  994.6 277.1 %reduce-scatter.33.cloned.1.call-start = ((), (), s32[]{:S(2)}) async-start(), calls=%async_computation.34 | async-start | bytes 1327104 | tf_op jit(solution)/shard_map/reduce_scatter | solution.py:276
  999.5 338.6 %reduce-scatter.31.cloned.1.call-start = ((), (), s32[]{:S(2)}) async-start(), calls=%async_computation.33 | async-start | bytes 1327104 | tf_op jit(solution)/shard_map/reduce_scatter | solution.py:273
  1003.9 400.7 %reduce-scatter.29.cloned.1.call-start = ((), (), s32[]{:S(2)}) async-start(), calls=%async_computation.32 | async-start | bytes 1327104 | tf_op jit(solution)/shard_map/reduce_scatter | solution.py:270
  1008.3 462.7 %reduce-scatter.21.cloned.1.call-start = ((), (), s32[]{:S(2)}) async-start(), calls=%async_computation.28 | async-start | bytes 1327104 | tf_op jit(solution)/shard_map/reduce_scatter | solution.py:279
  1013.2 534.7 %reduce-scatter.41.cloned.1.call-start = ((), (), s32[]{:S(2)}) async-start(), calls=%async_computation.38 | async-start | bytes 3538944 | tf_op jit(solution)/shard_map/reduce_scatter | solution.py:288
  1021.1 603.8 %reduce-scatter.37.cloned.1.call-start = ((), (), s32[]{:S(2)}) async-start(), calls=%async_computation.36 | async-start | bytes 3538944 | tf_op jit(solution)/shard_map/reduce_scatter | solution.py:282
  1029.0 673.1 %reduce-scatter.39.cloned.1.call-start = ((), (), s32[]{:S(2)}) async-start(), calls=%async_computation.37 | async-start | bytes 3538944 | tf_op jit(solution)/shard_map/reduce_scatter | solution.py:285
  1037.0 742.6 %reduce-scatter.23.cloned.1.call-start = ((), (), s32[]{:S(2)}) async-start(), calls=%async_computation.29 | async-start | bytes 3538944 | tf_op jit(solution)/shard_map/reduce_scatter | solution.py:282
  1044.9 811.5 %reduce-scatter.25.cloned.1.call-start = ((), (), s32[]{:S(2)}) async-start(), calls=%async_computation.30 | async-start | bytes 3538944 | tf_op jit(solution)/shard_map/reduce_scatter | solution.py:285
  1052.7 880.8 %reduce-scatter.27.cloned.1.call-start = ((), (), s32[]{:S(2)}) async-start(), calls=%async_computation.31 | async-start | bytes 3538944 | tf_op jit(solution)/shard_map/reduce_scatter | solution.py:288
  1061.2 955.4 %all-reduce.18.cloned.1.call-start = ((), (), s32[]{:S(2)}) async-start(), calls=%async_computation.42 | async-start | bytes 7372800 | tf_op jit(solution)/shard_map/psum | solution.py:300
  (126 other events, 1916.3 us)
Sparse Core Ops, SparseCore 0:
  10.3 43.8 all-gather.18
  56.3 39.8 all-gather.16
  98.4 39.8 all-gather.14
  140.3 39.8 all-gather.20
  182.2 59.2 all-gather.22
  243.5 59.0 all-gather.24
  304.7 59.0 all-gather.26
  366.0 39.6 all-gather.30
  407.9 39.8 all-gather.32
  449.8 39.8 all-gather.28
  491.9 39.8 all-gather.34
  533.8 59.2 all-gather.38
  595.3 59.0 all-gather.36
  656.4 59.0 all-gather.40
  943.6 62.7 reduce-scatter.46
  1009.7 63.0 reduce-scatter.42
  1076.0 63.0 reduce-scatter.44
  1142.3 62.9 reduce-scatter.34
  1208.7 62.9 reduce-scatter.32
  1275.0 63.0 reduce-scatter.30
  1341.5 63.0 reduce-scatter.28
  1408.0 63.0 reduce-scatter.20
  1474.6 73.2 reduce-scatter.40
  1551.3 73.5 reduce-scatter.36
  1628.5 73.5 reduce-scatter.38
  1706.1 73.4 reduce-scatter.22
  1783.0 73.3 reduce-scatter.24
  1860.0 73.5 reduce-scatter.26
  1937.6 79.0 all-reduce.17
where the time goes:
time: 2050 us; the launch traced here: 2040 us
  waiting for transfers between devices  1360 us (66%)
  matrix products  407 us (20%)
  other arithmetic  135 us (7%)
  local copies, waits for them, and re-layouts  66.4 us (3%)
  blocking collectives  49.1 us (2%)
    reduce_scatter x2, waiting for transfers between devices, reduce_grads(): lax.psum_scatter(gate_g.astype(jnp.bfloat16), 'fsdp', scatter_dimension=0...  155 us
    reduce_scatter x2, waiting for transfers between devices, reduce_grads(): lax.psum_scatter(down_g.astype(jnp.bfloat16), 'fsdp', scatter_dimension=0...  154 us
    reduce_scatter x2, waiting for transfers between devices, reduce_grads(): lax.psum_scatter(up_g.astype(jnp.bfloat16), 'fsdp', scatter_dimension=0,...  154 us
    reduce_scatter x2, waiting for transfers between devices, reduce_grads(): lax.psum_scatter(output_g.astype(jnp.bfloat16), 'fsdp', scatter_dimension...  131 us
    all_gather x2, waiting for transfers between devices, collect(): lax.all_gather(up_w, 'fsdp', axis=0, tiled=True)  106 us
    all_gather x2, waiting for transfers between devices, collect(): lax.all_gather(down_w, 'fsdp', axis=0, tiled=True)  104 us
    all_gather x2, waiting for transfers between devices, collect(): lax.all_gather(gate_w, 'fsdp', axis=0, tiled=True)  84.2 us
    unnamed x32, waiting for transfers between devices  82.4 us
  transfers between devices with their start and end apart: 29, of which 26 were waited for; matrix products, arithmetic and copies ran while one was open for 17% of the time, Pallas kernels for 0%

commit v1 on v0

v1 whole, which is shorter than its diff:
```python
import functools
import math

import jax
import jax.numpy as jnp
from jax import lax
from jax.experimental import pallas as pl
from jax.experimental.pallas import tpu as pltpu
from jax.sharding import PartitionSpec as P

HEAD_DIM = 64

epsilon = 1e-06
masked_score = -1e30


class Grid:
    def __init__(self, fsdp, rep):
        self.zs = fsdp // 2
        self.rep = rep

    def flat(self, z, y, x, c):
        return (z * 2 + y) * self.rep + x * 2 + c

    def pairs(self, move):
        out = []
        for z in range(self.zs):
            for y in range(2):
                for x in range(2):
                    for c in range(2):
                        out.append((self.flat(z, y, x, c), self.flat(*move(z, y, x, c))))
        return out


AXES = ("fsdp", "rep")


def send(grid, value, move):
    return lax.ppermute(value, AXES, grid.pairs(move))


def first_flip(z, y, x, c):
    return (z, y, 1 - x, c) if c == 0 else (z, 1 - y, x, c)


def second_flip(z, y, x, c):
    return (z, 1 - y, x, c) if c == 0 else (z, y, 1 - x, c)


def core_flip(z, y, x, c):
    return (z, y, x, 1 - c)


def x_flip(z, y, x, c):
    return (z, y, 1 - x, c)


def y_flip(z, y, x, c):
    return (z, 1 - y, x, c)

BLOCK = 256
PAIR = 2 * HEAD_DIM
VMEM = 60 * 1024 * 1024
F32 = jnp.float32
LOW = jnp.bfloat16


def dot(one, two):
    return jnp.dot(one, two, preferred_element_type=F32)


def dot_nt(one, two):
    return lax.dot_general(one, two, (((1,), (1,)), ((), ())), preferred_element_type=F32)


def dot_tn(one, two):
    return lax.dot_general(one, two, (((0,), (0,)), ((), ())), preferred_element_type=F32)


def inverse_rms(values):
    return lax.rsqrt(jnp.mean(values * values, axis=-1, keepdims=True) + epsilon)


def norm_back(values, scales, upstream):
    inv = inverse_rms(values)
    weighted = upstream * scales
    inner = jnp.mean(weighted * values, axis=-1, keepdims=True)
    return inv * weighted - values * (inv * inv * inv) * inner, upstream * values * inv


def fold_rows(values):
    return jnp.sum(values.reshape(values.shape[0] // 8, 8, values.shape[1]), axis=0)


def silu_parts(gate):
    sig = 1.0 / (1.0 + jnp.exp(-gate))
    return sig, gate * sig


def piece_place(at_ref, which, k, zs):
    z, y, x, c = at_ref[0], at_ref[1], at_ref[2], at_ref[3]
    cc = c if which < 4 else 1 - c
    first, second = which % 2, (which % 4) // 2
    flip_x = jnp.where(cc == 0, first, second)
    flip_y = jnp.where(cc == 0, second, first)
    zz = lax.rem(z + zs - k, zs)
    return zz * 2 + jnp.where(flip_y == 1, 1 - y, y), jnp.where(flip_x == 1, 1 - x, x), cc


def weight_copies(at_ref, pieces, w_ref, sems):
    if len(pieces) == 1:
        return [pltpu.make_async_copy(pieces[0], w_ref, sems.at[0])]
    zs, rows, _ = pieces[0].shape
    copies = []
    for which in range(8):
        for k in range(zs):
            shard, x, c = piece_place(at_ref, which, k, zs)
            row = pl.multiple_of(shard * (2 * rows) + x * rows, 16)
            copies.append(
                pltpu.make_async_copy(
                    pieces[which].at[k],
                    w_ref.at[c, pl.ds(row, rows), :],
                    sems.at[which * zs + k],
                )
            )
    return copies


def weight_shape(pieces):
    if len(pieces) == 1:
        return pieces[0].shape
    zs, rows, cols = pieces[0].shape
    return (2, zs * 4 * rows, cols)


def weight_scratch(pieces):
    copies = 1 if len(pieces) == 1 else 8 * pieces[0].shape[0]
    return [pltpu.VMEM(weight_shape(pieces), LOW), pltpu.SemaphoreType.DMA((copies,))]


def load_first(at_ref, *weights):
    @pl.when(pl.program_id(0) == 0)
    def _():
        copies = []
        for pieces, w_ref, sems in weights:
            copies += weight_copies(at_ref, pieces, w_ref, sems)
        for copy in copies:
            copy.start()
        for copy in copies:
            copy.wait()


ANYWHERE = pl.BlockSpec(memory_space=pl.ANY)


def rows_spec(cols, block=BLOCK):
    return pl.BlockSpec((block, cols), lambda i, at: (i, 0))


def whole_spec(shape):
    return pl.BlockSpec(shape, lambda i, at: (0,) * len(shape))


def pair_spec(rows, first_pair):
    return pl.BlockSpec((rows, PAIR), lambda p, at: (0, p + first_pair))


def logs_spec(rows, first_pair):
    return pl.BlockSpec((1, 16, rows), lambda p, at: (p + first_pair, 0, 0))


def call(kernel, at, arrays, specs, outs, out_specs, scratch, steps, micros=10.0, aliases={}):
    return pl.pallas_call(
        kernel,
        out_shape=outs,
        grid_spec=pltpu.PrefetchScalarGridSpec(
            num_scalar_prefetch=1,
            grid=(steps,),
            in_specs=specs,
            out_specs=out_specs,
            scratch_shapes=scratch,
        ),
        input_output_aliases=aliases,
        compiler_params=pltpu.CompilerParams(vmem_limit_bytes=VMEM),
        cost_estimate=pl.CostEstimate(
            flops=int(micros * 1.1e9), bytes_accessed=int(micros * 1e5), transcendentals=0
        ),
    )(at, *arrays)


def shape_of(shape, dtype):
    return jax.ShapeDtypeStruct(shape, dtype)


def turn_lanes(values, lane):
    return jnp.where(
        (lane & (HEAD_DIM - 1)) < HEAD_DIM // 2,
        pltpu.roll(values, PAIR - HEAD_DIM // 2, 1),
        pltpu.roll(values, HEAD_DIM // 2, 1),
    )


def project_heads(at, inputs, pieces, cosine, sine):
    rows, width = inputs.shape
    half = width // 2
    n = len(pieces)

    def kernel(at_ref, a_ref, cos_ref, sin_ref, *refs):
        parts, (q_ref, k_ref, v_ref), (w_ref, sems) = refs[:n], refs[n : n + 3], refs[n + 3 :]
        load_first(at_ref, (parts, w_ref, sems))
        a = a_ref[...]
        cos, sin = cos_ref[...], sin_ref[...]
        lane = lax.broadcasted_iota(jnp.int32, (BLOCK, PAIR), 1)
        for c in range(2):
            res = dot(a, w_ref[c])
            for t in range(half // PAIR):
                here = slice(c * half + t * PAIR, c * half + (t + 1) * PAIR)
                q = res[:, t * PAIR : (t + 1) * PAIR]
                k = res[:, half + t * PAIR : half + (t + 1) * PAIR]
                q = q * cos + turn_lanes(q, lane) * sin
                q_ref[:, here] = (q * HEAD_DIM**-0.5).astype(LOW)
                k_ref[:, here] = (k * cos + turn_lanes(k, lane) * sin).astype(LOW)
            v_ref[:, c * half : (c + 1) * half] = res[:, 2 * half :].astype(LOW)

    return call(
        kernel,
        at,
        [inputs, cosine, sine, *pieces],
        [rows_spec(width), rows_spec(PAIR), rows_spec(PAIR)] + [ANYWHERE] * n,
        [shape_of((rows, width), LOW)] * 3,
        [rows_spec(width)] * 3,
        weight_scratch(pieces),
        rows // BLOCK,
        10,
    )


def head_masks(head, lane):
    own = lane < HEAD_DIM if head == 0 else lane >= HEAD_DIM
    return own, lane == (HEAD_DIM if head == 0 else 0)


def attend(at, queries, key_rows, value_rows, first_pair, pairs, before=()):
    rows, width = queries.shape
    every = width // PAIR

    def kernel(at_ref, q_ref, k_ref, v_ref, *refs):
        o_ref, lse_ref = refs[len(before) :]
        lane = lax.broadcasted_iota(jnp.int32, (rows, PAIR), 1)
        row = lax.broadcasted_iota(jnp.int32, (rows, PAIR), 0)
        bias = jnp.where(row < at_ref[4], 0.0, masked_score)
        q, k, v = q_ref[...].astype(F32), k_ref[...].astype(F32), v_ref[...].astype(F32)
        below = lax.broadcasted_iota(jnp.int32, (BLOCK, BLOCK), 0) >= lax.broadcasted_iota(
            jnp.int32, (BLOCK, BLOCK), 1
        )
        heads = []
        for head in range(2):
            own, mark = head_masks(head, lane)
            heads.append(
                (
                    jnp.where(own, q, jnp.where(mark, 1.0, 0.0)).astype(LOW),
                    jnp.where(own, k, jnp.where(mark, bias, 0.0)).astype(LOW),
                    jnp.where(own, v, 1.0).astype(LOW),
                )
            )
        lane_here = lane[:BLOCK]
        for first in range(0, rows, BLOCK):
            end = first + BLOCK
            mixed, logs = [], []
            for qh, kh, vh in heads:
                scores = dot_nt(qh[first:end], kh[:end])
                edge = jnp.where(below, scores[:, first:], masked_score)
                scores = jnp.concatenate([scores[:, :first], edge], axis=1) if first else edge
                top = jnp.max(scores, axis=-1, keepdims=True)
                weights = jnp.exp(scores - top).astype(LOW)
                both = dot(weights, vh[:end])
                total = pltpu.roll(both, HEAD_DIM, 1)
                mixed.append(both / total)
                logs.append(top + jnp.log(total))
            o_ref[first:end, :] = jnp.where(lane_here < HEAD_DIM, mixed[0], mixed[1]).astype(LOW)
            turned = jnp.where(lane_here < HEAD_DIM, logs[0], logs[1]).T
            lse_ref[0, 0:8, first:end] = turned[0:8]
            lse_ref[0, 8:16, first:end] = turned[HEAD_DIM : HEAD_DIM + 8]

    return call(
        kernel,
        at,
        [queries, key_rows, value_rows, *before],
        [pair_spec(rows, first_pair)] * 3 + [ANYWHERE] * len(before),
        [shape_of((rows, width), LOW), shape_of((every, 16, rows), F32)],
        [pair_spec(rows, first_pair), logs_spec(rows, first_pair)],
        [],
        pairs,
        4 * pairs,
        {4 + i: i for i in range(len(before))},
    )


def attend_back(
    at, queries, key_rows, value_rows, mixed, logs, upstream, cosine, sine, first_pair, pairs, before=()
):
    rows, width = queries.shape

    def kernel(at_ref, q_ref, k_ref, v_ref, o_ref, lse_ref, g_ref, cos_ref, sin_ref, *refs):
        dq_ref, dk_ref, dv_ref, sum_ref = refs[len(before) :]
        lane = lax.broadcasted_iota(jnp.int32, (rows, PAIR), 1)
        row = lax.broadcasted_iota(jnp.int32, (rows, PAIR), 0)
        bias = jnp.where(row < at_ref[4], 0.0, masked_score)
        q, k, v = q_ref[...].astype(F32), k_ref[...].astype(F32), v_ref[...].astype(F32)
        q_low, k_low, g_low = q_ref[...], k_ref[...], g_ref[...]
        above = lax.broadcasted_iota(jnp.int32, (BLOCK, BLOCK), 0) <= lax.broadcasted_iota(
            jnp.int32, (BLOCK, BLOCK), 1
        )
        turned = (g_low.astype(F32) * o_ref[...].astype(F32)).T
        cos, sin = cos_ref[...], sin_ref[...]

        def unrotate(values, first, end):
            moved = values * sin[first:end]
            return values * cos[first:end] + turn_lanes(moved, lane[first:end])

        key_parts, value_parts = [], []
        for head in range(2):
            own, mark = head_masks(head, lane)
            qh = jnp.where(own, q, jnp.where(mark, 1.0, 0.0)).astype(LOW)
            kh = jnp.where(own, k, jnp.where(mark, bias, 0.0)).astype(LOW)
            vh = jnp.where(own, v, 0.0).astype(LOW)
            delta = jnp.sum(
                turned[head * HEAD_DIM : (head + 1) * HEAD_DIM], axis=0, keepdims=True
            )
            lse = lse_ref[0, head * 8 : head * 8 + 1, :]
            key_parts.append([])
            value_parts.append([])
            for first in range(0, rows, BLOCK):
                end = first + BLOCK
                scores = dot_nt(kh[first:end], qh[first:])
                soft = jnp.exp(scores - lse[:, first:])
                edge = jnp.where(above, soft[:, :BLOCK], 0.0)
                if end < rows:
                    soft = jnp.concatenate([edge, soft[:, BLOCK:]], axis=1)
                else:
                    soft = edge
                grad = dot_nt(vh[first:end], g_low[first:])
                grad = (soft * (grad - delta[:, first:])).astype(LOW)
                value_parts[head].append(dot(soft.astype(LOW), g_low[first:]))
                key_parts[head].append(dot(grad, q_low[first:]))
                added = dot_tn(grad, k_low[first:end])
                if first == 0:
                    sum_ref[head] = added
                else:
                    sum_ref[head, first:, :] += added
        lane_here = lane[:BLOCK]
        for step in range(rows // BLOCK):
            first, end = step * BLOCK, (step + 1) * BLOCK
            dk = jnp.where(lane_here < HEAD_DIM, key_parts[0][step], key_parts[1][step])
            dv = jnp.where(lane_here < HEAD_DIM, value_parts[0][step], value_parts[1][step])
            dq = jnp.where(lane_here < HEAD_DIM, sum_ref[0, first:end, :], sum_ref[1, first:end, :])
            dk_ref[first:end, :] = unrotate(dk, first, end).astype(LOW)
            dq_ref[first:end, :] = unrotate(dq * HEAD_DIM**-0.5, first, end).astype(LOW)
            dv_ref[first:end, :] = dv.astype(LOW)

    return call(
        kernel,
        at,
        [queries, key_rows, value_rows, mixed, logs, upstream, cosine, sine, *before],
        [pair_spec(rows, first_pair)] * 4
        + [logs_spec(rows, first_pair), pair_spec(rows, first_pair)]
        + [whole_spec((rows, PAIR))] * 2
        + [ANYWHERE] * len(before),
        [shape_of((rows, width), LOW)] * 3,
        [pair_spec(rows, first_pair)] * 3,
        [pltpu.VMEM((2, rows, PAIR), F32)],
        pairs,
        5 * pairs,
        {9 + i: i for i in range(len(before))},
    )


def open_block(at, mixed, resid, gain, pieces):
    rows, width = mixed.shape
    half = width // 2
    n = len(pieces)
    cols = weight_shape(pieces)[2]
    wide = (cols - half) // 2

    def kernel(at_ref, o_ref, resid_ref, gain_ref, *refs):
        parts, outs, (w_ref, sems) = refs[:n], refs[n : n + 5], refs[n + 5 :]
        r_ref, hl_ref, gate_ref, up_ref, z_ref = outs
        load_first(at_ref, (parts, w_ref, sems))
        o = o_ref[...]
        branch = jnp.concatenate([dot(o, w_ref[c, :, :half]) for c in range(2)], axis=1)
        r = resid_ref[...].astype(F32) + branch
        r_ref[...] = r
        hl = (r * inverse_rms(r) * gain_ref[...]).astype(LOW)
        hl_ref[...] = hl
        for c in range(2):
            gate = dot(hl, w_ref[c, :, half : half + wide])
            up = dot(hl, w_ref[c, :, half + wide :])
            here = slice(c * wide, (c + 1) * wide)
            gate_ref[:, here] = gate.astype(LOW)
            up_ref[:, here] = up.astype(LOW)
            z_ref[:, here] = (silu_parts(gate)[1] * up).astype(LOW)

    return call(
        kernel,
        at,
        [mixed, resid, gain, *pieces],
        [rows_spec(width), rows_spec(width), whole_spec((1, width))] + [ANYWHERE] * n,
        [shape_of((rows, width), F32), shape_of((rows, width), LOW)]
        + [shape_of((rows, 2 * wide), LOW)] * 3,
        [rows_spec(width)] * 2 + [rows_spec(2 * wide)] * 3,
        weight_scratch(pieces),
        rows // BLOCK,
        16,
    )


def close_first(at, hidden, resid, gains, pieces):
    rows, width = resid.shape
    wide = hidden.shape[1]
    n = len(pieces)

    def kernel(at_ref, z_ref, r_ref, gain_ref, *refs):
        parts, (r2_ref, out_ref, next_ref), (w_ref, sems) = refs[:n], refs[n : n + 3], refs[n + 3 :]
        load_first(at_ref, (parts, w_ref, sems))
        z = z_ref[...]
        r = r_ref[...]
        branch = jnp.concatenate([dot(z, w_ref[c]) for c in range(2)], axis=1)
        r2 = r * inverse_rms(r) * gain_ref[0:1] + branch
        r2_ref[...] = r2
        out = r2 * inverse_rms(r2) * gain_ref[1:2]
        out_ref[...] = out
        next_ref[...] = (out * inverse_rms(out) * gain_ref[2:3]).astype(LOW)

    return call(
        kernel,
        at,
        [hidden, resid, gains, *pieces],
        [rows_spec(wide), rows_spec(width), whole_spec(gains.shape)] + [ANYWHERE] * n,
        [shape_of((rows, width), F32)] * 2 + [shape_of((rows, width), LOW)],
        [rows_spec(width)] * 3,
        weight_scratch(pieces),
        rows // BLOCK,
        12,
    )


def close_second(at, hidden, resid, pieces):
    rows, width = resid.shape
    wide = hidden.shape[1]
    n = len(pieces)

    def kernel(at_ref, z_ref, r_ref, *refs):
        parts, out_ref, (w_ref, sems) = refs[:n], refs[n], refs[n + 1 :]
        load_first(at_ref, (parts, w_ref, sems))
        z = z_ref[...]
        branch = jnp.concatenate([dot(z, w_ref[c]) for c in range(2)], axis=1)
        out_ref[...] = r_ref[...] + branch

    return call(
        kernel,
        at,
        [hidden, resid, *pieces],
        [rows_spec(wide), rows_spec(width)] + [ANYWHERE] * n,
        shape_of((rows, width), F32),
        rows_spec(width),
        weight_scratch(pieces),
        rows // BLOCK,
        6,
    )


def feed_back(at, upstream, up_low, gate, up, resid, gain, pieces, down, post):
    rows, width = resid.shape
    half, wide = width // 2, gate.shape[1]
    part = wide // 2
    n, m = len(pieces), len(down)

    def kernel(at_ref, du_ref, dl_ref, gate_ref, up_ref, r_ref, gain_ref, *refs):
        parts, down_parts, refs = refs[:n], refs[n : n + m], refs[n + m :]
        dgate_ref, dup_ref, dr_ref, dlow_ref, do_ref, dgain_ref = refs[:6]
        w_ref, sems, d_ref, d_sems = refs[6:]
        load_first(at_ref, (parts, w_ref, sems), (down_parts, d_ref, d_sems))
        dl = dl_ref[...]
        inward = None
        for c in range(2):
            here = slice(c * part, (c + 1) * part)
            dz = dot_nt(dl[:, :half], d_ref[0, here, :]) + dot_nt(dl[:, half:], d_ref[1, here, :])
            gate = gate_ref[:, here].astype(F32)
            sig, act = silu_parts(gate)
            dup = (dz * act).astype(LOW)
            dgate = dz * up_ref[:, here].astype(F32) * sig * (1.0 + gate * (1.0 - sig))
            dgate = dgate.astype(LOW)
            dup_ref[:, here] = dup
            dgate_ref[:, here] = dgate
            added = dot_nt(dgate, w_ref[c, :, half : half + part])
            added = added + dot_nt(dup, w_ref[c, :, half + part :])
            inward = added if inward is None else inward + added
        du = du_ref[...].astype(F32)
        if post:
            dr, share = norm_back(r_ref[...], gain_ref[...], du + inward)
        else:
            dr, share = norm_back(r_ref[...], gain_ref[...], inward)
            dr = du + dr
        dr_ref[...] = dr
        low = dr.astype(LOW)
        dlow_ref[...] = low
        do = dot_nt(low[:, :half], w_ref[0, :, :half]) + dot_nt(low[:, half:], w_ref[1, :, :half])
        do_ref[...] = do.astype(LOW)

        @pl.when(pl.program_id(0) == 0)
        def _():
            dgain_ref[...] = jnp.zeros_like(dgain_ref)

        dgain_ref[...] += fold_rows(share)

    return call(
        kernel,
        at,
        [upstream, up_low, gate, up, resid, gain, *pieces, *down],
        [rows_spec(width)] * 2
        + [rows_spec(wide)] * 2
        + [rows_spec(width), whole_spec((1, width))]
        + [ANYWHERE] * (n + m),
        [shape_of((rows, wide), LOW)] * 2
        + [shape_of((rows, width), F32)]
        + [shape_of((rows, width), LOW)] * 2
        + [shape_of((8, width), F32)],
        [rows_spec(wide)] * 2 + [rows_spec(width)] * 3 + [whole_spec((8, width))],
        weight_scratch(pieces) + weight_scratch(down),
        rows // BLOCK,
        27,
    )


def heads_inward(dq, dk, dv, w_ref):
    half = dq.shape[1] // 2
    inward = None
    for c in range(2):
        here = slice(c * half, (c + 1) * half)
        joined = jnp.concatenate([dq[:, here], dk[:, here], dv[:, here]], axis=1)
        added = dot_nt(joined, w_ref[c])
        inward = added if inward is None else inward + added
    return inward


def heads_back_second(at, dq, dk, dv, upstream, first_out, resid_two, gains, pieces):
    rows, width = dq.shape
    n = len(pieces)

    def kernel(at_ref, dq_ref, dk_ref, dv_ref, du_ref, h_ref, r_ref, gain_ref, *refs):
        parts, refs = refs[:n], refs[n:]
        dr_ref, dlow_ref, ga_ref, gb_ref, w_ref, sems = refs
        load_first(at_ref, (parts, w_ref, sems))
        inward = heads_inward(dq_ref[...], dk_ref[...], dv_ref[...], w_ref)
        back, share_a = norm_back(h_ref[...], gain_ref[0:1], inward)
        dr, share_b = norm_back(r_ref[...], gain_ref[1:2], du_ref[...] + back)
        dr_ref[...] = dr
        dlow_ref[...] = dr.astype(LOW)

        @pl.when(pl.program_id(0) == 0)
        def _():
            ga_ref[...] = jnp.zeros_like(ga_ref)
            gb_ref[...] = jnp.zeros_like(gb_ref)

        ga_ref[...] += fold_rows(share_a)
        gb_ref[...] += fold_rows(share_b)

    return call(
        kernel,
        at,
        [dq, dk, dv, upstream, first_out, resid_two, gains, *pieces],
        [rows_spec(width)] * 6 + [whole_spec(gains.shape)] + [ANYWHERE] * n,
        [shape_of((rows, width), F32), shape_of((rows, width), LOW)]
        + [shape_of((8, width), F32)] * 2,
        [rows_spec(width)] * 2 + [whole_spec((8, width))] * 2,
        weight_scratch(pieces),
        rows // BLOCK,
        14,
    )


def heads_back_first(at, dq, dk, dv, upstream, pieces):
    rows, width = dq.shape
    n = len(pieces)

    def kernel(at_ref, dq_ref, dk_ref, dv_ref, du_ref, *refs):
        parts, (out_ref, w_ref, sems) = refs[:n], refs[n:]
        load_first(at_ref, (parts, w_ref, sems))
        out_ref[...] = du_ref[...] + heads_inward(dq_ref[...], dk_ref[...], dv_ref[...], w_ref)

    return call(
        kernel,
        at,
        [dq, dk, dv, upstream, *pieces],
        [rows_spec(width)] * 4 + [ANYWHERE] * n,
        shape_of((rows, width), F32),
        rows_spec(width),
        weight_scratch(pieces),
        rows // BLOCK,
        8,
    )


def weight_grad(half, groups, received):
    rows = groups[0][0].shape[0]
    lefts = [left for left, _ in groups]
    rights = [right for _, many in groups for right in many]
    counts = [len(many) for _, many in groups]
    tall = lefts[0].shape[1]
    sizes = [right.shape[1] // 2 for right in rights]
    extra = [] if received is None else [received]

    def kernel(half_ref, *refs):
        left_refs, refs = refs[: len(lefts)], refs[len(lefts) :]
        right_refs, refs = refs[: len(rights)], refs[len(rights) :]
        out_ref = refs[-1]
        offset, at = 0, 0
        for left_ref, count in zip(left_refs, counts):
            left = left_ref[...]
            for right_ref in right_refs[at : at + count]:
                size = right_ref.shape[1]
                here = slice(offset, offset + size)
                res = dot_tn(left, right_ref[...])
                if extra:
                    res = res + refs[0][:, here].astype(F32)
                out_ref[:, here] = res.astype(LOW)
                offset += size
            at += count

    total = sum(sizes)
    return call(
        kernel,
        half,
        lefts + rights + extra,
        [whole_spec((rows, tall))] * len(lefts)
        + [pl.BlockSpec((rows, size), lambda i, at: (0, at[0])) for size in sizes]
        + [whole_spec((tall, total))] * len(extra),
        shape_of((tall, total), LOW),
        whole_spec((tall, total)),
        [],
        1,
        7,
    )


def tie(value, *others):
    others = [other for other in others if other is not None]
    return lax.optimization_barrier((value, *others))[0] if others else value


def place_of():
    f = lax.axis_index("fsdp")
    r = lax.axis_index("rep")
    return (f // 2, f % 2, r // 2, r % 2)


def shift_z(grid, k):
    return lambda z, y, x, c: ((z + k) % grid.zs, y, x, c)


def pick(array, index, axis):
    return lax.dynamic_index_in_dim(array, index, axis, keepdims=False)


def add_low(one, two):
    return (one.astype(F32) + two.astype(F32)).astype(LOW)


def join_halves(left, right, widths):
    out, offset = [], 0
    for width in widths:
        here = slice(offset, offset + width // 2)
        out.append(jnp.concatenate([left[:, here], right[:, here]], axis=1))
        offset += width // 2
    return out


class Gather:
    def __init__(self, link, shards, after=None):
        z, y, x, c = link.place
        grid = self.grid = link.grid
        rows = shards[0].shape[0] // 2
        own = jnp.concatenate(
            [
                lax.dynamic_slice(
                    shard, (x * rows, c * (shard.shape[1] // 2)), (rows, shard.shape[1] // 2)
                )
                for shard in shards
            ],
            axis=1,
        )
        own = tie(own, after)
        around = [own] + [send(grid, own, shift_z(grid, k)) for k in range(1, grid.zs)]
        self.base = jnp.stack(around)

    def near(self, *after):
        base = tie(self.base, *after)
        self.one = send(self.grid, base, first_flip)
        self.two = send(self.grid, base, second_flip)
        return self.one

    def far(self, *after):
        self.three = send(self.grid, tie(self.one, *after), second_flip)
        return self.three

    def whole(self, *after):
        near = [self.base, self.one, self.two, self.three]
        return near + [send(self.grid, part, core_flip) for part in near]


class PlainGather:
    base = one = three = None

    def __init__(self, link, shards, after=None):
        self.shards = shards

    def near(self, *after):
        return None

    def far(self, *after):
        return None

    def whole(self, *after):
        full = [lax.all_gather(shard, "fsdp", axis=0, tiled=True) for shard in self.shards]
        halves = [
            jnp.concatenate([jnp.split(weight, 2, axis=1)[c] for weight in full], axis=1)
            for c in range(2)
        ]
        return [jnp.stack(halves)]


class Reduce:
    def __init__(self, link, make, widths, *after):
        self.link, self.make, self.widths = link, make, widths
        self.away = make(tie(link.other, *after), None)
        self.got = send(link.grid, self.away, core_flip)

    def mine(self, *after):
        z, y, x, c = self.link.place
        half = self.make(tie(self.link.mine, *after), self.got)
        zs = self.link.grid.zs
        rows, cols = half.shape[0] // (4 * zs), half.shape[1]
        view = half.reshape(zs, 2, 2, rows, cols)
        self.keep = jnp.where(c == 0, pick(view, y, 1), pick(view, x, 2))
        away = jnp.where(c == 0, pick(view, 1 - y, 1), pick(view, 1 - x, 2))
        self.got = send(self.link.grid, away, second_flip)
        return half

    def one(self, *after):
        z, y, x, c = self.link.place
        part = add_low(self.keep, tie(self.got, *after))
        b = jnp.where(c == 0, x, y)
        self.keep = pick(part, b, 1)
        away = pick(part, 1 - b, 1)
        self.got = send(self.link.grid, away, first_flip)
        return away

    def two(self, *after):
        grid = self.link.grid
        z = self.link.place[0]
        part = add_low(self.keep, tie(self.got, *after))
        self.keep = pick(part, z, 0)
        self.got = [
            send(grid, pick(part, (z + k) % grid.zs, 0), shift_z(grid, k))
            for k in range(1, grid.zs)
        ]
        return part

    def three(self, *after):
        total = tie(self.keep, *after).astype(F32)
        for got in self.got:
            total = total + got.astype(F32)
        self.keep = total.astype(LOW)
        self.got = send(self.link.grid, self.keep, x_flip)
        return self.keep

    def four(self, *after):
        x = self.link.place[2]
        self.got = tie(self.got, *after)
        self.keep = jnp.concatenate(
            [jnp.where(x == 0, self.keep, self.got), jnp.where(x == 0, self.got, self.keep)],
            axis=0,
        )
        self.got = send(self.link.grid, self.keep, core_flip)
        return self.keep

    def out(self, *after):
        c = self.link.place[3]
        self.got = tie(self.got, *after)
        left = jnp.where(c == 0, self.keep, self.got).astype(F32)
        right = jnp.where(c == 0, self.got, self.keep).astype(F32)
        return join_halves(left, right, self.widths)


class PlainReduce:
    away = None

    def __init__(self, link, make, widths, *after):
        self.make, self.widths = make, widths

    def mine(self, *after):
        return None

    one = two = three = four = mine

    def out(self, *after):
        halves = [self.make(jnp.full((1,), c, jnp.int32), None) for c in range(2)]
        share = lax.psum_scatter(
            jnp.stack(halves, axis=1), "fsdp", scatter_dimension=0, tiled=True
        )
        share = lax.psum(share, "rep").astype(F32)
        return join_halves(share[:, 0], share[:, 1], self.widths)


class Direct:
    gather, reduce = Gather, Reduce

    def __init__(self, fsdp, rep):
        self.grid = Grid(fsdp, rep)
        self.place = place_of()
        self.at = jnp.stack(self.place).astype(jnp.int32)
        self.mine = self.at[3:4]
        self.other = 1 - self.mine

    def gains(self, own):
        z, y, x, c = self.place
        grid = self.grid
        around = [own] + [send(grid, own, shift_z(grid, k)) for k in range(1, grid.zs)]
        base = jnp.stack(around)
        both = jnp.stack([base, send(grid, base, y_flip)])
        blocks = []
        for zz in range(grid.zs):
            level = pick(both, (z + grid.zs - zz) % grid.zs, 1)
            for yy in range(2):
                blocks.append(pick(level, jnp.abs(y - yy), 0))
        return jnp.concatenate(blocks, axis=1)

    def reduce_gains(self, value):
        z, y, x, c = self.place
        grid = self.grid
        for flip in (core_flip, x_flip, y_flip):
            value = value + send(grid, value, flip)
        total = value
        for k in range(1, grid.zs):
            total = total + send(grid, value, shift_z(grid, k))
        share = total.shape[1] // (2 * grid.zs)
        return lax.dynamic_slice_in_dim(total, (z * 2 + y) * share, share, 1)


class Plain:
    gather, reduce = PlainGather, PlainReduce

    def __init__(self):
        self.at = jnp.zeros((4,), jnp.int32)

    def gains(self, own):
        return lax.all_gather(own, "fsdp", axis=1, tiled=True)

    def reduce_gains(self, value):
        share = lax.psum_scatter(value, "fsdp", scatter_dimension=1, tiled=True)
        return lax.psum(share, "rep")


def rope_tables(positions):
    even_steps = jnp.arange(0, HEAD_DIM, 2).astype(F32)
    inverse = jnp.exp(even_steps * (-math.log(10000.0) / HEAD_DIM))
    angles = positions.astype(F32)[:, None] * inverse
    cosine, sine = jnp.cos(angles), jnp.sin(angles)
    return jnp.concatenate([cosine] * 4, axis=1), jnp.concatenate([-sine, sine] * 2, axis=1)


def body(
    fsdp,
    rep,
    tokens,
    cotangent,
    seq_lengths,
    token_positions,
    first_query,
    first_key,
    first_value,
    first_output,
    first_gate,
    first_up,
    first_down,
    first_attngain,
    first_ffngain,
    second_query,
    second_key,
    second_value,
    second_output,
    second_gate,
    second_up,
    second_down,
    second_attngain,
    second_ffngain,
):
    _, rows, width = tokens.shape
    wide = first_gate.shape[1]
    low_tokens = tokens.reshape(rows, width)
    low_cot = cotangent.reshape(rows, width)
    link = Direct(fsdp, rep) if (fsdp, rep) == (8, 4) else Plain()
    at = jnp.concatenate([link.at, seq_lengths.astype(jnp.int32)])
    cosine, sine = rope_tables(token_positions.reshape(rows))
    pairs = width // PAIR
    split = pairs // 2
    attn_widths, open_widths = (width,) * 3, (width, wide, wide)

    heads_one = link.gather(link, (first_query, first_key, first_value))
    gains = link.gains(
        jnp.stack([first_attngain, first_ffngain, second_attngain, second_ffngain])
    ).astype(F32)
    attn_one, ffn_one, attn_two, ffn_two = (gains[i : i + 1] for i in range(4))
    open_one = link.gather(link, (first_output, first_gate, first_up), heads_one.base)
    heads_one.near()
    far = heads_one.far()
    down_one = link.gather(link, (first_down,), open_one.base)
    open_one.near(far)
    heads_one = heads_one.whole()
    q1, k1, v1 = project_heads(at, low_tokens, heads_one, cosine, sine)
    half = attend(at, tie(q1, down_one.base), k1, v1, 0, split)
    open_one.far()
    heads_two = link.gather(link, (second_query, second_key, second_value), down_one.base)
    o1, log1 = attend(at, tie(q1, open_one.one), k1, v1, split, pairs - split, half)
    down_one.near(open_one.three)
    open_one = open_one.whole()
    r1, h1, gate1, up1, z1 = open_block(at, o1, low_tokens, attn_one, open_one)
    far = down_one.far()
    heads_two.near(far)
    open_two = link.gather(link, (second_output, second_gate, second_up), heads_two.base)
    down_one = down_one.whole()
    r2, first_out, n1 = close_first(at, z1, r1, gains, down_one)
    far = heads_two.far()
    heads_two = heads_two.whole()
    q2, k2, v2 = project_heads(at, n1, heads_two, cosine, sine)
    open_two.near(far)
    down_two = link.gather(link, (second_down,), open_two.base)
    half = attend(at, q2, k2, v2, 0, split)
    open_two.far()
    o2, log2 = attend(at, tie(q2, open_two.one), k2, v2, split, pairs - split, half)
    down_two.near(open_two.three)
    open_two = open_two.whole()
    r3, h2, gate2, up2, z2 = open_block(at, o2, first_out, ffn_two, open_two)
    down_two.far()
    down_two = down_two.whole()
    second_out = close_second(at, z2, r3, down_two)

    dgate2, dup2, dr3, dr3_low, do2, gain_d = feed_back(
        at, low_cot, low_cot, gate2, up2, r3, ffn_two, open_two, down_two, False
    )
    down_g2 = link.reduce(
        link, lambda half, got: weight_grad(half, [(z2, [low_cot])], got), (width,), dr3
    )
    open_g2 = link.reduce(
        link,
        lambda half, got: weight_grad(half, [(o2, [dr3_low]), (h2, [dgate2, dup2])], got),
        open_widths,
        down_g2.away,
    )
    sent = down_g2.mine(open_g2.away)
    sent = open_g2.mine(sent)
    half = attend_back(at, tie(q2, sent), k2, v2, o2, log2, do2, cosine, sine, 0, split)
    part = down_g2.one(half[0])
    dq2, dk2, dv2 = attend_back(
        at, tie(q2, part), k2, v2, o2, log2, do2, cosine, sine, split, pairs - split, half
    )
    part = (open_g2.one(dq2), down_g2.two(dq2))
    heads_g2 = link.reduce(
        link, lambda half, got: weight_grad(half, [(n1, [dq2, dk2, dv2])], got), attn_widths, *part
    )
    dr2, dr2_low, gain_c, gain_b = heads_back_second(
        tie(at, heads_g2.away),
        dq2,
        dk2,
        dv2,
        dr3,
        first_out,
        r2,
        jnp.concatenate([attn_two, ffn_one]),
        heads_two,
    )
    part = (open_g2.two(dr2), down_g2.three(dr2))
    sent = heads_g2.mine(dr2, *part)

    dgate1, dup1, dr1, dr1_low, do1, gain_a = feed_back(
        tie(at, sent), dr2, dr2_low, gate1, up1, r1, attn_one, open_one, down_one, True
    )
    part = (open_g2.three(dr1), heads_g2.one(dr1), down_g2.four(dr1))
    down_g1 = link.reduce(
        link, lambda half, got: weight_grad(half, [(z1, [dr2_low])], got), (width,), dr1, *part
    )
    open_g1 = link.reduce(
        link,
        lambda half, got: weight_grad(half, [(o1, [dr1_low]), (h1, [dgate1, dup1])], got),
        open_widths,
        down_g1.away,
    )
    part = (heads_g2.two(open_g1.away), open_g2.four(open_g1.away))
    sent = down_g1.mine(open_g1.away, *part)
    sent = open_g1.mine(sent)
    gain_grads = link.reduce_gains(
        jnp.stack([jnp.sum(share, axis=0) for share in (gain_a, gain_b, gain_c, gain_d)])
    )
    half = attend_back(at, tie(q1, sent), k1, v1, o1, log1, do1, cosine, sine, 0, split)
    part = (down_g1.one(half[0]), heads_g2.three(half[0]))
    dq1, dk1, dv1 = attend_back(
        at, tie(q1, *part), k1, v1, o1, log1, do1, cosine, sine, split, pairs - split, half
    )
    part = (open_g1.one(dq1), down_g1.two(dq1), heads_g2.four(dq1))
    heads_g1 = link.reduce(
        link,
        lambda half, got: weight_grad(half, [(low_tokens, [dq1, dk1, dv1])], got),
        attn_widths,
        *part,
    )
    part = (open_g1.two(heads_g1.away), down_g1.three(heads_g1.away))
    sent = heads_g1.mine(*part)
    input_grad = heads_back_first(tie(at, sent), dq1, dk1, dv1, dr1, heads_one)
    part = heads_g1.one(input_grad)
    down_g1.four(input_grad)
    part = heads_g1.two()
    open_g1.three(part)
    down_g1 = down_g1.out(part)
    output_g2, gate_g2, up_g2 = open_g2.out(part)
    query_g2, key_g2, value_g2 = heads_g2.out(part)
    (down_g2,) = down_g2.out(part)
    part = heads_g1.three()
    open_g1.four(part)
    (down_g1,) = down_g1
    heads_g1.four()
    query_g1, key_g1, value_g1 = heads_g1.out()
    output_g1, gate_g1, up_g1 = open_g1.out()
    return (
        first_out.reshape(tokens.shape),
        second_out.reshape(tokens.shape),
        input_grad.reshape(tokens.shape),
        query_g1,
        key_g1,
        value_g1,
        output_g1,
        gate_g1,
        up_g1,
        down_g1,
        gain_grads[0],
        gain_grads[1],
        query_g2,
        key_g2,
        value_g2,
        output_g2,
        gate_g2,
        up_g2,
        down_g2,
        gain_grads[2],
        gain_grads[3],
    )


def solution(mesh):
    per_seq = P(("fsdp", "rep"))
    shard = P("fsdp")
    return jax.shard_map(
        functools.partial(body, mesh.shape["fsdp"], mesh.shape["rep"]),
        mesh=mesh,
        in_specs=(per_seq,) * 4 + (shard,) * 18,
        out_specs=(per_seq,) * 3 + (shard,) * 18,
        check_vma=False,
    )
```

time: 2050 us -> 707 us (0.34)
  waiting for transfers between devices: 1360 us -> 120 us
  matrix products: 407 us -> 0 us
  Pallas kernels: 0 us -> 362 us
  starting transfers between devices: 1.94 us -> 126 us
  other arithmetic: 135 us -> 54.5 us
  blocking collectives: 49.1 us -> 0 us
  local copies, waits for them, and re-layouts: 66.4 us -> 28.1 us
    reduce_scatter x11 -> x0, waiting for transfers between devices: 793 us -> none  [the longest x2 155 us: reduce_grads(): lax.psum_scatter(gate_g.astype(jnp.bfloat16), 'fsdp', scatter_dimension=0...]
    all_gather x14 -> x0, waiting for transfers between devices: 462 us -> none  [the longest x2 106 us: collect(): lax.all_gather(up_w, 'fsdp', axis=0, tiled=True)]
    dot_general x66 -> x0, matrix products: 407 us -> none  [the longest x4 57 us: one_sequence(): jnp.einsum('qhd,khd->hqk', grad_block, value_seq[:end_row], preferred_ele...]
    pallas_call x0 -> x30, Pallas kernels: none -> 362 us  [call(): pl.pallas_call(kernel, out_shape=outs, grid_spec=pltpu.PrefetchScalarGrid...]
    ppermute x0 -> x118, starting transfers between devices: none -> 126 us  [send(): return lax.ppermute(value, AXES, grid.pairs(move))]
    ppermute x0 -> x118, waiting for transfers between devices: none -> 120 us  [send(): return lax.ppermute(value, AXES, grid.pairs(move))]
    unnamed x32 -> x0, waiting for transfers between devices: 82.4 us -> none
    convert_element_type x33 -> x24, other arithmetic: 78.4 us -> 22.6 us  [the longest x12 14.1 us: add_low(): return (one.astype(F32) + two.astype(F32)).astype(LOW)]
  transfers between devices with their start and end apart: 29 -> 118, of which waited for: 26 -> 33; matrix products, arithmetic and copies ran while one was open for 17% -> 9% of each run, Pallas kernels for 0% -> 44%
where the time goes in v1:
time: 707 us; the launch traced here: 693 us
  Pallas kernels  362 us (51%)
  starting transfers between devices  126 us (18%)
  waiting for transfers between devices  120 us (17%)
  other arithmetic  54.5 us (8%)
  local copies, waits for them, and re-layouts  28.1 us (4%)
    pallas_call x30, Pallas kernels, call(): pl.pallas_call(kernel, out_shape=outs, grid_spec=pltpu.PrefetchScalarGrid...  362 us
    ppermute x118, starting transfers between devices, send(): return lax.ppermute(value, AXES, grid.pairs(move))  126 us
    ppermute x118, waiting for transfers between devices, send(): return lax.ppermute(value, AXES, grid.pairs(move))  120 us
  transfers between devices with their start and end apart: 118, of which 33 were waited for; matrix products, arithmetic and copies ran while one was open for 9% of the time, Pallas kernels for 44%

profile of v1, /device:TPU:0, one launch (start us, length us, event | category | flops | bytes accessed | tf_op | source)
XLA Modules:
  0.0 693.4 jit_solution(4572646155641244470)
XLA Ops:
  28.5 8.6 %collective-permute-done.11 = bf16[48,2432]{1,0:T(8,128)(2,1)S(1)} collective-permute-done((bf16[48,2432]{1,0:T(8,128)(2,1)S(1)}, bf16[48,2432]{1,0:T(8,128)(2,1)S(1)}, u32[]{:S(2)}, u32[]{:S(2)}) %collective-permute-start.11) | collective-permute-done | bytes 233504 | tf_op jit(solution)/shard_map/ppermute | solution.py:39
  74.2 17.4 %collective-permute-done.18 = bf16[4,96]{1,0:T(4,128)(2,1)S(1)} collective-permute-done((bf16[4,96]{1,0:T(4,128)(2,1)S(1)}, bf16[4,96]{1,0:T(4,128)(2,1)S(1)}, u32[]{:S(2)}, u32[]{:S(2)}) %collective-permute-start.18) | collective-permute-done | bytes 800 | tf_op jit(solution)/shard_map/ppermute | solution.py:39
  120.5 10.4 %shard_map.373 = (bf16[1024,768]{1,0:T(8,128)(2,1)}, bf16[1024,768]{1,0:T(8,128)(2,1)}, bf16[1024,768]{1,0:T(8,128)(2,1)}) custom-call(s32[5]{0:T(128)} %concatenate.93.at_ref, bf16[1024,768]{1,0:T(8,128)(2,1)} %bitcast.304, f32[1024,128]{1,0:T(8,128)} %get-tuple-element.341.cos_ref, f32[1024,128]{1,0:T(8,128)} %get-tuple-element.342.sin_ref, ...), custom_call_target="tpu_custom_call" | custom-call | flops 11000000512 | bytes 1000000 | tf_op jit(solution)/shard_map/pallas_call | solution.py:173
  133.4 12.8 %shard_map.374 = (bf16[1024,768]{1,0:T(8,128)(2,1)}, f32[6,16,1024]{2,1,0:T(8,128)}) custom-call(s32[5]{0:T(128)} %concatenate.93.at_ref, bf16[1024,768]{1,0:T(8,128)(2,1)} %get-tuple-element.219.q_ref, bf16[1024,768]{1,0:T(8,128)(2,1)} %get-tuple-element.137.k_ref, bf16[1024,768]{1,0:T(8,128)(2,1)} %get-tuple-element.138.v_ref), custom_call_target="tpu_custom_call" | custom-call | flops 13200000000 | bytes 1200000 | tf_op jit(solution)/shard_map/pallas_call | solution.py:173
  148.9 12.7 %shard_map.375 = (bf16[1024,768]{1,0:T(8,128)(2,1)}, f32[6,16,1024]{2,1,0:T(8,128)}) custom-call(s32[5]{0:T(128)} %concatenate.93.at_ref, bf16[1024,768]{1,0:T(8,128)(2,1)} %get-tuple-element.219.q_ref, bf16[1024,768]{1,0:T(8,128)(2,1)} %get-tuple-element.137.k_ref, ...), custom_call_target="tpu_custom_call", output_to_operand_aliasing={{0}: (4, {}), {1}: (5, {})} | custom-call | flops 13200000000 | bytes 1200000 | tf_op jit(solution)/shard_map/pallas_call | solution.py:173
  163.2 16.6 %shard_map.376 = (f32[1024,768]{1,0:T(8,128)}, bf16[1024,768]{1,0:T(8,128)(2,1)}, bf16[1024,2048]{1,0:T(8,128)(2,1)}, bf16[1024,2048]{1,0:T(8,128)(2,1)}, bf16[1024,2048]{1,0:T(8,128)(2,1)}) custom-call(s32[5]{0:T(128)} %concatenate.93.at_ref, bf16[1024,768]{1,0:T(8,128)(2,1)} %get-tuple-element.143.o_ref.refs_0_, bf16[1024,768]{1,0:T(8,128)(2,1)} %bitcast.305, ...), custom_call_target="tpu_custom_call" | custom-call | flops 17600000000 | bytes 1600000 | tf_op jit(solution)/shard_map/pallas_call | solution.py:173
  182.1 12.1 %shard_map.377 = (f32[1024,768]{1,0:T(8,128)}, f32[1024,768]{1,0:T(8,128)}, bf16[1024,768]{1,0:T(8,128)(2,1)}) custom-call(s32[5]{0:T(128)} %concatenate.93.at_ref, bf16[1024,2048]{1,0:T(8,128)(2,1)} %get-tuple-element.144.z_ref.refs_0_, f32[1024,768]{1,0:T(8,128)} %get-tuple-element.145.r_ref, f32[4,768]{1,0:T(4,128)} %convert_element_type.270.gain_ref, ...), custom_call_target="tpu_custom_call" | custom-call | flops 13200000000 | bytes 1200000 | tf_op jit(solution)/shard_map/pallas_call | solution.py:173
  196.9 10.2 %shard_map.378 = (bf16[1024,768]{1,0:T(8,128)(2,1)}, bf16[1024,768]{1,0:T(8,128)(2,1)}, bf16[1024,768]{1,0:T(8,128)(2,1)}) custom-call(s32[5]{0:T(128)} %concatenate.93.at_ref, bf16[1024,768]{1,0:T(8,128)(2,1)} %get-tuple-element.148.a_ref.refs_0_, f32[1024,128]{1,0:T(8,128)} %get-tuple-element.341.cos_ref, f32[1024,128]{1,0:T(8,128)} %get-tuple-element.342.sin_ref, ...), custom_call_target="tpu_custom_call" | custom-call | flops 11000000512 | bytes 1000000 | tf_op jit(solution)/shard_map/pallas_call | solution.py:173
  207.1 11.4 %collective-permute-done.49.refs_3_ = bf16[4,48,2432]{2,1,0:T(8,128)(2,1)} collective-permute-done((bf16[4,48,2432]{2,1,0:T(8,128)(2,1)S(1)}, bf16[4,48,2432]{2,1,0:T(8,128)(2,1)}, u32[]{:S(2)}, u32[]{:S(2)}) %collective-permute-start.49) | collective-permute-done | bytes 933920 | tf_op jit(solution)/shard_map/ppermute | solution.py:39
  219.4 12.8 %shard_map.379 = (bf16[1024,768]{1,0:T(8,128)(2,1)}, f32[6,16,1024]{2,1,0:T(8,128)}) custom-call(s32[5]{0:T(128)} %concatenate.93.at_ref, bf16[1024,768]{1,0:T(8,128)(2,1)} %get-tuple-element.180.q_ref, bf16[1024,768]{1,0:T(8,128)(2,1)} %get-tuple-element.155.k_ref, bf16[1024,768]{1,0:T(8,128)(2,1)} %get-tuple-element.156.v_ref), custom_call_target="tpu_custom_call" | custom-call | flops 13200000000 | bytes 1200000 | tf_op jit(solution)/shard_map/pallas_call | solution.py:173
  234.8 12.7 %shard_map.380 = (bf16[1024,768]{1,0:T(8,128)(2,1)}, f32[6,16,1024]{2,1,0:T(8,128)}) custom-call(s32[5]{0:T(128)} %concatenate.93.at_ref, bf16[1024,768]{1,0:T(8,128)(2,1)} %get-tuple-element.180.q_ref, bf16[1024,768]{1,0:T(8,128)(2,1)} %get-tuple-element.155.k_ref, ...), custom_call_target="tpu_custom_call", output_to_operand_aliasing={{0}: (4, {}), {1}: (5, {})} | custom-call | flops 13200000000 | bytes 1200000 | tf_op jit(solution)/shard_map/pallas_call | solution.py:173
  249.6 17.2 %shard_map.381 = (f32[1024,768]{1,0:T(8,128)}, bf16[1024,768]{1,0:T(8,128)(2,1)}, bf16[1024,2048]{1,0:T(8,128)(2,1)}, bf16[1024,2048]{1,0:T(8,128)(2,1)}, bf16[1024,2048]{1,0:T(8,128)(2,1)}) custom-call(s32[5]{0:T(128)} %concatenate.93.at_ref, bf16[1024,768]{1,0:T(8,128)(2,1)} %get-tuple-element.159.o_ref.refs_0_, ...), custom_call_target="tpu_custom_call" | custom-call | flops 17600000000 | bytes 1600000 | tf_op jit(solution)/shard_map/pallas_call | solution.py:173
  268.0 27.5 %shard_map.383 = (bf16[1024,2048]{1,0:T(8,128)(2,1)}, bf16[1024,2048]{1,0:T(8,128)(2,1)}, f32[1024,768]{1,0:T(8,128)}, bf16[1024,768]{1,0:T(8,128)(2,1)}, bf16[1024,768]{1,0:T(8,128)(2,1)}, /*index=5*/f32[8,768]{1,0:T(8,128)}) custom-call(s32[5]{0:T(128)} %concatenate.93.at_ref, bf16[1024,768]{1,0:T(8,128)(2,1)} %bitcast.300, bf16[1024,768]{1,0:T(8,128)(2,1)} %bitcast.301, ...), custom_call_target="tpu_custom_call" | custom-call | flops 29699999744 | bytes 2700000 | tf_op jit(solution)/shard_map/pallas_call | solution.py:173
  301.5 9.7 %shard_map.385 = bf16[768,2432]{1,0:T(8,128)(2,1)} custom-call(s32[1]{0:T(128)S(6)} %sub.55.half_ref, bf16[1024,768]{1,0:T(8,128)(2,1)} %get-tuple-element.159.o_ref.refs_0_, bf16[1024,768]{1,0:T(8,128)(2,1)} %get-tuple-element.169.refs_1_, bf16[1024,768]{1,0:T(8,128)(2,1)} %get-tuple-element.170.refs_2_, bf16[1024,2048]{1,0:T(8,128)(2,1)} %get-tuple-element.171.refs_3_, ...), custom_call_target="tpu_custom_call" | custom-call | flops 7699999744 | bytes 700000 | tf_op jit(solution)/shard_map/pallas_call | solution.py:173
  312.3 7.4 %collective-permute-done.64.refs_2_ = bf16[2048,384]{1,0:T(8,128)(2,1)S(1)} collective-permute-done((bf16[2048,384]{1,0:T(8,128)(2,1)S(1)}, bf16[2048,384]{1,0:T(8,128)(2,1)S(1)}, u32[]{:S(2)}, u32[]{:S(2)}) %collective-permute-start.64) | collective-permute-done | bytes 1572896 | tf_op jit(solution)/shard_map/ppermute | solution.py:39
  320.9 6.4 shard_map.386
  329.9 10.7 %shard_map.387 = bf16[768,2432]{1,0:T(8,128)(2,1)} custom-call(s32[1]{0:T(128)} %bitcast.3.half_ref, bf16[1024,768]{1,0:T(8,128)(2,1)} %get-tuple-element.159.o_ref.refs_0_, bf16[1024,768]{1,0:T(8,128)(2,1)} %get-tuple-element.169.refs_1_, bf16[1024,768]{1,0:T(8,128)(2,1)} %get-tuple-element.170.refs_2_, bf16[1024,2048]{1,0:T(8,128)(2,1)} %get-tuple-element.171.refs_3_, ...), custom_call_target="tpu_custom_call" | custom-call | flops 7699999744 | bytes 700000 | tf_op jit(solution)/shard_map/pallas_call | solution.py:173
  340.5 16.0 %shard_map.388 = (bf16[1024,768]{1,0:T(8,128)(2,1)}, bf16[1024,768]{1,0:T(8,128)(2,1)}, bf16[1024,768]{1,0:T(8,128)(2,1)}) custom-call(s32[5]{0:T(128)} %concatenate.93.at_ref, bf16[1024,768]{1,0:T(8,128)(2,1)} %get-tuple-element.180.q_ref, bf16[1024,768]{1,0:T(8,128)(2,1)} %get-tuple-element.155.k_ref, bf16[1024,768]{1,0:T(8,128)(2,1)} %get-tuple-element.156.v_ref, ...), custom_call_target="tpu_custom_call" | custom-call | flops 16499999744 | bytes 1500000 | tf_op jit(solution)/shard_map/pallas_call | solution.py:173
  364.8 15.7 %shard_map.389 = (bf16[1024,768]{1,0:T(8,128)(2,1)}, bf16[1024,768]{1,0:T(8,128)(2,1)}, bf16[1024,768]{1,0:T(8,128)(2,1)}) custom-call(s32[5]{0:T(128)} %concatenate.93.at_ref, bf16[1024,768]{1,0:T(8,128)(2,1)} %get-tuple-element.180.q_ref, bf16[1024,768]{1,0:T(8,128)(2,1)} %get-tuple-element.155.k_ref, ...), custom_call_target="tpu_custom_call", output_to_operand_aliasing={{0}: (9, {}), {1}: (10, {}), {2}: (11, {})} | custom-call | flops 16499999744 | bytes 1500000 | tf_op jit(solution)/shard_map/pallas_call | solution.py:173
  399.6 14.1 %shard_map.391 = (f32[1024,768]{1,0:T(8,128)}, bf16[1024,768]{1,0:T(8,128)(2,1)}, f32[8,768]{1,0:T(8,128)}, f32[8,768]{1,0:T(8,128)}) custom-call(s32[5]{0:T(128)} %concatenate.93.at_ref, bf16[1024,768]{1,0:T(8,128)(2,1)} %get-tuple-element.183.refs_1_.dq_ref, bf16[1024,768]{1,0:T(8,128)(2,1)} %get-tuple-element.187.refs_2_.dk_ref, ...), custom_call_target="tpu_custom_call" | custom-call | flops 15399999488 | bytes 1400000 | tf_op jit(solution)/shard_map/pallas_call | solution.py:173
  422.1 6.5 shard_map.392
  430.2 27.5 %shard_map.393 = (bf16[1024,2048]{1,0:T(8,128)(2,1)}, bf16[1024,2048]{1,0:T(8,128)(2,1)}, f32[1024,768]{1,0:T(8,128)}, bf16[1024,768]{1,0:T(8,128)(2,1)}, bf16[1024,768]{1,0:T(8,128)(2,1)}, /*index=5*/f32[8,768]{1,0:T(8,128)}) custom-call(s32[5]{0:T(128)} %concatenate.93.at_ref, f32[1024,768]{1,0:T(8,128)} %get-tuple-element.191.du_ref, ...), custom_call_target="tpu_custom_call" | custom-call | flops 29699999744 | bytes 2700000 | tf_op jit(solution)/shard_map/pallas_call | solution.py:173
  462.0 9.2 %collective-permute-done.77 = bf16[4,2,48,1152]{3,2,0,1:T(8,128)(2,1)S(1)} collective-permute-done((bf16[4,2,48,1152]{3,2,0,1:T(8,128)(2,1)S(1)}, bf16[4,2,48,1152]{3,2,0,1:T(8,128)(2,1)S(1)}, u32[]{:S(2)}, u32[]{:S(2)}) %collective-permute-start.77) | collective-permute-done | bytes 884768 | tf_op jit(solution)/shard_map/ppermute | solution.py:39
  477.5 9.5 %shard_map.395 = bf16[768,2432]{1,0:T(8,128)(2,1)} custom-call(s32[1]{0:T(128)S(6)} %sub.55.half_ref, bf16[1024,768]{1,0:T(8,128)(2,1)} %get-tuple-element.143.o_ref.refs_0_, bf16[1024,768]{1,0:T(8,128)(2,1)} %get-tuple-element.205.refs_1_, bf16[1024,768]{1,0:T(8,128)(2,1)} %get-tuple-element.206.refs_2_, bf16[1024,2048]{1,0:T(8,128)(2,1)} %get-tuple-element.207.refs_3_, ...), custom_call_target="tpu_custom_call" | custom-call | flops 7699999744 | bytes 700000 | tf_op jit(solution)/shard_map/pallas_call | solution.py:173
  512.3 6.4 shard_map.396
  522.1 10.5 %shard_map.397 = bf16[768,2432]{1,0:T(8,128)(2,1)} custom-call(s32[1]{0:T(128)} %bitcast.3.half_ref, bf16[1024,768]{1,0:T(8,128)(2,1)} %get-tuple-element.143.o_ref.refs_0_, bf16[1024,768]{1,0:T(8,128)(2,1)} %get-tuple-element.205.refs_1_, bf16[1024,768]{1,0:T(8,128)(2,1)} %get-tuple-element.206.refs_2_, bf16[1024,2048]{1,0:T(8,128)(2,1)} %get-tuple-element.207.refs_3_, ...), custom_call_target="tpu_custom_call" | custom-call | flops 7699999744 | bytes 700000 | tf_op jit(solution)/shard_map/pallas_call | solution.py:173
  532.6 15.7 %shard_map.398 = (bf16[1024,768]{1,0:T(8,128)(2,1)}, bf16[1024,768]{1,0:T(8,128)(2,1)}, bf16[1024,768]{1,0:T(8,128)(2,1)}) custom-call(s32[5]{0:T(128)} %concatenate.93.at_ref, bf16[1024,768]{1,0:T(8,128)(2,1)} %get-tuple-element.219.q_ref, bf16[1024,768]{1,0:T(8,128)(2,1)} %get-tuple-element.137.k_ref, bf16[1024,768]{1,0:T(8,128)(2,1)} %get-tuple-element.138.v_ref, ...), custom_call_target="tpu_custom_call" | custom-call | flops 16499999744 | bytes 1500000 | tf_op jit(solution)/shard_map/pallas_call | solution.py:173
  558.4 15.8 %shard_map.399 = (bf16[1024,768]{1,0:T(8,128)(2,1)}, bf16[1024,768]{1,0:T(8,128)(2,1)}, bf16[1024,768]{1,0:T(8,128)(2,1)}) custom-call(s32[5]{0:T(128)} %concatenate.93.at_ref, bf16[1024,768]{1,0:T(8,128)(2,1)} %get-tuple-element.219.q_ref, bf16[1024,768]{1,0:T(8,128)(2,1)} %get-tuple-element.137.k_ref, ...), custom_call_target="tpu_custom_call", output_to_operand_aliasing={{0}: (9, {}), {1}: (10, {}), {2}: (11, {})} | custom-call | flops 16499999744 | bytes 1500000 | tf_op jit(solution)/shard_map/pallas_call | solution.py:173
  586.7 5.9 shard_map.400
  592.8 11.2 %shard_map.382 = f32[1024,768]{1,0:T(8,128)} custom-call(s32[5]{0:T(128)} %concatenate.93.at_ref, bf16[1024,2048]{1,0:T(8,128)(2,1)} %get-tuple-element.160.z_ref.refs_0_, f32[1024,768]{1,0:T(8,128)} %get-tuple-element.161.r_ref, bf16[4,128,384]{2,1,0:T(8,128)(2,1)} %copy-done.25, bf16[4,128,384]{2,1,0:T(8,128)(2,1)} %copy-done.49, ...), custom_call_target="tpu_custom_call" | custom-call | flops 6600000000 | bytes 600000 | tf_op jit(solution)/shard_map/pallas_call | solution.py:173
  620.6 6.5 shard_map.401
  632.7 10.9 %shard_map.402 = f32[1024,768]{1,0:T(8,128)} custom-call(s32[5]{0:T(128)} %concatenate.93.at_ref, bf16[1024,768]{1,0:T(8,128)(2,1)} %get-tuple-element.222.refs_1_.dq_ref, bf16[1024,768]{1,0:T(8,128)(2,1)} %get-tuple-element.227.refs_2_.dk_ref, bf16[1024,768]{1,0:T(8,128)(2,1)} %get-tuple-element.228.refs_3_.dv_ref, f32[1024,768]{1,0:T(8,128)} %get-tuple-element.199.du_ref, ...), custom_call_target="tpu_custom_call" | custom-call | flops 8800000000 | bytes 800000 | tf_op jit(solution)/shard_map/pallas_call | solution.py:173
  (490 shorter events, 291.9 us)
Async XLA Ops:
  23.2 49.5 %collective-permute-start.17 = (bf16[4,96]{1,0:T(4,128)(2,1)S(1)}, bf16[4,96]{1,0:T(4,128)(2,1)S(1)}, u32[]{:S(2)}, u32[]{:S(2)}) collective-permute-start(bf16[4,96]{1,0:T(4,128)(2,1)S(1)} %pad_maximum_fusion.33), channel_id=1, source_target_pairs={{0,8},{1,9},{2,10},{3,11},{4,12},{5,13},{6,14},{7,15},{8,16},{9,17... | collective-permute-start | bytes 2312 | tf_op jit(solution)/shard_map/ppermute | solution.py:39
  37.4 25.1 %collective-permute-start.13 = (bf16[4,48,2432]{2,1,0:T(8,128)(2,1)S(1)}, bf16[4,48,2432]{2,1,0:T(8,128)(2,1)}, u32[]{:S(2)}, u32[]{:S(2)}) collective-permute-start(bf16[4,48,2432]{2,1,0:T(8,128)(2,1)S(1)} %pad_maximum_fusion.refs_0_), channel_id=1, source_target_pairs={{0,2},{1,5},{2,0},{3,7},{4,6},{5,1},{6,4},{7,3},{8,10},{9,13},{10,... | collective-permute-start | bytes 2801672 | tf_op jit(solution)/shard_map/ppermute | solution.py:39
  62.5 41.2 %collective-permute-start.22 = (bf16[4,48,2432]{2,1,0:T(8,128)(2,1)}, bf16[4,48,2432]{2,1,0:T(8,128)(2,1)}, u32[]{:S(2)}, u32[]{:S(2)}) collective-permute-start(bf16[4,48,2432]{2,1,0:T(8,128)(2,1)} %collective-permute-done.13.refs_1_), channel_id=1, source_target_pairs={{0,4},{1,3},{2,6},{3,1},{4,0},{5,7},{6,2},{7,5},{8,12},{9,11},{10,... | collective-permute-start | bytes 2801672 | tf_op jit(solution)/shard_map/ppermute | solution.py:39
  67.2 29.2 %collective-permute-start.44 = (bf16[48,2432]{1,0:T(8,128)(2,1)S(1)}, bf16[48,2432]{1,0:T(8,128)(2,1)S(1)}, u32[]{:S(2)}, u32[]{:S(2)}) collective-permute-start(bf16[48,2432]{1,0:T(8,128)(2,1)S(1)} %pad_maximum_fusion.23), channel_id=1, source_target_pairs={{0,8},{1,9},{2,10},{3,11},{4,12},{5,13},{6,14},{7,15},{8,16},{9,17... | collective-permute-start | bytes 700424 | tf_op jit(solution)/shard_map/ppermute | solution.py:39
  70.1 27.3 %collective-permute-start.45 = (bf16[48,2432]{1,0:T(8,128)(2,1)S(1)}, bf16[48,2432]{1,0:T(8,128)(2,1)S(1)}, u32[]{:S(2)}, u32[]{:S(2)}) collective-permute-start(bf16[48,2432]{1,0:T(8,128)(2,1)S(1)} %pad_maximum_fusion.23), channel_id=1, source_target_pairs={{0,16},{1,17},{2,18},{3,19},{4,20},{5,21},{6,22},{7,23},{8,24},{9,... | collective-permute-start | bytes 700424 | tf_op jit(solution)/shard_map/ppermute | solution.py:39
  71.6 25.9 %collective-permute-start.46 = (bf16[48,2432]{1,0:T(8,128)(2,1)S(1)}, bf16[48,2432]{1,0:T(8,128)(2,1)S(1)}, u32[]{:S(2)}, u32[]{:S(2)}) collective-permute-start(bf16[48,2432]{1,0:T(8,128)(2,1)S(1)} %pad_maximum_fusion.23), channel_id=1, source_target_pairs={{0,24},{1,25},{2,26},{3,27},{4,28},{5,29},{6,30},{7,31},{8,0},{9,1... | collective-permute-start | bytes 700424 | tf_op jit(solution)/shard_map/ppermute | solution.py:39
  112.3 35.4 %collective-permute-start.23 = (bf16[4,48,2432]{2,1,0:T(8,128)(2,1)S(1)}, bf16[4,48,2432]{2,1,0:T(8,128)(2,1)}, u32[]{:S(2)}, u32[]{:S(2)}) collective-permute-start(bf16[4,48,2432]{2,1,0:T(8,128)(2,1)S(1)} %pad_maximum_fusion.refs_0_), channel_id=1, source_target_pairs={{0,1},{1,0},{2,3},{3,2},{4,5},{5,4},{6,7},{7,6},{8,9},{9,8},{10,11... | collective-permute-start | bytes 2801672 | tf_op jit(solution)/shard_map/ppermute | solution.py:39
  112.4 33.8 %collective-permute-start.21 = (bf16[4,48,2432]{2,1,0:T(8,128)(2,1)S(1)}, bf16[4,48,2432]{2,1,0:T(8,128)(2,1)}, u32[]{:S(2)}, u32[]{:S(2)}) collective-permute-start(bf16[4,48,2432]{2,1,0:T(8,128)(2,1)S(1)} %pad_maximum_fusion.refs_0_), channel_id=1, source_target_pairs={{0,4},{1,3},{2,6},{3,1},{4,0},{5,7},{6,2},{7,5},{8,12},{9,11},{10,... | collective-permute-start | bytes 2801672 | tf_op jit(solution)/shard_map/ppermute | solution.py:39
  194.3 39.5 %collective-permute-start.50 = (bf16[4,48,2432]{2,1,0:T(8,128)(2,1)S(1)}, bf16[4,48,2432]{2,1,0:T(8,128)(2,1)S(1)}, u32[]{:S(2)}, u32[]{:S(2)}) collective-permute-start(bf16[4,48,2432]{2,1,0:T(8,128)(2,1)S(1)} %pad_maximum_fusion.1.refs_0_), channel_id=1, source_target_pairs={{0,1},{1,0},{2,3},{3,2},{4,5},{5,4},{6,7},{7,6},{8,9},{9,8},{10,11... | collective-permute-start | bytes 2801672 | tf_op jit(solution)/shard_map/ppermute | solution.py:39
  194.8 37.3 %collective-permute-start.48 = (bf16[4,48,2432]{2,1,0:T(8,128)(2,1)S(1)}, bf16[4,48,2432]{2,1,0:T(8,128)(2,1)}, u32[]{:S(2)}, u32[]{:S(2)}) collective-permute-start(bf16[4,48,2432]{2,1,0:T(8,128)(2,1)S(1)} %pad_maximum_fusion.1.refs_0_), channel_id=1, source_target_pairs={{0,4},{1,3},{2,6},{3,1},{4,0},{5,7},{6,2},{7,5},{8,12},{9,11},{10,... | collective-permute-start | bytes 2801672 | tf_op jit(solution)/shard_map/ppermute | solution.py:39
  328.8 27.7 %collective-permute-start.67 = (bf16[4,2,128,384]{3,2,1,0:T(8,128)(2,1)S(1)}, bf16[4,2,128,384]{3,2,1,0:T(8,128)(2,1)S(1)}, u32[]{:S(2)}, u32[]{:S(2)}) collective-permute-start(bf16[4,2,128,384]{3,2,1,0:T(8,128)(2,1)S(1)} %bitcast_select_fusion.10), channel_id=1, source_target_pairs={{0,4},{1,3},{2,6},{3,1},{4,0},{5,7},{6,2},{7,5},{8,12},{9,11},{10,... | collective-permute-start | bytes 2359304 | tf_op jit(solution)/shard_map/ppermute | solution.py:39
  363.6 24.8 %collective-permute-start.66 = (bf16[4,2,48,2432]{3,2,1,0:T(8,128)(2,1)}, bf16[4,2,48,2432]{3,2,1,0:T(8,128)(2,1)}, u32[]{:S(2)}, u32[]{:S(2)}) collective-permute-start(bf16[4,2,48,2432]{3,2,1,0:T(8,128)(2,1)} %bitcast_select_fusion.2), channel_id=1, source_target_pairs={{0,4},{1,3},{2,6},{3,1},{4,0},{5,7},{6,2},{7,5},{8,12},{9,11},{10,... | collective-permute-start | bytes 5603336 | tf_op jit(solution)/shard_map/ppermute | solution.py:39
  381.7 32.1 %collective-permute-start.70 = (bf16[128,384]{1,0:T(8,128)(2,1)S(1)}, bf16[128,384]{1,0:T(8,128)(2,1)}, u32[]{:S(2)}, u32[]{:S(2)}) collective-permute-start(bf16[128,384]{1,0:T(8,128)(2,1)S(1)} %get-tuple-element.311), channel_id=1, source_target_pairs={{0,8},{1,9},{2,10},{3,11},{4,12},{5,13},{6,14},{7,15},{8,16},{9,17... | collective-permute-start | bytes 294920 | tf_op jit(solution)/shard_map/ppermute | solution.py:39
  383.8 30.0 %collective-permute-start.71 = (bf16[128,384]{1,0:T(8,128)(2,1)S(1)}, bf16[128,384]{1,0:T(8,128)(2,1)}, u32[]{:S(2)}, u32[]{:S(2)}) collective-permute-start(bf16[128,384]{1,0:T(8,128)(2,1)S(1)} %get-tuple-element.310), channel_id=1, source_target_pairs={{0,16},{1,17},{2,18},{3,19},{4,20},{5,21},{6,22},{7,23},{8,24},{9,... | collective-permute-start | bytes 294920 | tf_op jit(solution)/shard_map/ppermute | solution.py:39
  384.2 29.6 %collective-permute-start.72 = (bf16[128,384]{1,0:T(8,128)(2,1)S(1)}, bf16[128,384]{1,0:T(8,128)(2,1)}, u32[]{:S(2)}, u32[]{:S(2)}) collective-permute-start(bf16[128,384]{1,0:T(8,128)(2,1)S(1)} %get-tuple-element.309), channel_id=1, source_target_pairs={{0,24},{1,25},{2,26},{3,27},{4,28},{5,29},{6,30},{7,31},{8,0},{9,1... | collective-permute-start | bytes 294920 | tf_op jit(solution)/shard_map/ppermute | solution.py:39
  391.9 24.7 %collective-permute-start.69 = (bf16[4,48,2432]{2,1,0:T(8,128)(2,1)S(1)}, bf16[4,48,2432]{2,1,0:T(8,128)(2,1)S(1)}, u32[]{:S(2)}, u32[]{:S(2)}) collective-permute-start(bf16[4,48,2432]{2,1,0:T(8,128)(2,1)S(1)} %dynamic-slice_bitcast_fusion.1), channel_id=1, source_target_pairs={{0,2},{1,5},{2,0},{3,7},{4,6},{5,1},{6,4},{7,3},{8,10},{9,13},{10,... | collective-permute-start | bytes 2801672 | tf_op jit(solution)/shard_map/ppermute | solution.py:39
  415.5 42.4 %collective-permute-start.78 = (bf16[128,384]{1,0:T(8,128)(2,1)}, bf16[128,384]{1,0:T(8,128)(2,1)}, u32[]{:S(2)}, u32[]{:S(2)}) collective-permute-start(bf16[128,384]{1,0:T(8,128)(2,1)} %add_convert_fusion.10), channel_id=1, source_target_pairs={{0,2},{1,3},{2,0},{3,1},{4,6},{5,7},{6,4},{7,5},{8,10},{9,11},{10,... | collective-permute-start | bytes 294920 | tf_op jit(solution)/shard_map/ppermute | solution.py:39
  417.7 43.0 %collective-permute-start.74 = (bf16[48,2432]{1,0:T(8,128)(2,1)}, bf16[48,2432]{1,0:T(8,128)(2,1)}, u32[]{:S(2)}, u32[]{:S(2)}) collective-permute-start(bf16[48,2432]{1,0:T(8,128)(2,1)} %get-tuple-element.272), channel_id=1, source_target_pairs={{0,8},{1,9},{2,10},{3,11},{4,12},{5,13},{6,14},{7,15},{8,16},{9,17... | collective-permute-start | bytes 700424 | tf_op jit(solution)/shard_map/ppermute | solution.py:39
  419.8 40.9 %collective-permute-start.75 = (bf16[48,2432]{1,0:T(8,128)(2,1)}, bf16[48,2432]{1,0:T(8,128)(2,1)}, u32[]{:S(2)}, u32[]{:S(2)}) collective-permute-start(bf16[48,2432]{1,0:T(8,128)(2,1)} %get-tuple-element.271), channel_id=1, source_target_pairs={{0,16},{1,17},{2,18},{3,19},{4,20},{5,21},{6,22},{7,23},{8,24},{9,... | collective-permute-start | bytes 700424 | tf_op jit(solution)/shard_map/ppermute | solution.py:39
  420.2 40.5 %collective-permute-start.76 = (bf16[48,2432]{1,0:T(8,128)(2,1)}, bf16[48,2432]{1,0:T(8,128)(2,1)}, u32[]{:S(2)}, u32[]{:S(2)}) collective-permute-start(bf16[48,2432]{1,0:T(8,128)(2,1)} %get-tuple-element.270), channel_id=1, source_target_pairs={{0,24},{1,25},{2,26},{3,27},{4,28},{5,29},{6,30},{7,31},{8,0},{9,1... | collective-permute-start | bytes 700424 | tf_op jit(solution)/shard_map/ppermute | solution.py:39
  487.1 34.1 %collective-permute-start.82 = (bf16[768,2432]{1,0:T(8,128)(2,1)}, bf16[768,2432]{1,0:T(8,128)(2,1)}, u32[]{:S(2)}, u32[]{:S(2)}) collective-permute-start(bf16[768,2432]{1,0:T(8,128)(2,1)} %shard_map.395), channel_id=1, source_target_pairs={{0,1},{1,0},{2,3},{3,2},{4,5},{5,4},{6,7},{7,6},{8,9},{9,8},{10,11... | collective-permute-start | bytes 11206664 | tf_op jit(solution)/shard_map/ppermute | solution.py:39
  497.2 106.8 %collective-permute-start.111 = (f32[4,768]{1,0:T(4,128)S(1)}, f32[4,768]{1,0:T(4,128)S(1)}, u32[]{:S(2)}, u32[]{:S(2)}) collective-permute-start(f32[4,768]{1,0:T(4,128)S(1)} %fusion.40), channel_id=1, source_target_pairs={{0,4},{1,5},{2,6},{3,7},{4,0},{5,1},{6,2},{7,3},{8,12},{9,13},{10,... | collective-permute-start | bytes 36872 | tf_op jit(solution)/shard_map/ppermute | solution.py:39
  507.5 44.6 %collective-permute-start.85 = (bf16[48,1152]{1,0:T(8,128)(2,1)}, bf16[48,1152]{1,0:T(8,128)(2,1)}, u32[]{:S(2)}, u32[]{:S(2)}) collective-permute-start(bf16[48,1152]{1,0:T(8,128)(2,1)} %get-tuple-element.299), channel_id=1, source_target_pairs={{0,8},{1,9},{2,10},{3,11},{4,12},{5,13},{6,14},{7,15},{8,16},{9,17... | collective-permute-start | bytes 331784 | tf_op jit(solution)/shard_map/ppermute | solution.py:39
  507.9 44.2 %collective-permute-start.86 = (bf16[48,1152]{1,0:T(8,128)(2,1)}, bf16[48,1152]{1,0:T(8,128)(2,1)}, u32[]{:S(2)}, u32[]{:S(2)}) collective-permute-start(bf16[48,1152]{1,0:T(8,128)(2,1)} %get-tuple-element.298), channel_id=1, source_target_pairs={{0,16},{1,17},{2,18},{3,19},{4,20},{5,21},{6,22},{7,23},{8,24},{9,... | collective-permute-start | bytes 331784 | tf_op jit(solution)/shard_map/ppermute | solution.py:39
  510.1 42.0 %collective-permute-start.87 = (bf16[48,1152]{1,0:T(8,128)(2,1)}, bf16[48,1152]{1,0:T(8,128)(2,1)}, u32[]{:S(2)}, u32[]{:S(2)}) collective-permute-start(bf16[48,1152]{1,0:T(8,128)(2,1)} %get-tuple-element.297), channel_id=1, source_target_pairs={{0,24},{1,25},{2,26},{3,27},{4,28},{5,29},{6,30},{7,31},{8,0},{9,1... | collective-permute-start | bytes 331784 | tf_op jit(solution)/shard_map/ppermute | solution.py:39
  521.1 27.2 %collective-permute-start.84 = (bf16[4,2,128,384]{3,2,1,0:T(8,128)(2,1)}, bf16[4,2,128,384]{3,2,1,0:T(8,128)(2,1)}, u32[]{:S(2)}, u32[]{:S(2)}) collective-permute-start(bf16[4,2,128,384]{3,2,1,0:T(8,128)(2,1)} %bitcast_select_fusion.8), channel_id=1, source_target_pairs={{0,4},{1,3},{2,6},{3,1},{4,0},{5,7},{6,2},{7,5},{8,12},{9,11},{10,... | collective-permute-start | bytes 2359304 | tf_op jit(solution)/shard_map/ppermute | solution.py:39
  557.3 23.9 %collective-permute-start.83 = (bf16[4,2,48,2432]{3,2,1,0:T(8,128)(2,1)}, bf16[4,2,48,2432]{3,2,1,0:T(8,128)(2,1)}, u32[]{:S(2)}, u32[]{:S(2)}) collective-permute-start(bf16[4,2,48,2432]{3,2,1,0:T(8,128)(2,1)} %bitcast_select_fusion), channel_id=1, source_target_pairs={{0,4},{1,3},{2,6},{3,1},{4,0},{5,7},{6,2},{7,5},{8,12},{9,11},{10,... | collective-permute-start | bytes 5603336 | tf_op jit(solution)/shard_map/ppermute | solution.py:39
  585.6 34.8 %collective-permute-start.88 = (bf16[4,48,2432]{2,1,0:T(8,128)(2,1)}, bf16[4,48,2432]{2,1,0:T(8,128)(2,1)S(1)}, u32[]{:S(2)}, u32[]{:S(2)}) collective-permute-start(bf16[4,48,2432]{2,1,0:T(8,128)(2,1)} %dynamic-slice_bitcast_fusion), channel_id=1, source_target_pairs={{0,2},{1,5},{2,0},{3,7},{4,6},{5,1},{6,4},{7,3},{8,10},{9,13},{10,... | collective-permute-start | bytes 2801672 | tf_op jit(solution)/shard_map/ppermute | solution.py:39
  592.7 27.9 %collective-permute-start.94 = (bf16[768,1152]{1,0:T(8,128)(2,1)}, bf16[768,1152]{1,0:T(8,128)(2,1)}, u32[]{:S(2)}, u32[]{:S(2)}) collective-permute-start(bf16[768,1152]{1,0:T(8,128)(2,1)} %shard_map.400), channel_id=1, source_target_pairs={{0,1},{1,0},{2,3},{3,2},{4,5},{5,4},{6,7},{7,6},{8,9},{9,8},{10,11... | collective-permute-start | bytes 5308424 | tf_op jit(solution)/shard_map/ppermute | solution.py:39
  617.1 42.0 %collective-permute-start.117 = (bf16[256,384]{1,0:T(8,128)(2,1)}, bf16[256,384]{1,0:T(8,128)(2,1)}, u32[]{:S(2)}, u32[]{:S(2)}) collective-permute-start(bf16[256,384]{1,0:T(8,128)(2,1)} %pad_maximum_fusion.26), channel_id=1, source_target_pairs={{0,1},{1,0},{2,3},{3,2},{4,5},{5,4},{6,7},{7,6},{8,9},{9,8},{10,11... | collective-permute-start | bytes 589832 | tf_op jit(solution)/shard_map/ppermute | solution.py:39
  631.0 23.2 %collective-permute-start.116 = (bf16[96,2432]{1,0:T(8,128)(2,1)}, bf16[96,2432]{1,0:T(8,128)(2,1)}, u32[]{:S(2)}, u32[]{:S(2)}) collective-permute-start(bf16[96,2432]{1,0:T(8,128)(2,1)} %pad_maximum_fusion.8), channel_id=1, source_target_pairs={{0,1},{1,0},{2,3},{3,2},{4,5},{5,4},{6,7},{7,6},{8,9},{9,8},{10,11... | collective-permute-start | bytes 1400840 | tf_op jit(solution)/shard_map/ppermute | solution.py:39
  631.0 29.8 %collective-permute-start.115 = (bf16[96,1152]{1,0:T(8,128)(2,1)}, bf16[96,1152]{1,0:T(8,128)(2,1)}, u32[]{:S(2)}, u32[]{:S(2)}) collective-permute-start(bf16[96,1152]{1,0:T(8,128)(2,1)} %pad_maximum_fusion.24), channel_id=1, source_target_pairs={{0,1},{1,0},{2,3},{3,2},{4,5},{5,4},{6,7},{7,6},{8,9},{9,8},{10,11... | collective-permute-start | bytes 663560 | tf_op jit(solution)/shard_map/ppermute | solution.py:39
  (149 other events, 2132.5 us)

commit v2 on v1

v2 whole, which is shorter than its diff:
```python
import functools
import math

import jax
import jax.numpy as jnp
from jax import lax
from jax.experimental import pallas as pl
from jax.experimental.pallas import tpu as pltpu
from jax.sharding import PartitionSpec as P

HEAD_DIM = 64

epsilon = 1e-06
masked_score = -1e30


class Grid:
    def __init__(self, fsdp, rep):
        self.zs = fsdp // 2
        self.rep = rep

    def flat(self, z, y, x, c):
        return (z * 2 + y) * self.rep + x * 2 + c

    def pairs(self, move):
        out = []
        for z in range(self.zs):
            for y in range(2):
                for x in range(2):
                    for c in range(2):
                        out.append((self.flat(z, y, x, c), self.flat(*move(z, y, x, c))))
        return out


AXES = ("fsdp", "rep")


def send(grid, value, move):
    return lax.ppermute(value, AXES, grid.pairs(move))


def first_flip(z, y, x, c):
    return (z, y, 1 - x, c) if c == 0 else (z, 1 - y, x, c)


def second_flip(z, y, x, c):
    return (z, 1 - y, x, c) if c == 0 else (z, y, 1 - x, c)


def core_flip(z, y, x, c):
    return (z, y, x, 1 - c)


def x_flip(z, y, x, c):
    return (z, y, 1 - x, c)


def y_flip(z, y, x, c):
    return (z, 1 - y, x, c)

BLOCK = 256
PAIR = 2 * HEAD_DIM
VMEM = 32 * 1024 * 1024
F32 = jnp.float32
LOW = jnp.bfloat16


def dot(one, two):
    return jnp.dot(one, two, preferred_element_type=F32)


def dot_nt(one, two):
    return lax.dot_general(one, two, (((1,), (1,)), ((), ())), preferred_element_type=F32)


def dot_tn(one, two):
    return lax.dot_general(one, two, (((0,), (0,)), ((), ())), preferred_element_type=F32)


def inverse_rms(values):
    return lax.rsqrt(jnp.mean(values * values, axis=-1, keepdims=True) + epsilon)


def norm_back(values, scales, upstream):
    inv = inverse_rms(values)
    weighted = upstream * scales
    inner = jnp.mean(weighted * values, axis=-1, keepdims=True)
    return inv * weighted - values * (inv * inv * inv) * inner, upstream * values * inv


def fold_rows(values):
    return jnp.sum(values.reshape(values.shape[0] // 8, 8, values.shape[1]), axis=0)


def silu_parts(gate):
    sig = 0.5 * jnp.tanh(0.5 * gate) + 0.5
    return sig, gate * sig


def piece_place(at_ref, which, k):
    z, y, x, c = at_ref[0], at_ref[1], at_ref[2], at_ref[3]
    cc = c if which < 4 else 1 - c
    first, second = which % 2, (which % 4) // 2
    flip_x = jnp.where(cc == 0, first, second)
    flip_y = jnp.where(cc == 0, second, first)
    return jnp.bitwise_xor(z, k) * 2 + jnp.where(flip_y == 1, 1 - y, y), jnp.where(flip_x == 1, 1 - x, x), cc


def slabs(at_ref, pieces):
    count, rows, _ = pieces[0].shape
    if len(pieces) == 1:
        return [(pieces[0].at[i], i // 2 * rows, i % 2) for i in range(count)], rows
    out = []
    for which in range(8):
        for k in range(count):
            shard, x, c = piece_place(at_ref, which, k)
            row = pl.multiple_of(shard * (2 * rows) + x * rows, 16)
            out.append((pieces[which].at[k], row, c))
    return out, rows


def weight_copies(at_ref, pieces, w_refs, sems):
    copies = []
    places, rows = slabs(at_ref, pieces)
    for slab, row, c in places:
        offset = 0
        for w_ref in w_refs:
            half = w_ref.shape[1] // 2
            col = c * half if isinstance(c, int) else pl.multiple_of(c * half, 128)
            copies.append(
                pltpu.make_async_copy(
                    slab.at[:, pl.ds(offset, half)],
                    w_ref.at[pl.ds(row, rows), pl.ds(col, half)],
                    sems.at[len(copies)],
                )
            )
            offset += half
    return copies


def weight_scratch(pieces, widths):
    count, rows, _ = pieces[0].shape
    tall = count * rows // 2 if len(pieces) == 1 else count * 4 * rows
    copies = len(pieces) * count * len(widths)
    return [pltpu.VMEM((tall, width), LOW) for width in widths] + [
        pltpu.SemaphoreType.DMA((copies,))
    ]


def start_all(copies):
    for copy in copies:
        copy.start()
    return copies


def wait_all(copies):
    for copy in copies:
        copy.wait()


ANYWHERE = pl.BlockSpec(memory_space=pl.ANY)
HELD = pl.BlockSpec(memory_space=pltpu.HBM)
NEAR = pl.BlockSpec(memory_space=pltpu.VMEM)
SCALARS = pl.BlockSpec(memory_space=pltpu.SMEM)
MIB = 1024 * 1024


def cost(micros):
    return pl.CostEstimate(
        flops=int(micros * 1.1e9), bytes_accessed=int(micros * 1e5), transcendentals=0
    )


def call(kernel, at, near, weights, outs, scratch, micros, room):
    weights = [pltpu.with_memory_space_constraint(weight, pltpu.HBM) for weight in weights]
    return pl.pallas_call(
        kernel,
        out_shape=outs,
        in_specs=[SCALARS] + [NEAR] * len(near) + [HELD] * len(weights),
        out_specs=jax.tree.map(lambda _: NEAR, outs),
        scratch_shapes=scratch,
        compiler_params=pltpu.CompilerParams(vmem_limit_bytes=room * MIB),
        cost_estimate=cost(micros),
    )(at, *near, *weights)


def shape_of(shape, dtype):
    return jax.ShapeDtypeStruct(shape, dtype)


def blocks(rows):
    return [slice(first, first + BLOCK) for first in range(0, rows, BLOCK)]


def pair_spec(rows, first_pair):
    return pl.BlockSpec((rows, PAIR), lambda p, at: (0, p + first_pair))


def logs_spec(rows, first_pair):
    return pl.BlockSpec((1, 16, rows), lambda p, at: (p + first_pair, 0, 0))


def whole_spec(shape):
    return pl.BlockSpec(shape, lambda i, at: (0,) * len(shape))


def call_pairs(kernel, at, arrays, specs, outs, out_specs, scratch, steps, micros, aliases):
    arrays = [pltpu.with_memory_space_constraint(array, pltpu.HBM) for array in arrays]
    outs = [pltpu.HBM(out.shape, out.dtype) for out in outs]
    return pl.pallas_call(
        kernel,
        out_shape=outs,
        grid_spec=pltpu.PrefetchScalarGridSpec(
            num_scalar_prefetch=1,
            grid=(steps,),
            in_specs=specs,
            out_specs=out_specs,
            scratch_shapes=scratch,
        ),
        input_output_aliases=aliases,
        compiler_params=pltpu.CompilerParams(vmem_limit_bytes=16 * MIB),
        cost_estimate=cost(micros),
    )(at, *arrays)


def turn_lanes(values, lane):
    return jnp.where(
        (lane & (HEAD_DIM - 1)) < HEAD_DIM // 2,
        pltpu.roll(values, PAIR - HEAD_DIM // 2, 1),
        pltpu.roll(values, HEAD_DIM // 2, 1),
    )


def project_heads(at, inputs, pieces, cosine, sine):
    rows, width = inputs.shape
    n = len(pieces)

    def kernel(at_ref, a_ref, cos_ref, sin_ref, *refs):
        parts, (q_ref, k_ref, v_ref), (*w_refs, sems) = refs[:n], refs[n : n + 3], refs[n + 3 :]
        wait_all(start_all(weight_copies(at_ref, parts, w_refs, sems)))
        lane = lax.broadcasted_iota(jnp.int32, (BLOCK, PAIR), 1)
        for block in blocks(rows):
            a = a_ref[block, :]
            cos, sin = cos_ref[block, :], sin_ref[block, :]
            for first in range(0, width, 2 * PAIR):
                q = dot(a, w_refs[0][:, first : first + 2 * PAIR])
                k = dot(a, w_refs[1][:, first : first + 2 * PAIR])
                v = dot(a, w_refs[2][:, first : first + 2 * PAIR])
                for t in range(2):
                    here = slice(first + t * PAIR, first + (t + 1) * PAIR)
                    q_pair = q[:, t * PAIR : (t + 1) * PAIR]
                    k_pair = k[:, t * PAIR : (t + 1) * PAIR]
                    q_pair = q_pair * cos + turn_lanes(q_pair, lane) * sin
                    q_ref[block, here] = (q_pair * HEAD_DIM**-0.5).astype(LOW)
                    k_ref[block, here] = (k_pair * cos + turn_lanes(k_pair, lane) * sin).astype(LOW)
                v_ref[block, first : first + 2 * PAIR] = v.astype(LOW)

    return call(
        kernel,
        at,
        [inputs, cosine, sine],
        pieces,
        [shape_of((rows, width), LOW)] * 3,
        weight_scratch(pieces, (width,) * 3),
        8,
        16,
    )


def head_masks(head, lane):
    own = lane < HEAD_DIM if head == 0 else lane >= HEAD_DIM
    return own, lane == (HEAD_DIM if head == 0 else 0)


def attend(at, queries, key_rows, value_rows, first_pair, pairs, before=()):
    rows, width = queries.shape
    every = width // PAIR

    def kernel(at_ref, q_ref, k_ref, v_ref, *refs):
        o_ref, lse_ref = refs[len(before) :]
        lane = lax.broadcasted_iota(jnp.int32, (rows, PAIR), 1)
        row = lax.broadcasted_iota(jnp.int32, (rows, PAIR), 0)
        bias = jnp.where(row < at_ref[4], 0.0, masked_score)
        q, k, v = q_ref[...].astype(F32), k_ref[...].astype(F32), v_ref[...].astype(F32)
        below = lax.broadcasted_iota(jnp.int32, (BLOCK, BLOCK), 0) >= lax.broadcasted_iota(
            jnp.int32, (BLOCK, BLOCK), 1
        )
        heads = []
        for head in range(2):
            own, mark = head_masks(head, lane)
            heads.append(
                (
                    jnp.where(own, q, jnp.where(mark, 1.0, 0.0)).astype(LOW),
                    jnp.where(own, k, jnp.where(mark, bias, 0.0)).astype(LOW),
                    jnp.where(own, v, 1.0).astype(LOW),
                )
            )
        lane_here = lane[:BLOCK]
        for first in range(0, rows, BLOCK):
            end = first + BLOCK
            mixed, logs = [], []
            for qh, kh, vh in heads:
                scores = [
                    dot_nt(qh[first:end], kh[start : start + BLOCK]) for start in range(0, end, BLOCK)
                ]
                scores[-1] = jnp.where(below, scores[-1], masked_score)
                top = functools.reduce(jnp.maximum, scores)
                top = jnp.max(top, axis=-1, keepdims=True)
                weights = [jnp.exp(part - top).astype(LOW) for part in scores]
                weights = jnp.concatenate(weights, axis=1) if first else weights[0]
                both = dot(weights, vh[:end])
                total = pltpu.roll(both, HEAD_DIM, 1)
                mixed.append(both / total)
                logs.append(top + jnp.log(total))
            o_ref[first:end, :] = jnp.where(lane_here < HEAD_DIM, mixed[0], mixed[1]).astype(LOW)
            turned = jnp.where(lane_here < HEAD_DIM, logs[0], logs[1]).T
            lse_ref[0, 0:8, first:end] = turned[0:8]
            lse_ref[0, 8:16, first:end] = turned[HEAD_DIM : HEAD_DIM + 8]

    return call_pairs(
        kernel,
        at,
        [queries, key_rows, value_rows, *before],
        [pair_spec(rows, first_pair)] * 3 + [ANYWHERE] * len(before),
        [shape_of((rows, width), LOW), shape_of((every, 16, rows), F32)],
        [pair_spec(rows, first_pair), logs_spec(rows, first_pair)],
        [],
        pairs,
        4 * pairs,
        {4 + i: i for i in range(len(before))},
    )


def attend_back(
    at, queries, key_rows, value_rows, mixed, logs, upstream, cosine, sine, first_pair, pairs, before=()
):
    rows, width = queries.shape

    def kernel(at_ref, q_ref, k_ref, v_ref, o_ref, lse_ref, g_ref, cos_ref, sin_ref, *refs):
        dq_ref, dk_ref, dv_ref, sum_ref = refs[len(before) :]
        lane = lax.broadcasted_iota(jnp.int32, (rows, PAIR), 1)
        row = lax.broadcasted_iota(jnp.int32, (rows, PAIR), 0)
        bias = jnp.where(row < at_ref[4], 0.0, masked_score)
        q, k, v = q_ref[...].astype(F32), k_ref[...].astype(F32), v_ref[...].astype(F32)
        q_low, k_low, g_low = q_ref[...], k_ref[...], g_ref[...]
        above = lax.broadcasted_iota(jnp.int32, (BLOCK, BLOCK), 0) <= lax.broadcasted_iota(
            jnp.int32, (BLOCK, BLOCK), 1
        )
        turned = (g_low.astype(F32) * o_ref[...].astype(F32)).T
        cos, sin = cos_ref[...], sin_ref[...]

        def unrotate(values, first, end):
            moved = values * sin[first:end]
            return values * cos[first:end] + turn_lanes(moved, lane[first:end])

        key_parts, value_parts = [], []
        for head in range(2):
            own, mark = head_masks(head, lane)
            qh = jnp.where(own, q, jnp.where(mark, 1.0, 0.0)).astype(LOW)
            kh = jnp.where(own, k, jnp.where(mark, bias, 0.0)).astype(LOW)
            vh = jnp.where(own, v, 0.0).astype(LOW)
            delta = jnp.sum(
                turned[head * HEAD_DIM : (head + 1) * HEAD_DIM], axis=0, keepdims=True
            )
            lse = lse_ref[0, head * 8 : head * 8 + 1, :]
            key_parts.append([])
            value_parts.append([])
            for first in range(0, rows, BLOCK):
                end = first + BLOCK
                scores = dot_nt(kh[first:end], qh[first:])
                soft = jnp.exp(scores - lse[:, first:])
                edge = jnp.where(above, soft[:, :BLOCK], 0.0)
                if end < rows:
                    soft = jnp.concatenate([edge, soft[:, BLOCK:]], axis=1)
                else:
                    soft = edge
                grad = dot_nt(vh[first:end], g_low[first:])
                grad = (soft * (grad - delta[:, first:])).astype(LOW)
                value_parts[head].append(dot(soft.astype(LOW), g_low[first:]))
                key_parts[head].append(dot(grad, q_low[first:]))
                added = dot_tn(grad, k_low[first:end])
                if first == 0:
                    sum_ref[head] = added
                else:
                    sum_ref[head, first:, :] += added
        lane_here = lane[:BLOCK]
        for step in range(rows // BLOCK):
            first, end = step * BLOCK, (step + 1) * BLOCK
            dk = jnp.where(lane_here < HEAD_DIM, key_parts[0][step], key_parts[1][step])
            dv = jnp.where(lane_here < HEAD_DIM, value_parts[0][step], value_parts[1][step])
            dq = jnp.where(lane_here < HEAD_DIM, sum_ref[0, first:end, :], sum_ref[1, first:end, :])
            dk_ref[first:end, :] = unrotate(dk, first, end).astype(LOW)
            dq_ref[first:end, :] = unrotate(dq * HEAD_DIM**-0.5, first, end).astype(LOW)
            dv_ref[first:end, :] = dv.astype(LOW)

    return call_pairs(
        kernel,
        at,
        [queries, key_rows, value_rows, mixed, logs, upstream, cosine, sine, *before],
        [pair_spec(rows, first_pair)] * 4
        + [logs_spec(rows, first_pair), pair_spec(rows, first_pair)]
        + [whole_spec((rows, PAIR))] * 2
        + [ANYWHERE] * len(before),
        [shape_of((rows, width), LOW)] * 3,
        [pair_spec(rows, first_pair)] * 3,
        [pltpu.VMEM((2, rows, PAIR), F32)],
        pairs,
        5 * pairs,
        {9 + i: i for i in range(len(before))},
    )


def open_block(at, mixed, resid, gain, pieces, wide):
    rows, width = mixed.shape
    n = len(pieces)

    def kernel(at_ref, o_ref, resid_ref, gain_ref, *refs):
        parts, outs, (*w_refs, sems) = refs[:n], refs[n : n + 5], refs[n + 5 :]
        r_ref, hl_ref, gate_ref, up_ref, z_ref = outs
        wait_all(start_all(weight_copies(at_ref, parts, w_refs, sems)))
        for block in blocks(rows):
            r = resid_ref[block, :].astype(F32) + dot(o_ref[block, :], w_refs[0][...])
            r_ref[block, :] = r
            hl = (r * inverse_rms(r) * gain_ref[...]).astype(LOW)
            hl_ref[block, :] = hl
            for first in range(0, wide, BLOCK):
                here = slice(first, first + BLOCK)
                gate = dot(hl, w_refs[1][:, here])
                up = dot(hl, w_refs[2][:, here])
                gate_ref[block, here] = gate.astype(LOW)
                up_ref[block, here] = up.astype(LOW)
                z_ref[block, here] = (silu_parts(gate)[1] * up).astype(LOW)

    return call(
        kernel,
        at,
        [mixed, resid, gain],
        pieces,
        [shape_of((rows, width), F32), shape_of((rows, width), LOW)]
        + [shape_of((rows, wide), LOW)] * 3,
        weight_scratch(pieces, (width, wide, wide)),
        12,
        20,
    )


def close_first(at, hidden, resid, gains, pieces):
    rows, width = resid.shape
    n = len(pieces)

    def kernel(at_ref, z_ref, r_ref, gain_ref, *refs):
        parts, (r2_ref, out_ref, next_ref), (w_ref, sems) = refs[:n], refs[n : n + 3], refs[n + 3 :]
        wait_all(start_all(weight_copies(at_ref, parts, [w_ref], sems)))
        for block in blocks(rows):
            r = r_ref[block, :]
            r2 = r * inverse_rms(r) * gain_ref[0:1] + dot(z_ref[block, :], w_ref[...])
            r2_ref[block, :] = r2
            out = r2 * inverse_rms(r2) * gain_ref[1:2]
            out_ref[block, :] = out
            next_ref[block, :] = (out * inverse_rms(out) * gain_ref[2:3]).astype(LOW)

    return call(
        kernel,
        at,
        [hidden, resid, gains],
        pieces,
        [shape_of((rows, width), F32)] * 2 + [shape_of((rows, width), LOW)],
        weight_scratch(pieces, (width,)),
        8,
        16,
    )


def close_second(at, hidden, resid, pieces):
    rows, width = resid.shape
    n = len(pieces)

    def kernel(at_ref, z_ref, r_ref, *refs):
        parts, out_ref, (w_ref, sems) = refs[:n], refs[n], refs[n + 1 :]
        wait_all(start_all(weight_copies(at_ref, parts, [w_ref], sems)))
        for block in blocks(rows):
            out_ref[block, :] = r_ref[block, :] + dot(z_ref[block, :], w_ref[...])

    return call(
        kernel,
        at,
        [hidden, resid],
        pieces,
        shape_of((rows, width), F32),
        weight_scratch(pieces, (width,)),
        7,
        16,
    )


def feed_back(at, upstream, up_low, gate, up, resid, gain, pieces, down, post):
    rows, width = resid.shape
    wide = gate.shape[1]
    n, m = len(pieces), len(down)

    def kernel(at_ref, du_ref, dl_ref, gate_ref, up_ref, r_ref, gain_ref, *refs):
        parts, down_parts, refs = refs[:n], refs[n : n + m], refs[n + m :]
        dgate_ref, dup_ref, dr_ref, dlow_ref, do_ref, dgain_ref = refs[:6]
        *w_refs, sems, d_ref, d_sems = refs[6:]
        down_copies = start_all(weight_copies(at_ref, down_parts, [d_ref], d_sems))
        copies = start_all(weight_copies(at_ref, parts, w_refs, sems))
        wait_all(down_copies)
        for block in blocks(rows):
            dl = dl_ref[block, :]
            for first in range(0, wide, BLOCK):
                here = slice(first, first + BLOCK)
                dz = dot_nt(dl, d_ref[here, :])
                gate = gate_ref[block, here].astype(F32)
                sig, act = silu_parts(gate)
                dup_ref[block, here] = (dz * act).astype(LOW)
                dgate = dz * up_ref[block, here].astype(F32) * (sig + act * (1.0 - sig))
                dgate_ref[block, here] = dgate.astype(LOW)
        wait_all(copies)
        shares = None
        for block in blocks(rows):
            inward = dot_nt(dgate_ref[block, :], w_refs[1][...])
            inward = inward + dot_nt(dup_ref[block, :], w_refs[2][...])
            du = du_ref[block, :].astype(F32)
            if post:
                dr, share = norm_back(r_ref[block, :], gain_ref[...], du + inward)
            else:
                dr, share = norm_back(r_ref[block, :], gain_ref[...], inward)
                dr = du + dr
            dr_ref[block, :] = dr
            low = dr.astype(LOW)
            dlow_ref[block, :] = low
            do_ref[block, :] = dot_nt(low, w_refs[0][...]).astype(LOW)
            share = fold_rows(share)
            shares = share if shares is None else shares + share
        dgain_ref[...] = shares

    return call(
        kernel,
        at,
        [upstream, up_low, gate, up, resid, gain],
        [*pieces, *down],
        [shape_of((rows, wide), LOW)] * 2
        + [shape_of((rows, width), F32)]
        + [shape_of((rows, width), LOW)] * 2
        + [shape_of((8, width), F32)],
        weight_scratch(pieces, (width, wide, wide)) + weight_scratch(down, (width,)),
        24,
        18,
    )


def heads_inward(block, grad_refs, w_refs):
    inward = dot_nt(grad_refs[0][block, :], w_refs[0][...])
    inward = inward + dot_nt(grad_refs[1][block, :], w_refs[1][...])
    return inward + dot_nt(grad_refs[2][block, :], w_refs[2][...])


def heads_back_second(at, dq, dk, dv, upstream, first_out, resid_two, gains, pieces):
    rows, width = dq.shape
    n = len(pieces)

    def kernel(at_ref, dq_ref, dk_ref, dv_ref, du_ref, h_ref, r_ref, gain_ref, *refs):
        parts, refs = refs[:n], refs[n:]
        dr_ref, dlow_ref, ga_ref, gb_ref, *w_refs, sems = refs
        wait_all(start_all(weight_copies(at_ref, parts, w_refs, sems)))
        sums = [None, None]
        for block in blocks(rows):
            inward = heads_inward(block, (dq_ref, dk_ref, dv_ref), w_refs)
            back, share_a = norm_back(h_ref[block, :], gain_ref[0:1], inward)
            dr, share_b = norm_back(r_ref[block, :], gain_ref[1:2], du_ref[block, :] + back)
            dr_ref[block, :] = dr
            dlow_ref[block, :] = dr.astype(LOW)
            for i, share in enumerate((share_a, share_b)):
                share = fold_rows(share)
                sums[i] = share if sums[i] is None else sums[i] + share
        ga_ref[...] = sums[0]
        gb_ref[...] = sums[1]

    return call(
        kernel,
        at,
        [dq, dk, dv, upstream, first_out, resid_two, gains],
        pieces,
        [shape_of((rows, width), F32), shape_of((rows, width), LOW)]
        + [shape_of((8, width), F32)] * 2,
        weight_scratch(pieces, (width,) * 3),
        8,
        16,
    )


def heads_back_first(at, dq, dk, dv, upstream, pieces):
    rows, width = dq.shape
    n = len(pieces)

    def kernel(at_ref, dq_ref, dk_ref, dv_ref, du_ref, *refs):
        parts, (out_ref, *w_refs, sems) = refs[:n], refs[n:]
        wait_all(start_all(weight_copies(at_ref, parts, w_refs, sems)))
        for block in blocks(rows):
            out_ref[block, :] = du_ref[block, :] + heads_inward(
                block, (dq_ref, dk_ref, dv_ref), w_refs
            )

    return call(
        kernel,
        at,
        [dq, dk, dv, upstream],
        pieces,
        shape_of((rows, width), F32),
        weight_scratch(pieces, (width,) * 3),
        7,
        16,
    )


def weight_grads(half, bundles, received):
    near, plan, outs = [], [], []
    for groups in bundles:
        total = 0
        for left, rights in groups:
            near.append(left)
            sizes = [right.shape[1] // 2 for right in rights]
            near += rights
            plan.append((len(outs), sizes, total))
            total += sum(sizes)
        outs.append(shape_of((groups[0][0].shape[1], total), LOW))
    extra = [] if received is None else list(received)

    def kernel(half_ref, *refs):
        out_refs = refs[len(near) + len(extra) :]
        at = 0
        for bundle, sizes, offset in plan:
            left = refs[at][...]
            for i, size in enumerate(sizes):
                here = slice(offset, offset + size)
                start = pl.multiple_of(half_ref[0] * size, 128)
                res = dot_tn(left, refs[at + 1 + i][:, pl.ds(start, size)])
                if extra:
                    res = res + refs[len(near) + bundle][:, here].astype(F32)
                out_refs[bundle][:, here] = res.astype(LOW)
                offset += size
            at += 1 + len(sizes)

    return call(kernel, half, near + extra, [], outs, [], 3 * len(plan), 16)


def tie(value, *others):
    others = [other for other in others if other is not None]
    return lax.optimization_barrier((value, *others))[0] if others else value


def place_of():
    f = lax.axis_index("fsdp")
    r = lax.axis_index("rep")
    return (f // 2, f % 2, r // 2, r % 2)


def z_flip(bit):
    return lambda z, y, x, c: (z ^ bit, y, x, c)


def pick(array, index, axis):
    return lax.dynamic_index_in_dim(array, index, axis, keepdims=False)


def add_low(one, two):
    return (one.astype(F32) + two.astype(F32)).astype(LOW)


def join_halves(left, right, widths):
    out, offset = [], 0
    for width in widths:
        here = slice(offset, offset + width // 2)
        out.append(jnp.concatenate([left[:, here], right[:, here]], axis=1))
        offset += width // 2
    return out


def own_piece(link, shards):
    _, _, x, c = link.place
    rows = shards[0].shape[0] // 2
    return jnp.concatenate(
        [
            lax.dynamic_slice(
                shard, (x * rows, c * (shard.shape[1] // 2)), (rows, shard.shape[1] // 2)
            )
            for shard in shards
        ],
        axis=1,
    )


class Gather:
    def __init__(self, link, shards, *after, extra=None):
        self.link = link
        grid = self.grid = link.grid
        own = own_piece(link, shards)
        rows = own.shape[0]
        if extra is not None:
            extra = jnp.pad(extra, ((0, rows - extra.shape[0]), (0, 128 - extra.shape[1])))
            own = jnp.concatenate([own, extra], axis=1)
        own = tie(own, *after)
        self.pair = jnp.stack([own, send(grid, own, z_flip(1))])
        self.base = None

    def long(self, *after):
        pair = tie(self.pair, *after)
        self.base = jnp.concatenate([self.pair, send(self.grid, pair, z_flip(2))])
        return self.base

    def near(self, *after):
        base = tie(self.base, *after)
        self.one = send(self.grid, base, first_flip)
        self.two = send(self.grid, base, second_flip)
        return self.one

    def far(self, *after):
        self.three = send(self.grid, tie(self.one, *after), second_flip)
        return self.three

    def extras(self, shape):
        rows, cols = shape
        z, y, x, c = self.link.place
        zs = self.grid.zs
        keep = [part[:, :rows, -128:][:, :, :cols] for part in (self.base, self.one, self.two, self.three)]
        near = keep[0]
        far = jnp.where(c == 0, keep[2], keep[1])
        blocks = []
        for zz in range(zs):
            k = jnp.bitwise_xor(z, zz)
            for yy in range(2):
                blocks.append(jnp.where(y == yy, pick(near, k, 0), pick(far, k, 0)))
        return jnp.concatenate(blocks, axis=1)

    def whole(self, *after):
        near = [self.base, self.one, self.two, self.three]
        return near + [send(self.grid, part, core_flip) for part in near]


class Offloaded:
    def __init__(self, link, shards):
        self.own = own_piece(link, shards)

    def whole(self, *after):
        return [lax.all_gather(tie(self.own, *after), AXES, axis=0)]


class PlainGather:
    pair = base = one = three = None

    def long(self, *after):
        return None

    def __init__(self, link, shards, *after, extra=None):
        self.shards, self.extra = shards, extra

    def extras(self, shape):
        return lax.all_gather(self.extra, "fsdp", axis=1, tiled=True)

    def near(self, *after):
        return None

    def far(self, *after):
        return None

    def whole(self, *after):
        full = [lax.all_gather(shard, "fsdp", axis=0, tiled=True) for shard in self.shards]
        halves = [
            jnp.concatenate([jnp.split(weight, 2, axis=1)[c] for weight in full], axis=1)
            for c in range(2)
        ]
        return [jnp.stack(halves)]


class Reduce:
    def __init__(self, link, half, widths):
        self.link, self.widths = link, widths
        z, y, x, c = link.place
        zs = self.link.grid.zs
        rows, cols = half.shape[0] // (4 * zs), half.shape[1]
        view = half.reshape(zs, 2, 2, rows, cols)
        self.keep = jnp.where(c == 0, pick(view, y, 1), pick(view, x, 2))
        away = jnp.where(c == 0, pick(view, 1 - y, 1), pick(view, 1 - x, 2))
        self.got = send(self.link.grid, away, second_flip)

    def one(self, *after):
        z, y, x, c = self.link.place
        part = add_low(self.keep, tie(self.got, *after))
        b = jnp.where(c == 0, x, y)
        self.keep = pick(part, b, 1)
        away = pick(part, 1 - b, 1)
        self.got = send(self.link.grid, away, first_flip)
        return away

    def two(self, *after):
        z = self.link.place[0]
        part = add_low(self.keep, tie(self.got, *after))
        self.keep = lax.dynamic_slice_in_dim(part, z // 2 * 2, 2, 0)
        away = lax.dynamic_slice_in_dim(part, (1 - z // 2) * 2, 2, 0)
        self.got = send(self.link.grid, away, z_flip(2))
        return away

    def next(self, *after):
        z = self.link.place[0]
        part = add_low(self.keep, tie(self.got, *after))
        self.keep = pick(part, z % 2, 0)
        away = pick(part, 1 - z % 2, 0)
        self.got = send(self.link.grid, away, z_flip(1))
        return away

    def three(self, *after):
        self.keep = add_low(self.keep, tie(self.got, *after))
        self.got = send(self.link.grid, self.keep, x_flip)
        return self.keep

    def four(self, *after):
        x = self.link.place[2]
        self.got = tie(self.got, *after)
        self.keep = jnp.concatenate(
            [jnp.where(x == 0, self.keep, self.got), jnp.where(x == 0, self.got, self.keep)],
            axis=0,
        )
        self.got = send(self.link.grid, self.keep, core_flip)
        return self.keep

    def out(self, *after):
        c = self.link.place[3]
        self.got = tie(self.got, *after)
        left = jnp.where(c == 0, self.keep, self.got).astype(F32)
        right = jnp.where(c == 0, self.got, self.keep).astype(F32)
        return join_halves(left, right, self.widths)


class PlainReduce:
    def __init__(self, link, half, widths):
        self.half, self.widths = half, widths

    def one(self, *after):
        return None

    two = next = three = four = one

    def out(self, *after):
        share = lax.psum_scatter(self.half, "fsdp", scatter_dimension=0, tiled=True)
        share = lax.psum(share, "rep").astype(F32)
        return join_halves(share[:, 0], share[:, 1], self.widths)


class Direct:
    gather, wide, reduce = Gather, Offloaded, Reduce

    def __init__(self, fsdp, rep):
        self.grid = Grid(fsdp, rep)
        self.place = place_of()
        self.at = jnp.stack(self.place).astype(jnp.int32)
        self.mine = self.at[3:4]
        self.other = 1 - self.mine

    def others(self, bundles, *after):
        away = weight_grads(tie(self.other, *after), bundles, None)
        return away, [send(self.grid, half, core_flip) for half in away]

    def mine_of(self, bundles, got, *after):
        return weight_grads(tie(self.mine, *after), bundles, got)

    def reduce_gains(self, value, *after):
        z, y = self.place[:2]
        flips = (core_flip, x_flip, y_flip, z_flip(1), z_flip(2))
        for flip, late in zip(flips, after):
            value = value + tie(send(self.grid, value, flip), late)
        share = value.shape[1] // (2 * self.grid.zs)
        return lax.dynamic_slice_in_dim(value, (z * 2 + y) * share, share, 1)


class Plain:
    gather, wide, reduce = PlainGather, PlainGather, PlainReduce

    def __init__(self):
        self.at = jnp.zeros((4,), jnp.int32)

    def others(self, bundles, *after):
        return [None], None

    def mine_of(self, bundles, got, *after):
        halves = [weight_grads(jnp.full((1,), c, jnp.int32), bundles, None) for c in range(2)]
        return [jnp.stack(pair, axis=1) for pair in zip(*halves)]

    def reduce_gains(self, value, *after):
        share = lax.psum_scatter(value, "fsdp", scatter_dimension=1, tiled=True)
        return lax.psum(share, "rep")


def rope_tables(positions):
    even_steps = jnp.arange(0, HEAD_DIM, 2).astype(F32)
    inverse = jnp.exp(even_steps * (-math.log(10000.0) / HEAD_DIM))
    angles = positions.astype(F32)[:, None] * inverse
    cosine, sine = jnp.cos(angles), jnp.sin(angles)
    return jnp.concatenate([cosine] * 4, axis=1), jnp.concatenate([-sine, sine] * 2, axis=1)


def body(
    fsdp,
    rep,
    tokens,
    cotangent,
    seq_lengths,
    token_positions,
    first_query,
    first_key,
    first_value,
    first_output,
    first_gate,
    first_up,
    first_down,
    first_attngain,
    first_ffngain,
    second_query,
    second_key,
    second_value,
    second_output,
    second_gate,
    second_up,
    second_down,
    second_attngain,
    second_ffngain,
):
    _, rows, width = tokens.shape
    wide = first_gate.shape[1]
    low_tokens = tokens.reshape(rows, width)
    low_cot = cotangent.reshape(rows, width)
    link = Direct(fsdp, rep) if (fsdp, rep) == (8, 4) else Plain()
    at = jnp.concatenate([link.at, seq_lengths.astype(jnp.int32)])
    cosine, sine = rope_tables(token_positions.reshape(rows))
    pairs = width // PAIR
    split = pairs // 2
    attn_widths, open_widths = (width,) * 3, (width, wide, wide)

    own_gains = jnp.stack([first_attngain, first_ffngain, second_attngain, second_ffngain])
    heads_one = link.gather(link, (first_query, first_key, first_value), extra=own_gains)
    heads_one.long()
    open_one = link.gather(link, (first_output, first_gate, first_up), heads_one.base)
    heads_one.near()
    open_one.long(heads_one.one)
    far = heads_one.far()
    heads_two = link.wide(link, (second_query, second_key, second_value)).whole(far)
    open_one.near(far)
    down_one = link.gather(link, (first_down,), heads_one.base)
    parts = heads_one.whole()
    q1, k1, v1 = project_heads(at, low_tokens, parts, cosine, sine)
    gains = heads_one.extras(own_gains.shape).astype(F32)
    heads_one = parts
    attn_one, ffn_one, attn_two, ffn_two = (gains[i : i + 1] for i in range(4))
    down_one.long(q1)
    half = attend(at, q1, k1, v1, 0, split)
    open_one.far(half[0])
    down_one.near(half[0])
    open_two = link.gather(link, (second_output, second_gate, second_up), half[0])
    o1, log1 = attend(
        at, tie(q1, open_one.one, down_one.base), k1, v1, split, pairs - split, half
    )
    open_one = open_one.whole()
    open_two.long(o1)
    r1, h1, gate1, up1, z1 = open_block(at, o1, low_tokens, attn_one, open_one, wide)
    down_one.far(r1)
    open_two.near(r1)
    down_two = link.gather(link, (second_down,), r1)
    down_one = down_one.whole()
    r2, first_out, n1 = close_first(at, z1, r1, gains, down_one)
    down_two.long(first_out)
    q2, k2, v2 = project_heads(at, n1, heads_two, cosine, sine)
    open_two.far(q2)
    down_two.near(q2)
    half = attend(at, q2, k2, v2, 0, split)
    down_two.far(half[0])
    o2, log2 = attend(at, tie(q2, open_two.three, down_two.one), k2, v2, split, pairs - split, half)
    open_two = open_two.whole()
    r3, h2, gate2, up2, z2 = open_block(at, o2, first_out, ffn_two, open_two, wide)
    down_two = down_two.whole()

    dgate2, dup2, dr3, dr3_low, do2, gain_d = feed_back(
        at, low_cot, low_cot, gate2, up2, r3, ffn_two, open_two, down_two, False
    )
    bundles = [[(o2, [dr3_low]), (h2, [dgate2, dup2])], [(z2, [low_cot])]]
    away, got = link.others(bundles, dr3)
    half = attend_back(at, tie(q2, away[0]), k2, v2, o2, log2, do2, cosine, sine, 0, split)
    sent = link.mine_of(bundles, got, half[0])
    open_g2, down_g2 = (
        link.reduce(link, grad, widths) for grad, widths in zip(sent, (open_widths, (width,)))
    )
    dq2, dk2, dv2 = attend_back(
        at, tie(q2, sent[0]), k2, v2, o2, log2, do2, cosine, sine, split, pairs - split, half
    )
    bundles = [[(n1, [dq2, dk2, dv2])]]
    part = down_g2.one(dq2)
    away, got = link.others(bundles, part)
    dr2, dr2_low, gain_c, gain_b = heads_back_second(
        tie(at, away[0]),
        dq2,
        dk2,
        dv2,
        dr3,
        first_out,
        r2,
        jnp.concatenate([attn_two, ffn_one]),
        heads_two,
    )
    part = (open_g2.one(dr2), down_g2.two(dr2))
    sent = link.mine_of(bundles, got, dr2, *part)
    heads_g2 = link.reduce(link, sent[0], attn_widths)

    dgate1, dup1, dr1, dr1_low, do1, gain_a = feed_back(
        tie(at, sent[0]), dr2, dr2_low, gate1, up1, r1, attn_one, open_one, down_one, True
    )
    part = (open_g2.two(dr1), heads_g2.one(dr1), down_g2.next(dr1))
    bundles = [[(o1, [dr1_low]), (h1, [dgate1, dup1])], [(z1, [dr2_low])]]
    away, got = link.others(bundles, dr1, *part)
    second_out = close_second(tie(at, away[0]), z2, r3, down_two)
    part = (heads_g2.two(second_out), open_g2.next(second_out), down_g2.three(second_out))
    sent = link.mine_of(bundles, got, second_out, *part)
    open_g1, down_g1 = (
        link.reduce(link, grad, widths) for grad, widths in zip(sent, (open_widths, (width,)))
    )
    gain_grads = jnp.stack([jnp.sum(share, axis=0) for share in (gain_a, gain_b, gain_c, gain_d)])
    half = attend_back(at, tie(q1, sent[0]), k1, v1, o1, log1, do1, cosine, sine, 0, split)
    part = (down_g1.one(half[0]), heads_g2.next(half[0]), open_g2.three(half[0]), down_g2.four(half[0]))
    dq1, dk1, dv1 = attend_back(
        at, tie(q1, *part), k1, v1, o1, log1, do1, cosine, sine, split, pairs - split, half
    )
    part = (open_g1.one(dq1), down_g1.two(dq1), heads_g2.three(dq1), open_g2.four(dq1))
    bundles = [[(low_tokens, [dq1, dk1, dv1])]]
    away, got = link.others(bundles, *part)
    heads_g2.four(away[0])
    part = (down_g1.next(away[0]), open_g1.two(away[0]))
    (down_g2,) = down_g2.out(away[0])
    output_g2, gate_g2, up_g2 = open_g2.out(away[0])
    sent = link.mine_of(bundles, got, *part, down_g2, output_g2, gate_g2, up_g2)
    heads_g1 = link.reduce(link, sent[0], attn_widths)
    input_grad = heads_back_first(tie(at, sent[0]), dq1, dk1, dv1, dr1, heads_one)
    part = (heads_g1.one(input_grad), open_g1.next(input_grad), down_g1.three(input_grad))
    query_g2, key_g2, value_g2 = heads_g2.out(*part)
    part = (heads_g1.two(query_g2), open_g1.three(query_g2), down_g1.four(query_g2))
    heads_g1.next(part[0])
    open_g1.four(part[0])
    (down_g1,) = down_g1.out(part[0])
    part = heads_g1.three()
    output_g1, gate_g1, up_g1 = open_g1.out(part)
    gain_grads = link.reduce_gains(gain_grads, second_out, half[0], dq1, sent[0], input_grad)
    heads_g1.four()
    query_g1, key_g1, value_g1 = heads_g1.out()
    return (
        first_out.reshape(tokens.shape),
        second_out.reshape(tokens.shape),
        input_grad.reshape(tokens.shape),
        query_g1,
        key_g1,
        value_g1,
        output_g1,
        gate_g1,
        up_g1,
        down_g1,
        gain_grads[0],
        gain_grads[1],
        query_g2,
        key_g2,
        value_g2,
        output_g2,
        gate_g2,
        up_g2,
        down_g2,
        gain_grads[2],
        gain_grads[3],
    )


def solution(mesh):
    per_seq = P(("fsdp", "rep"))
    shard = P("fsdp")
    return jax.shard_map(
        functools.partial(body, mesh.shape["fsdp"], mesh.shape["rep"]),
        mesh=mesh,
        in_specs=(per_seq,) * 4 + (shard,) * 18,
        out_specs=(per_seq,) * 3 + (shard,) * 18,
        check_vma=False,
    )
```

time: 707 us -> 614 us (0.87)
  Pallas kernels: 362 us -> 284 us
  starting transfers between devices: 126 us -> 76.2 us
  local copies, waits for them, and re-layouts: 28.1 us -> 65.9 us
  other arithmetic: 54.5 us -> 29.5 us
  between operations: 3.1 us -> 17.6 us
  waiting for transfers between devices: 120 us -> 132 us
    pallas_call x30 -> x26, Pallas kernels: 362 us -> 284 us  [the longest x18 169 us: call(): pl.pallas_call(kernel, out_shape=outs, in_specs=[SCALARS] + [NEAR] * len(...]
    ppermute x118 -> x92, starting transfers between devices: 126 us -> 76.2 us  [send(): return lax.ppermute(value, AXES, grid.pairs(move))]
    unnamed x112 -> x212, local copies, waits for them, and re-layouts: 11.5 us -> 53.1 us
    ppermute x118 -> x92, waiting for transfers between devices: 120 us -> 132 us  [send(): return lax.ppermute(value, AXES, grid.pairs(move))]
    convert_element_type x12 -> x24, other arithmetic: 14.1 us -> 5.44 us  [add_low(): return (one.astype(F32) + two.astype(F32)).astype(LOW)]
  transfers between devices with their start and end apart: 118 -> 93, of which waited for: 33 -> 25; matrix products, arithmetic and copies ran while one was open for 9% -> 6% of each run, Pallas kernels for 44% -> 39%
where the time goes in v2:
time: 614 us; the launch traced here: 605 us
  Pallas kernels  284 us (46%)
  waiting for transfers between devices  132 us (21%)
  starting transfers between devices  76.2 us (12%)
  local copies, waits for them, and re-layouts  65.9 us (11%)
  other arithmetic  29.5 us (5%)
  between operations  17.6 us (3%)
    pallas_call x18, Pallas kernels, call(): pl.pallas_call(kernel, out_shape=outs, in_specs=[SCALARS] + [NEAR] * len(...  169 us
    ppermute x92, waiting for transfers between devices, send(): return lax.ppermute(value, AXES, grid.pairs(move))  132 us
    pallas_call x8, Pallas kernels, call_pairs(): pl.pallas_call(kernel, out_shape=outs, grid_spec=pltpu.PrefetchScalarGrid...  115 us
    ppermute x92, starting transfers between devices, send(): return lax.ppermute(value, AXES, grid.pairs(move))  76.2 us
    unnamed x212, local copies, waits for them, and re-layouts  53.1 us
  transfers between devices with their start and end apart: 93, of which 25 were waited for; matrix products, arithmetic and copies ran while one was open for 6% of the time, Pallas kernels for 39%

profile of v2, /device:TPU:0, one launch (start us, length us, event | category | flops | bytes accessed | tf_op | source)
XLA Modules:
  0.0 605.4 jit_solution(14923111023396137535)
XLA Ops:
  19.7 10.5 %collective-permute-done.1 = bf16[2,48,1280]{2,1,0:T(8,128)(2,1)S(1)} collective-permute-done((bf16[2,48,1280]{2,1,0:T(8,128)(2,1)S(1)}, bf16[2,48,1280]{2,1,0:T(8,128)(2,1)S(1)}, u32[]{:S(2)}, u32[]{:S(2)}) %collective-permute-start.1) | collective-permute-done | bytes 245792 | tf_op jit(solution)/shard_map/ppermute | solution.py:39
  54.6 9.8 %collective-permute-done.10 = bf16[2,48,2432]{2,1,0:T(8,128)(2,1)} collective-permute-done((bf16[2,48,2432]{2,1,0:T(8,128)(2,1)}, bf16[2,48,2432]{2,1,0:T(8,128)(2,1)}, u32[]{:S(2)}, u32[]{:S(2)}) %collective-permute-start.10) | collective-permute-done | bytes 466976 | tf_op jit(solution)/shard_map/ppermute | solution.py:39
  69.0 7.6 %shard_map.373 = (bf16[1024,768]{1,0:T(8,128)(2,1)S(1)}, bf16[1024,768]{1,0:T(8,128)(2,1)S(1)}, bf16[1024,768]{1,0:T(8,128)(2,1)S(1)}) custom-call(s32[5]{0:T(128)S(1)} %concatenate.113.at_ref, bf16[1024,768]{1,0:T(8,128)(2,1)S(1)} %bitcast.192, f32[1024,128]{1,0:T(8,128)S(1)} %get-tuple-element.382.cos_ref, f32[1024,128]{1,0:T(8,128)S(1)} %get-tuple-element.383.sin_ref, ...), custom_call_target="tpu_custom_call" | custom-call | flops 8800000000 | bytes 800000 | tf_op jit(solution)/shard_map/pallas_call | solution.py:176
  80.1 12.8 %shard_map.374 = (bf16[1024,768]{1,0:T(8,128)(2,1)}, f32[6,16,1024]{2,1,0:T(8,128)}) custom-call(s32[5]{0:T(128)S(1)} %concatenate.113.at_ref, bf16[1024,768]{1,0:T(8,128)(2,1)} %copy-done.68, bf16[1024,768]{1,0:T(8,128)(2,1)} %copy-done.69, bf16[1024,768]{1,0:T(8,128)(2,1)} %copy-done.70), custom_call_target="tpu_custom_call" | custom-call | flops 13200000000 | bytes 1200000 | tf_op jit(solution)/shard_map/pallas_call | solution.py:210
  100.0 7.6 %collective-permute-done.13 = bf16[2,128,384]{2,1,0:T(8,128)(2,1)S(1)} collective-permute-done((bf16[2,128,384]{2,1,0:T(8,128)(2,1)S(1)}, bf16[2,128,384]{2,1,0:T(8,128)(2,1)S(1)}, u32[]{:S(2)}, u32[]{:S(2)}) %collective-permute-start.13) | collective-permute-done | bytes 196640 | tf_op jit(solution)/shard_map/ppermute | solution.py:39
  110.1 13.0 %shard_map.375 = (bf16[1024,768]{1,0:T(8,128)(2,1)}, f32[6,16,1024]{2,1,0:T(8,128)}) custom-call(s32[5]{0:T(128)S(1)} %concatenate.113.at_ref, bf16[1024,768]{1,0:T(8,128)(2,1)} %copy-done.68, bf16[1024,768]{1,0:T(8,128)(2,1)} %copy-done.69, bf16[1024,768]{1,0:T(8,128)(2,1)} %copy-done.70, ...), custom_call_target="tpu_custom_call", output_to_operand_aliasing={{0}: (4, {}), {1}: (5, {})} | custom-call | flops 13200000000 | bytes 1200000 | tf_op jit(solution)/shard_map/pallas_call | solution.py:210
  130.4 14.2 %shard_map.376 = (f32[1024,768]{1,0:T(8,128)S(1)}, bf16[1024,768]{1,0:T(8,128)(2,1)S(1)}, bf16[1024,2048]{1,0:T(8,128)(2,1)S(1)}, bf16[1024,2048]{1,0:T(8,128)(2,1)S(1)}, bf16[1024,2048]{1,0:T(8,128)(2,1)S(1)}) custom-call(s32[5]{0:T(128)S(1)} %concatenate.113.at_ref, bf16[1024,768]{1,0:T(8,128)(2,1)S(1)} %copy-done.52, bf16[1024,768]{1,0:T(8,128)(2,1)S(1)} %bitcast.193, ...), custom_call_target="tpu_custom_call" | custom-call | flops 13200000000 | bytes 1200000 | tf_op jit(solution)/shard_map/pallas_call | solution.py:176
  160.4 8.8 %shard_map.377 = (f32[1024,768]{1,0:T(8,128)S(1)}, f32[1024,768]{1,0:T(8,128)}, bf16[1024,768]{1,0:T(8,128)(2,1)S(1)}) custom-call(s32[5]{0:T(128)S(1)} %concatenate.113.at_ref, bf16[1024,2048]{1,0:T(8,128)(2,1)S(1)} %get-tuple-element.170.z_ref.refs_5_, f32[1024,768]{1,0:T(8,128)S(1)} %get-tuple-element.171.r_ref, ...), custom_call_target="tpu_custom_call" | custom-call | flops 8800000000 | bytes 800000 | tf_op jit(solution)/shard_map/pallas_call | solution.py:176
  173.3 7.7 %collective-permute-done.29.refs_1_ = bf16[4,48,2432]{2,1,0:T(8,128)(2,1)} collective-permute-done((bf16[4,48,2432]{2,1,0:T(8,128)(2,1)}, bf16[4,48,2432]{2,1,0:T(8,128)(2,1)}, u32[]{:S(2)}, u32[]{:S(2)}) %collective-permute-start.29) | collective-permute-done | bytes 933920 | tf_op jit(solution)/shard_map/ppermute | solution.py:39
  185.5 7.6 %shard_map.378 = (bf16[1024,768]{1,0:T(8,128)(2,1)S(1)}, bf16[1024,768]{1,0:T(8,128)(2,1)S(1)}, bf16[1024,768]{1,0:T(8,128)(2,1)S(1)}) custom-call(s32[5]{0:T(128)S(1)} %concatenate.113.at_ref, bf16[1024,768]{1,0:T(8,128)(2,1)S(1)} %copy-done.10, f32[1024,128]{1,0:T(8,128)S(1)} %get-tuple-element.382.cos_ref, f32[1024,128]{1,0:T(8,128)S(1)} %get-tuple-element.383.sin_ref, ...), custom_call_target="tpu_custom_call" | custom-call | flops 8800000000 | bytes 800000 | tf_op jit(solution)/shard_map/pallas_call | solution.py:176
  198.8 12.6 %shard_map.379 = (bf16[1024,768]{1,0:T(8,128)(2,1)}, f32[6,16,1024]{2,1,0:T(8,128)}) custom-call(s32[5]{0:T(128)S(1)} %concatenate.113.at_ref, bf16[1024,768]{1,0:T(8,128)(2,1)} %copy-done.71, bf16[1024,768]{1,0:T(8,128)(2,1)} %copy-done.72, bf16[1024,768]{1,0:T(8,128)(2,1)} %copy-done.73), custom_call_target="tpu_custom_call" | custom-call | flops 13200000000 | bytes 1200000 | tf_op jit(solution)/shard_map/pallas_call | solution.py:210
  214.4 13.3 %shard_map.380 = (bf16[1024,768]{1,0:T(8,128)(2,1)}, f32[6,16,1024]{2,1,0:T(8,128)}) custom-call(s32[5]{0:T(128)S(1)} %concatenate.113.at_ref, bf16[1024,768]{1,0:T(8,128)(2,1)} %copy-done.71, bf16[1024,768]{1,0:T(8,128)(2,1)} %copy-done.72, bf16[1024,768]{1,0:T(8,128)(2,1)} %copy-done.73, ...), custom_call_target="tpu_custom_call", output_to_operand_aliasing={{0}: (4, {}), {1}: (5, {})} | custom-call | flops 13200000000 | bytes 1200000 | tf_op jit(solution)/shard_map/pallas_call | solution.py:210
  231.3 14.1 %shard_map.381 = (f32[1024,768]{1,0:T(8,128)S(1)}, bf16[1024,768]{1,0:T(8,128)(2,1)S(1)}, bf16[1024,2048]{1,0:T(8,128)(2,1)S(1)}, bf16[1024,2048]{1,0:T(8,128)(2,1)S(1)}, bf16[1024,2048]{1,0:T(8,128)(2,1)S(1)}) custom-call(s32[5]{0:T(128)S(1)} %concatenate.113.at_ref, bf16[1024,768]{1,0:T(8,128)(2,1)S(1)} %copy-done.55, f32[1024,768]{1,0:T(8,128)S(1)} %copy-done.7, ...), custom_call_target="tpu_custom_call" | custom-call | flops 13200000000 | bytes 1200000 | tf_op jit(solution)/shard_map/pallas_call | solution.py:176
  257.4 24.1 %shard_map.382 = (bf16[1024,2048]{1,0:T(8,128)(2,1)S(1)}, bf16[1024,2048]{1,0:T(8,128)(2,1)S(1)}, f32[1024,768]{1,0:T(8,128)S(1)}, bf16[1024,768]{1,0:T(8,128)(2...) custom-call(s32[5]{0:T(128)S(1)} %concatenate.113.at_ref, bf16[1024,768]{1,0:T(8,128)(2,1)S(1)} %bitcast.188, ...), custom_call_target="tpu_custom_call" | custom-call | flops 26400000000 | bytes 2400000 | tf_op jit(solution)/shard_map/pallas_call | solution.py:176
  282.6 6.7 %shard_map.383 = (bf16[768,2432]{1,0:T(8,128)(2,1)}, bf16[2048,384]{1,0:T(8,128)(2,1)S(1)}) custom-call(s32[1]{0:T(128)S(6)} %sub.66.half_ref, bf16[1024,768]{1,0:T(8,128)(2,1)S(1)} %copy-done.56, bf16[1024,768]{1,0:T(8,128)(2,1)S(1)} %get-tuple-element.197.refs_1_, bf16[1024,768]{1,0:T(8,128)(2,1)S(1)} %get-tuple-element.198.refs_2_, ...), custom_call_target="tpu_custom_call" | custom-call | flops 9900000256 | bytes 900000 | tf_op jit(solution)/shard_map/pallas_call | solution.py:176
  290.1 16.3 %shard_map.384 = (bf16[1024,768]{1,0:T(8,128)(2,1)}, bf16[1024,768]{1,0:T(8,128)(2,1)}, bf16[1024,768]{1,0:T(8,128)(2,1)}) custom-call(s32[5]{0:T(128)S(1)} %concatenate.113.at_ref, bf16[1024,768]{1,0:T(8,128)(2,1)} %copy-done.71, bf16[1024,768]{1,0:T(8,128)(2,1)} %copy-done.72, bf16[1024,768]{1,0:T(8,128)(2,1)} %copy-done.73, ...), custom_call_target="tpu_custom_call" | custom-call | flops 16499999744 | bytes 1500000 | tf_op jit(solution)/shard_map/pallas_call | solution.py:210
  306.5 8.6 %shard_map.385 = (bf16[768,2432]{1,0:T(8,128)(2,1)S(1)}, bf16[2048,384]{1,0:T(8,128)(2,1)S(1)}) custom-call(s32[1]{0:T(128)} %bitcast.3.half_ref, bf16[1024,768]{1,0:T(8,128)(2,1)S(1)} %copy-done.57, bf16[1024,768]{1,0:T(8,128)(2,1)S(1)} %copy-done.51, bf16[1024,768]{1,0:T(8,128)(2,1)S(1)} %copy-done.49, bf16[1024,2048]{1,0:T(8,128)(2,1)S(1)} %copy-done.31, ...), custom_call_target="tpu_custom_call" | custom-call | flops 9900000256 | bytes 900000 | tf_op jit(solution)/shard_map/pallas_call | solution.py:176
  318.6 16.1 %shard_map.386 = (bf16[1024,768]{1,0:T(8,128)(2,1)}, bf16[1024,768]{1,0:T(8,128)(2,1)}, bf16[1024,768]{1,0:T(8,128)(2,1)}) custom-call(s32[5]{0:T(128)S(1)} %concatenate.113.at_ref, bf16[1024,768]{1,0:T(8,128)(2,1)} %copy-done.71, bf16[1024,768]{1,0:T(8,128)(2,1)} %copy-done.72, ...), custom_call_target="tpu_custom_call", output_to_operand_aliasing={{0}: (9, {}), {1}: (10, {}), {2}: (11, {})} | custom-call | flops 16499999744 | bytes 1500000 | tf_op jit(solution)/shard_map/pallas_call | solution.py:210
  343.1 9.6 %shard_map.388 = (f32[1024,768]{1,0:T(8,128)S(1)}, bf16[1024,768]{1,0:T(8,128)(2,1)S(1)}, f32[8,768]{1,0:T(8,128)S(1)}, f32[8,768]{1,0:T(8,128)S(1)}) custom-call(s32[5]{0:T(128)S(1)} %concatenate.113.at_ref, bf16[1024,768]{1,0:T(8,128)(2,1)S(1)} %copy-done.15, bf16[1024,768]{1,0:T(8,128)(2,1)S(1)} %copy-done.17, bf16[1024,768]{1,0:T(8,128)(2,1)S(1)} %copy-done.19, ...), custom_call_target="tpu_custom_call" | custom-call | flops 8800000000 | bytes 800000 | tf_op jit(solution)/shard_map/pallas_call | solution.py:176
  359.7 24.6 %shard_map.390 = (bf16[1024,2048]{1,0:T(8,128)(2,1)S(1)}, bf16[1024,2048]{1,0:T(8,128)(2,1)S(1)}, f32[1024,768]{1,0:T(8,128)S(1)}, bf16[1024,768]{1,0:T(8,128)(2...) custom-call(s32[5]{0:T(128)S(1)} %concatenate.113.at_ref, f32[1024,768]{1,0:T(8,128)S(1)} %get-tuple-element.221.du_ref, ...), custom_call_target="tpu_custom_call" | custom-call | flops 26400000000 | bytes 2400000 | tf_op jit(solution)/shard_map/pallas_call | solution.py:176
  391.4 9.2 %collective-permute-done.52 = bf16[4,2,48,1152]{3,2,0,1:T(8,128)(2,1)S(1)} collective-permute-done((bf16[4,2,48,1152]{3,2,0,1:T(8,128)(2,1)S(1)}, bf16[4,2,48,1152]{3,2,0,1:T(8,128)(2,1)S(1)}, u32[]{:S(2)}, u32[]{:S(2)}) %collective-permute-start.52) | collective-permute-done | bytes 884768 | tf_op jit(solution)/shard_map/ppermute | solution.py:39
  403.3 6.5 %shard_map.391 = (bf16[768,2432]{1,0:T(8,128)(2,1)}, bf16[2048,384]{1,0:T(8,128)(2,1)S(1)}) custom-call(s32[1]{0:T(128)S(6)} %sub.66.half_ref, bf16[1024,768]{1,0:T(8,128)(2,1)S(1)} %copy-done.53, bf16[1024,768]{1,0:T(8,128)(2,1)S(1)} %get-tuple-element.234.refs_1_, bf16[1024,768]{1,0:T(8,128)(2,1)S(1)} %copy-done.43, ...), custom_call_target="tpu_custom_call" | custom-call | flops 9900000256 | bytes 900000 | tf_op jit(solution)/shard_map/pallas_call | solution.py:176
  418.8 8.2 %shard_map.392 = f32[1024,768]{1,0:T(8,128)} custom-call(s32[5]{0:T(128)S(1)} %concatenate.113.at_ref, bf16[1024,2048]{1,0:T(8,128)(2,1)S(1)} %copy-done.25, f32[1024,768]{1,0:T(8,128)S(1)} %copy-done.37, bf16[4,128,384]{2,1,0:T(8,128)(2,1)} %copy-done.83, bf16[4,128,384]{2,1,0:T(8,128)(2,1)} %copy-done.95, bf16[4,128,384]{2,1,0:T(8,128)(2,1)} %copy-done.98, ...), custom_call_target="tpu_custom_call" | custom-call | flops 7699999744 | bytes 700000 | tf_op jit(solution)/shard_map/pallas_call | solution.py:176
  427.0 10.3 %collective-permute-done.55 = bf16[2,48,2432]{2,1,0:T(8,128)(2,1)S(1)} collective-permute-done((bf16[2,48,2432]{2,1,0:T(8,128)(2,1)}, bf16[2,48,2432]{2,1,0:T(8,128)(2,1)S(1)}, u32[]{:S(2)}, u32[]{:S(2)}) %collective-permute-start.55) | collective-permute-done | bytes 466976 | tf_op jit(solution)/shard_map/ppermute | solution.py:39
  443.1 8.8 %shard_map.393 = (bf16[768,2432]{1,0:T(8,128)(2,1)S(1)}, bf16[2048,384]{1,0:T(8,128)(2,1)S(1)}) custom-call(s32[1]{0:T(128)} %bitcast.3.half_ref, bf16[1024,768]{1,0:T(8,128)(2,1)S(1)} %copy-done.54, bf16[1024,768]{1,0:T(8,128)(2,1)S(1)} %copy-done.47, bf16[1024,768]{1,0:T(8,128)(2,1)S(1)} %copy-done.43, bf16[1024,2048]{1,0:T(8,128)(2,1)S(1)} %copy-done.27, ...), custom_call_target="tpu_custom_call" | custom-call | flops 9900000256 | bytes 900000 | tf_op jit(solution)/shard_map/pallas_call | solution.py:176
  452.2 15.5 %shard_map.394 = (bf16[1024,768]{1,0:T(8,128)(2,1)}, bf16[1024,768]{1,0:T(8,128)(2,1)}, bf16[1024,768]{1,0:T(8,128)(2,1)}) custom-call(s32[5]{0:T(128)S(1)} %concatenate.113.at_ref, bf16[1024,768]{1,0:T(8,128)(2,1)} %copy-done.68, bf16[1024,768]{1,0:T(8,128)(2,1)} %copy-done.69, bf16[1024,768]{1,0:T(8,128)(2,1)} %copy-done.70, ...), custom_call_target="tpu_custom_call" | custom-call | flops 16499999744 | bytes 1500000 | tf_op jit(solution)/shard_map/pallas_call | solution.py:210
  472.2 8.5 %collective-permute-done.59 = bf16[4,2,128,384]{3,2,0,1:T(8,128)(2,1)S(1)} collective-permute-done((bf16[4,2,128,384]{3,2,0,1:T(8,128)(2,1)S(1)}, bf16[4,2,128,384]{3,2,0,1:T(8,128)(2,1)S(1)}, u32[]{:S(2)}, u32[]{:S(2)}) %collective-permute-start.59) | collective-permute-done | bytes 786464 | tf_op jit(solution)/shard_map/ppermute | solution.py:39
  482.0 15.7 %shard_map.395 = (bf16[1024,768]{1,0:T(8,128)(2,1)}, bf16[1024,768]{1,0:T(8,128)(2,1)}, bf16[1024,768]{1,0:T(8,128)(2,1)}) custom-call(s32[5]{0:T(128)S(1)} %concatenate.113.at_ref, bf16[1024,768]{1,0:T(8,128)(2,1)} %copy-done.68, bf16[1024,768]{1,0:T(8,128)(2,1)} %copy-done.69, ...), custom_call_target="tpu_custom_call", output_to_operand_aliasing={{0}: (9, {}), {1}: (10, {}), {2}: (11, {})} | custom-call | flops 16499999744 | bytes 1500000 | tf_op jit(solution)/shard_map/pallas_call | solution.py:210
  501.9 7.5 %collective-permute-done.60 = bf16[4,128,384]{2,1,0:T(8,128)(2,1)S(1)} collective-permute-done((bf16[4,128,384]{2,1,0:T(8,128)(2,1)S(1)}, bf16[4,128,384]{2,1,0:T(8,128)(2,1)S(1)}, u32[]{:S(2)}, u32[]{:S(2)}) %collective-permute-start.60) | collective-permute-done | bytes 393248 | tf_op jit(solution)/shard_map/ppermute | solution.py:39
  524.2 7.7 %collective-permute-done.68 = bf16[4,48,2432]{2,1,0:T(8,128)(2,1)S(1)} collective-permute-done((bf16[4,48,2432]{2,1,0:T(8,128)(2,1)S(1)}, bf16[4,48,2432]{2,1,0:T(8,128)(2,1)S(1)}, u32[]{:S(2)}, u32[]{:S(2)}) %collective-permute-start.68) | collective-permute-done | bytes 933920 | tf_op jit(solution)/shard_map/ppermute | solution.py:39
  535.3 9.0 %shard_map.398 = f32[1024,768]{1,0:T(8,128)} custom-call(s32[5]{0:T(128)S(1)} %concatenate.113.at_ref, bf16[1024,768]{1,0:T(8,128)(2,1)S(1)} %copy-done.12, bf16[1024,768]{1,0:T(8,128)(2,1)S(1)} %copy-done.13, bf16[1024,768]{1,0:T(8,128)(2,1)S(1)} %copy-done.14, f32[1024,768]{1,0:T(8,128)S(1)} %copy-done.35, bf16[4,48,1280]{2,1,0:T(8,128)(2,1)} %pad_maximum_fusion.8.refs_0_, ...), custom_call_target="tpu_custom_call" | custom-call | flops 7699999744 | bytes 700000 | tf_op jit(solution)/shard_map/pallas_call | solution.py:176
  557.5 6.6 %collective-permute-done.72 = bf16[4,2,48,1152]{3,2,0,1:T(8,128)(2,1)S(1)} collective-permute-done((bf16[4,2,48,1152]{3,2,0,1:T(8,128)(2,1)S(1)}, bf16[4,2,48,1152]{3,2,0,1:T(8,128)(2,1)S(1)}, u32[]{:S(2)}, u32[]{:S(2)}) %collective-permute-start.72) | collective-permute-done | bytes 884768 | tf_op jit(solution)/shard_map/ppermute | solution.py:39
  (560 shorter events, 228.8 us)
Async XLA Ops:
  7.2 176.8 %all-gather.3.cloned.1.call-start = ((), (), s32[]{:S(2)}) async-start(), calls=%async_computation | async-start | bytes 3649536 | tf_op jit(solution)/shard_map/all_gather | solution.py:745
  45.6 23.3 %collective-permute-start.5 = (bf16[4,48,1280]{2,1,0:T(8,128)(2,1)}, bf16[4,48,1280]{2,1,0:T(8,128)(2,1)}, u32[]{:S(2)}, u32[]{:S(2)}) collective-permute-start(bf16[4,48,1280]{2,1,0:T(8,128)(2,1)} %pad_maximum_fusion.8.refs_0_), channel_id=1, source_target_pairs={{0,1},{1,0},{2,3},{3,2},{4,5},{5,4},{6,7},{7,6},{8,9},{9,8},{10,11... | collective-permute-start | bytes 1474568 | tf_op jit(solution)/shard_map/ppermute | solution.py:39
  45.6 23.4 %collective-permute-start.6 = (bf16[4,48,1280]{2,1,0:T(8,128)(2,1)}, bf16[4,48,1280]{2,1,0:T(8,128)(2,1)}, u32[]{:S(2)}, u32[]{:S(2)}) collective-permute-start(bf16[4,48,1280]{2,1,0:T(8,128)(2,1)} %collective-permute-done.2.refs_1_), channel_id=1, source_target_pairs={{0,1},{1,0},{2,3},{3,2},{4,5},{5,4},{6,7},{7,6},{8,9},{9,8},{10,11... | collective-permute-start | bytes 1474568 | tf_op jit(solution)/shard_map/ppermute | solution.py:39
  66.4 26.5 %collective-permute-start.11 = (bf16[4,48,2432]{2,1,0:T(8,128)(2,1)}, bf16[4,48,2432]{2,1,0:T(8,128)(2,1)}, u32[]{:S(2)}, u32[]{:S(2)}) collective-permute-start(bf16[4,48,2432]{2,1,0:T(8,128)(2,1)} %pad_maximum_fusion.refs_0_), channel_id=1, source_target_pairs={{0,2},{1,5},{2,0},{3,7},{4,6},{5,1},{6,4},{7,3},{8,10},{9,13},{10,... | collective-permute-start | bytes 2801672 | tf_op jit(solution)/shard_map/ppermute | solution.py:39
  68.9 40.7 %collective-permute-start.14 = (bf16[4,48,2432]{2,1,0:T(8,128)(2,1)}, bf16[4,48,2432]{2,1,0:T(8,128)(2,1)}, u32[]{:S(2)}, u32[]{:S(2)}) collective-permute-start(bf16[4,48,2432]{2,1,0:T(8,128)(2,1)} %pad_maximum_fusion.refs_0_), channel_id=1, source_target_pairs={{0,4},{1,3},{2,6},{3,1},{4,0},{5,7},{6,2},{7,5},{8,12},{9,11},{10,... | collective-permute-start | bytes 2801672 | tf_op jit(solution)/shard_map/ppermute | solution.py:39
  100.0 23.2 %collective-permute-start.16 = (bf16[4,48,2432]{2,1,0:T(8,128)(2,1)}, bf16[4,48,2432]{2,1,0:T(8,128)(2,1)S(1)}, u32[]{:S(2)}, u32[]{:S(2)}) collective-permute-start(bf16[4,48,2432]{2,1,0:T(8,128)(2,1)} %pad_maximum_fusion.refs_0_), channel_id=1, source_target_pairs={{0,1},{1,0},{2,3},{3,2},{4,5},{5,4},{6,7},{7,6},{8,9},{9,8},{10,11... | collective-permute-start | bytes 2801672 | tf_op jit(solution)/shard_map/ppermute | solution.py:39
  107.7 40.8 %collective-permute-start.20 = (bf16[4,128,384]{2,1,0:T(8,128)(2,1)S(1)}, bf16[4,128,384]{2,1,0:T(8,128)(2,1)S(1)}, u32[]{:S(2)}, u32[]{:S(2)}) collective-permute-start(bf16[4,128,384]{2,1,0:T(8,128)(2,1)S(1)} %pad_maximum_fusion.13.refs_0_.refs_8_), channel_id=1, source_target_pairs={{0,2},{1,5},{2,0},{3,7},{4,6},{5,1},{6,4},{7,3},{8,10},{9,13},{10,... | collective-permute-start | bytes 1179656 | tf_op jit(solution)/shard_map/ppermute | solution.py:39
  123.1 28.0 %collective-permute-start.21 = (bf16[4,128,384]{2,1,0:T(8,128)(2,1)S(1)}, bf16[4,128,384]{2,1,0:T(8,128)(2,1)S(1)}, u32[]{:S(2)}, u32[]{:S(2)}) collective-permute-start(bf16[4,128,384]{2,1,0:T(8,128)(2,1)S(1)} %pad_maximum_fusion.13.refs_0_.refs_8_), channel_id=1, source_target_pairs={{0,4},{1,3},{2,6},{3,1},{4,0},{5,7},{6,2},{7,5},{8,12},{9,11},{10,... | collective-permute-start | bytes 1179656 | tf_op jit(solution)/shard_map/ppermute | solution.py:39
  124.7 26.9 %collective-permute-start.28 = (bf16[2,48,2432]{2,1,0:T(8,128)(2,1)S(1)}, bf16[2,48,2432]{2,1,0:T(8,128)(2,1)S(1)}, u32[]{:S(2)}, u32[]{:S(2)}) collective-permute-start(bf16[2,48,2432]{2,1,0:T(8,128)(2,1)S(1)} %pad_maximum_fusion.10), channel_id=1, source_target_pairs={{0,16},{1,17},{2,18},{3,19},{4,20},{5,21},{6,22},{7,23},{8,24},{9,... | collective-permute-start | bytes 1400840 | tf_op jit(solution)/shard_map/ppermute | solution.py:39
  157.4 23.6 %collective-permute-start.29 = (bf16[4,48,2432]{2,1,0:T(8,128)(2,1)}, bf16[4,48,2432]{2,1,0:T(8,128)(2,1)}, u32[]{:S(2)}, u32[]{:S(2)}) collective-permute-start(bf16[4,48,2432]{2,1,0:T(8,128)(2,1)} %pad_maximum_fusion.1.refs_0_), channel_id=1, source_target_pairs={{0,2},{1,5},{2,0},{3,7},{4,6},{5,1},{6,4},{7,3},{8,10},{9,13},{10,... | collective-permute-start | bytes 2801672 | tf_op jit(solution)/shard_map/ppermute | solution.py:39
  173.3 41.1 %collective-permute-start.35 = (bf16[4,48,2432]{2,1,0:T(8,128)(2,1)}, bf16[4,48,2432]{2,1,0:T(8,128)(2,1)}, u32[]{:S(2)}, u32[]{:S(2)}) collective-permute-start(bf16[4,48,2432]{2,1,0:T(8,128)(2,1)} %pad_maximum_fusion.1.refs_0_), channel_id=1, source_target_pairs={{0,1},{1,0},{2,3},{3,2},{4,5},{5,4},{6,7},{7,6},{8,9},{9,8},{10,11... | collective-permute-start | bytes 2801672 | tf_op jit(solution)/shard_map/ppermute | solution.py:39
  181.1 46.7 %collective-permute-start.36 = (bf16[4,48,2432]{2,1,0:T(8,128)(2,1)}, bf16[4,48,2432]{2,1,0:T(8,128)(2,1)}, u32[]{:S(2)}, u32[]{:S(2)}) collective-permute-start(bf16[4,48,2432]{2,1,0:T(8,128)(2,1)} %collective-permute-done.29.refs_1_), channel_id=1, source_target_pairs={{0,1},{1,0},{2,3},{3,2},{4,5},{5,4},{6,7},{7,6},{8,9},{9,8},{10,11... | collective-permute-start | bytes 2801672 | tf_op jit(solution)/shard_map/ppermute | solution.py:39
  181.1 47.2 %collective-permute-start.37 = (bf16[4,48,2432]{2,1,0:T(8,128)(2,1)}, bf16[4,48,2432]{2,1,0:T(8,128)(2,1)}, u32[]{:S(2)}, u32[]{:S(2)}) collective-permute-start(bf16[4,48,2432]{2,1,0:T(8,128)(2,1)} %collective-permute-done.34.refs_2_), channel_id=1, source_target_pairs={{0,1},{1,0},{2,3},{3,2},{4,5},{5,4},{6,7},{7,6},{8,9},{9,8},{10,11... | collective-permute-start | bytes 2801672 | tf_op jit(solution)/shard_map/ppermute | solution.py:39
  317.4 35.6 %collective-permute-start.48 = (bf16[4,2,48,2432]{3,2,0,1:T(8,128)(2,1)S(1)}, bf16[4,2,48,2432]{3,2,0,1:T(8,128)(2,1)S(1)}, u32[]{:S(2)}, u32[]{:S(2)}) collective-permute-start(bf16[4,2,48,2432]{3,2,0,1:T(8,128)(2,1)S(1)} %bitcast_select_fusion.2), channel_id=1, source_target_pairs={{0,4},{1,3},{2,6},{3,1},{4,0},{5,7},{6,2},{7,5},{8,12},{9,11},{10,... | collective-permute-start | bytes 5603336 | tf_op jit(solution)/shard_map/ppermute | solution.py:39
  352.9 34.4 %collective-permute-start.53 = (bf16[2,128,384]{2,1,0:T(8,128)(2,1)S(1)}, bf16[2,128,384]{2,1,0:T(8,128)(2,1)S(1)}, u32[]{:S(2)}, u32[]{:S(2)}) collective-permute-start(bf16[2,128,384]{2,1,0:T(8,128)(2,1)S(1)} %constant_dynamic-slice_fusion.23), channel_id=1, source_target_pairs={{0,16},{1,17},{2,18},{3,19},{4,20},{5,21},{6,22},{7,23},{8,24},{9,... | collective-permute-start | bytes 589832 | tf_op jit(solution)/shard_map/ppermute | solution.py:39
  353.8 34.8 %collective-permute-start.51 = (bf16[4,48,2432]{2,1,0:T(8,128)(2,1)S(1)}, bf16[4,48,2432]{2,1,0:T(8,128)(2,1)S(1)}, u32[]{:S(2)}, u32[]{:S(2)}) collective-permute-start(bf16[4,48,2432]{2,1,0:T(8,128)(2,1)S(1)} %dynamic-slice_bitcast_fusion.1), channel_id=1, source_target_pairs={{0,2},{1,5},{2,0},{3,7},{4,6},{5,1},{6,4},{7,3},{8,10},{9,13},{10,... | collective-permute-start | bytes 2801672 | tf_op jit(solution)/shard_map/ppermute | solution.py:39
  409.8 33.2 %collective-permute-start.57 = (bf16[768,2432]{1,0:T(8,128)(2,1)}, bf16[768,2432]{1,0:T(8,128)(2,1)}, u32[]{:S(2)}, u32[]{:S(2)}) collective-permute-start(bf16[768,2432]{1,0:T(8,128)(2,1)} %get-tuple-element.238), channel_id=1, source_target_pairs={{0,1},{1,0},{2,3},{3,2},{4,5},{5,4},{6,7},{7,6},{8,9},{9,8},{10,11... | collective-permute-start | bytes 11206664 | tf_op jit(solution)/shard_map/ppermute | solution.py:39
  410.0 27.4 %collective-permute-start.56 = (bf16[128,384]{1,0:T(8,128)(2,1)S(1)}, bf16[128,384]{1,0:T(8,128)(2,1)}, u32[]{:S(2)}, u32[]{:S(2)}) collective-permute-start(bf16[128,384]{1,0:T(8,128)(2,1)S(1)} %dynamic-slice_bitcast_fusion.11), channel_id=1, source_target_pairs={{0,8},{1,9},{2,10},{3,11},{4,12},{5,13},{6,14},{7,15},{8,0},{9,1},... | collective-permute-start | bytes 294920 | tf_op jit(solution)/shard_map/ppermute | solution.py:39
  413.1 26.5 %collective-permute-start.87 = (f32[4,768]{1,0:T(4,128)S(1)}, f32[4,768]{1,0:T(4,128)S(1)}, u32[]{:S(2)}, u32[]{:S(2)}) collective-permute-start(f32[4,768]{1,0:T(4,128)S(1)} %pad_maximum_fusion.34), channel_id=1, source_target_pairs={{0,1},{1,0},{2,3},{3,2},{4,5},{5,4},{6,7},{7,6},{8,9},{9,8},{10,11... | collective-permute-start | bytes 36872 | tf_op jit(solution)/shard_map/ppermute | solution.py:39
  413.4 23.9 %collective-permute-start.55 = (bf16[2,48,2432]{2,1,0:T(8,128)(2,1)}, bf16[2,48,2432]{2,1,0:T(8,128)(2,1)S(1)}, u32[]{:S(2)}, u32[]{:S(2)}) collective-permute-start(bf16[2,48,2432]{2,1,0:T(8,128)(2,1)} %constant_dynamic-slice_fusion.22), channel_id=1, source_target_pairs={{0,16},{1,17},{2,18},{3,19},{4,20},{5,21},{6,22},{7,23},{8,24},{9,... | collective-permute-start | bytes 1400840 | tf_op jit(solution)/shard_map/ppermute | solution.py:39
  413.7 26.0 %collective-permute-start.54 = (bf16[4,48,1152]{2,1,0:T(8,128)(2,1)}, bf16[4,48,1152]{2,1,0:T(8,128)(2,1)S(1)}, u32[]{:S(2)}, u32[]{:S(2)}) collective-permute-start(bf16[4,48,1152]{2,1,0:T(8,128)(2,1)} %dynamic-slice_bitcast_fusion.3), channel_id=1, source_target_pairs={{0,2},{1,5},{2,0},{3,7},{4,6},{5,1},{6,4},{7,3},{8,10},{9,13},{10,... | collective-permute-start | bytes 1327112 | tf_op jit(solution)/shard_map/ppermute | solution.py:39
  438.5 30.1 %collective-permute-start.63 = (bf16[128,384]{1,0:T(8,128)(2,1)S(1)}, bf16[128,384]{1,0:T(8,128)(2,1)S(1)}, u32[]{:S(2)}, u32[]{:S(2)}) collective-permute-start(bf16[128,384]{1,0:T(8,128)(2,1)S(1)} %fusion.11), channel_id=1, source_target_pairs={{0,2},{1,3},{2,0},{3,1},{4,6},{5,7},{6,4},{7,5},{8,10},{9,11},{10,... | collective-permute-start | bytes 294920 | tf_op jit(solution)/shard_map/ppermute | solution.py:39
  439.7 28.4 %collective-permute-start.62 = (bf16[48,2432]{1,0:T(8,128)(2,1)S(1)}, bf16[48,2432]{1,0:T(8,128)(2,1)S(1)}, u32[]{:S(2)}, u32[]{:S(2)}) collective-permute-start(bf16[48,2432]{1,0:T(8,128)(2,1)S(1)} %dynamic-slice_bitcast_fusion.7), channel_id=1, source_target_pairs={{0,8},{1,9},{2,10},{3,11},{4,12},{5,13},{6,14},{7,15},{8,0},{9,1},... | collective-permute-start | bytes 700424 | tf_op jit(solution)/shard_map/ppermute | solution.py:39
  439.7 29.9 %collective-permute-start.88 = (f32[4,768]{1,0:T(4,128)S(1)}, f32[4,768]{1,0:T(4,128)S(1)}, u32[]{:S(2)}, u32[]{:S(2)}) collective-permute-start(f32[4,768]{1,0:T(4,128)S(1)} %fusion.26), channel_id=1, source_target_pairs={{0,2},{1,3},{2,0},{3,1},{4,6},{5,7},{6,4},{7,5},{8,10},{9,11},{10,... | collective-permute-start | bytes 36872 | tf_op jit(solution)/shard_map/ppermute | solution.py:39
  440.9 27.5 %collective-permute-start.61 = (bf16[2,48,1152]{2,1,0:T(8,128)(2,1)S(1)}, bf16[2,48,1152]{2,1,0:T(8,128)(2,1)S(1)}, u32[]{:S(2)}, u32[]{:S(2)}) collective-permute-start(bf16[2,48,1152]{2,1,0:T(8,128)(2,1)S(1)} %constant_dynamic-slice_fusion.17), channel_id=1, source_target_pairs={{0,16},{1,17},{2,18},{3,19},{4,20},{5,21},{6,22},{7,23},{8,24},{9,... | collective-permute-start | bytes 663560 | tf_op jit(solution)/shard_map/ppermute | solution.py:39
  469.6 28.1 %collective-permute-start.67 = (bf16[48,2432]{1,0:T(8,128)(2,1)S(1)}, bf16[48,2432]{1,0:T(8,128)(2,1)S(1)}, u32[]{:S(2)}, u32[]{:S(2)}) collective-permute-start(bf16[48,2432]{1,0:T(8,128)(2,1)S(1)} %fusion.7), channel_id=1, source_target_pairs={{0,2},{1,3},{2,0},{3,1},{4,6},{5,7},{6,4},{7,5},{8,10},{9,11},{10,... | collective-permute-start | bytes 700424 | tf_op jit(solution)/shard_map/ppermute | solution.py:39
  470.6 28.2 %collective-permute-start.66 = (bf16[48,1152]{1,0:T(8,128)(2,1)S(1)}, bf16[48,1152]{1,0:T(8,128)(2,1)S(1)}, u32[]{:S(2)}, u32[]{:S(2)}) collective-permute-start(bf16[48,1152]{1,0:T(8,128)(2,1)S(1)} %dynamic-slice_bitcast_fusion.9), channel_id=1, source_target_pairs={{0,8},{1,9},{2,10},{3,11},{4,12},{5,13},{6,14},{7,15},{8,0},{9,1},... | collective-permute-start | bytes 331784 | tf_op jit(solution)/shard_map/ppermute | solution.py:39
  471.0 38.9 %collective-permute-start.65 = (bf16[4,2,48,2432]{3,2,0,1:T(8,128)(2,1)S(1)}, bf16[4,2,48,2432]{3,2,0,1:T(8,128)(2,1)S(1)}, u32[]{:S(2)}, u32[]{:S(2)}) collective-permute-start(bf16[4,2,48,2432]{3,2,0,1:T(8,128)(2,1)S(1)} %bitcast_select_fusion), channel_id=1, source_target_pairs={{0,4},{1,3},{2,6},{3,1},{4,0},{5,7},{6,2},{7,5},{8,12},{9,11},{10,... | collective-permute-start | bytes 5603336 | tf_op jit(solution)/shard_map/ppermute | solution.py:39
  472.1 47.4 %collective-permute-start.69 = (bf16[256,384]{1,0:T(8,128)(2,1)S(1)}, bf16[256,384]{1,0:T(8,128)(2,1)S(1)}, u32[]{:S(2)}, u32[]{:S(2)}) collective-permute-start(bf16[256,384]{1,0:T(8,128)(2,1)S(1)} %pad_maximum_fusion.30), channel_id=1, source_target_pairs={{0,1},{1,0},{2,3},{3,2},{4,5},{5,4},{6,7},{7,6},{8,9},{9,8},{10,11... | collective-permute-start | bytes 589832 | tf_op jit(solution)/shard_map/ppermute | solution.py:39
  509.4 42.7 %collective-permute-start.90 = (f32[4,768]{1,0:T(4,128)S(1)}, f32[4,768]{1,0:T(4,128)S(1)}, u32[]{:S(2)}, u32[]{:S(2)}) collective-permute-start(f32[4,768]{1,0:T(4,128)S(1)} %add.323), channel_id=1, source_target_pairs={{0,8},{1,9},{2,10},{3,11},{4,12},{5,13},{6,14},{7,15},{8,0},{9,1},... | collective-permute-start | bytes 36872 | tf_op jit(solution)/shard_map/ppermute | solution.py:39
  519.8 31.2 %collective-permute-start.77 = (bf16[128,384]{1,0:T(8,128)(2,1)S(1)}, bf16[128,384]{1,0:T(8,128)(2,1)S(1)}, u32[]{:S(2)}, u32[]{:S(2)}) collective-permute-start(bf16[128,384]{1,0:T(8,128)(2,1)S(1)} %dynamic-slice_bitcast_fusion.10), channel_id=1, source_target_pairs={{0,8},{1,9},{2,10},{3,11},{4,12},{5,13},{6,14},{7,15},{8,0},{9,1},... | collective-permute-start | bytes 294920 | tf_op jit(solution)/shard_map/ppermute | solution.py:39
  520.3 45.2 %collective-permute-start.75 = (bf16[96,1152]{1,0:T(8,128)(2,1)S(1)}, bf16[96,1152]{1,0:T(8,128)(2,1)S(1)}, u32[]{:S(2)}, u32[]{:S(2)}) collective-permute-start(bf16[96,1152]{1,0:T(8,128)(2,1)S(1)} %pad_maximum_fusion.26), channel_id=1, source_target_pairs={{0,1},{1,0},{2,3},{3,2},{4,5},{5,4},{6,7},{7,6},{8,9},{9,8},{10,11... | collective-permute-start | bytes 663560 | tf_op jit(solution)/shard_map/ppermute | solution.py:39
  (174 other events, 2192.7 us)
Sparse Core Ops, SparseCore 0:
  69.0 76.0 all-gather.2

commit v3 on v2

--- a/solution.py
+++ b/solution.py
@@ -1011,40 +1011,47 @@
     dgate1, dup1, dr1, dr1_low, do1, gain_a = feed_back(
         tie(at, sent[0]), dr2, dr2_low, gate1, up1, r1, attn_one, open_one, down_one, True
     )
-    part = (open_g2.two(dr1), heads_g2.one(dr1), down_g2.next(dr1))
+    part = (open_g2.two(dr1), down_g2.next(dr1))
     bundles = [[(o1, [dr1_low]), (h1, [dgate1, dup1])], [(z1, [dr2_low])]]
     away, got = link.others(bundles, dr1, *part)
     second_out = close_second(tie(at, away[0]), z2, r3, down_two)
-    part = (heads_g2.two(second_out), open_g2.next(second_out), down_g2.three(second_out))
+    part = (heads_g2.one(second_out), down_g2.three(second_out))
     sent = link.mine_of(bundles, got, second_out, *part)
     open_g1, down_g1 = (
         link.reduce(link, grad, widths) for grad, widths in zip(sent, (open_widths, (width,)))
     )
     gain_grads = jnp.stack([jnp.sum(share, axis=0) for share in (gain_a, gain_b, gain_c, gain_d)])
     half = attend_back(at, tie(q1, sent[0]), k1, v1, o1, log1, do1, cosine, sine, 0, split)
-    part = (down_g1.one(half[0]), heads_g2.next(half[0]), open_g2.three(half[0]), down_g2.four(half[0]))
+    part = (heads_g2.two(half[0]), open_g2.next(half[0]), down_g2.four(half[0]))
     dq1, dk1, dv1 = attend_back(
         at, tie(q1, *part), k1, v1, o1, log1, do1, cosine, sine, split, pairs - split, half
     )
-    part = (open_g1.one(dq1), down_g1.two(dq1), heads_g2.three(dq1), open_g2.four(dq1))
+    part = (open_g1.one(dq1), down_g1.one(dq1), heads_g2.next(dq1))
     bundles = [[(low_tokens, [dq1, dk1, dv1])]]
     away, got = link.others(bundles, *part)
-    heads_g2.four(away[0])
-    part = (down_g1.next(away[0]), open_g1.two(away[0]))
-    (down_g2,) = down_g2.out(away[0])
-    output_g2, gate_g2, up_g2 = open_g2.out(away[0])
-    sent = link.mine_of(bundles, got, *part, down_g2, output_g2, gate_g2, up_g2)
+    input_grad = heads_back_first(tie(at, away[0]), dq1, dk1, dv1, dr1, heads_one)
+    part = (open_g1.two(input_grad), down_g1.two(input_grad))
+    sent = link.mine_of(bundles, got, input_grad, *part)
     heads_g1 = link.reduce(link, sent[0], attn_widths)
-    input_grad = heads_back_first(tie(at, sent[0]), dq1, dk1, dv1, dr1, heads_one)
-    part = (heads_g1.one(input_grad), open_g1.next(input_grad), down_g1.three(input_grad))
-    query_g2, key_g2, value_g2 = heads_g2.out(*part)
-    part = (heads_g1.two(query_g2), open_g1.three(query_g2), down_g1.four(query_g2))
-    heads_g1.next(part[0])
-    open_g1.four(part[0])
-    (down_g1,) = down_g1.out(part[0])
+    (down_g2,) = down_g2.out(sent[0])
+    part = (open_g2.three(sent[0]), heads_g2.three(sent[0]))
+    part = heads_g1.one(down_g2, *part)
+    open_g1.next(part)
+    down_g1.next(part)
+    open_g2.four(part)
+    heads_g2.four(part)
+    part = heads_g1.two()
+    open_g1.three(part)
+    down_g1.three(part)
+    output_g2, gate_g2, up_g2 = open_g2.out(part)
+    query_g2, key_g2, value_g2 = heads_g2.out(part)
+    last = heads_g1.next()
+    open_g1.four(last)
+    down_g1.four(last)
+    gain_grads = link.reduce_gains(gain_grads, half[0], sent[0], part, last, last)
     part = heads_g1.three()
+    (down_g1,) = down_g1.out(part)
     output_g1, gate_g1, up_g1 = open_g1.out(part)
-    gain_grads = link.reduce_gains(gain_grads, second_out, half[0], dq1, sent[0], input_grad)
     heads_g1.four()
     query_g1, key_g1, value_g1 = heads_g1.out()
     return (

time: 614 us -> 595 us (0.969)
  waiting for transfers between devices: 132 us -> 97.8 us
  starting transfers between devices: 76.2 us -> 85.4 us
    ppermute x92, waiting for transfers between devices: 132 us -> 97.7 us  [send(): return lax.ppermute(value, AXES, grid.pairs(move))]
    ppermute x92, starting transfers between devices: 76.2 us -> 85.4 us  [send(): return lax.ppermute(value, AXES, grid.pairs(move))]
    unnamed x212 -> x222, local copies, waits for them, and re-layouts: 53.1 us -> 56.5 us
  transfers between devices with their start and end apart: 93 -> 93, of which waited for: 25 -> 20; matrix products, arithmetic and copies ran while one was open for 6% -> 6% of each run, Pallas kernels for 39% -> 41%
where the time goes in v3:
time: 595 us; the launch traced here: 586 us
  Pallas kernels  285 us (48%)
  waiting for transfers between devices  97.8 us (16%)
  starting transfers between devices  85.4 us (14%)
  local copies, waits for them, and re-layouts  71.5 us (12%)
  other arithmetic  29.3 us (5%)
  between operations  17.6 us (3%)
    pallas_call x18, Pallas kernels, call(): pl.pallas_call(kernel, out_shape=outs, in_specs=[SCALARS] + [NEAR] * len(...  169 us
    pallas_call x8, Pallas kernels, call_pairs(): pl.pallas_call(kernel, out_shape=outs, grid_spec=pltpu.PrefetchScalarGrid...  115 us
    ppermute x92, waiting for transfers between devices, send(): return lax.ppermute(value, AXES, grid.pairs(move))  97.7 us
    ppermute x92, starting transfers between devices, send(): return lax.ppermute(value, AXES, grid.pairs(move))  85.4 us
    unnamed x222, local copies, waits for them, and re-layouts  56.5 us
  transfers between devices with their start and end apart: 93, of which 20 were waited for; matrix products, arithmetic and copies ran while one was open for 6% of the time, Pallas kernels for 41%

profile of v3, /device:TPU:0, one launch (start us, length us, event | category | flops | bytes accessed | tf_op | source)
XLA Modules:
  0.0 586.3 jit_solution(3040239040962943073)
XLA Ops:
  19.7 10.5 %collective-permute-done.1 = bf16[2,48,1280]{2,1,0:T(8,128)(2,1)S(1)} collective-permute-done((bf16[2,48,1280]{2,1,0:T(8,128)(2,1)S(1)}, bf16[2,48,1280]{2,1,0:T(8,128)(2,1)S(1)}, u32[]{:S(2)}, u32[]{:S(2)}) %collective-permute-start.1) | collective-permute-done | bytes 245792 | tf_op jit(solution)/shard_map/ppermute | solution.py:39
  46.1 5.0 collective-permute-done.4.refs_3_
  54.6 9.8 %collective-permute-done.10 = bf16[2,48,2432]{2,1,0:T(8,128)(2,1)} collective-permute-done((bf16[2,48,2432]{2,1,0:T(8,128)(2,1)}, bf16[2,48,2432]{2,1,0:T(8,128)(2,1)}, u32[]{:S(2)}, u32[]{:S(2)}) %collective-permute-start.10) | collective-permute-done | bytes 466976 | tf_op jit(solution)/shard_map/ppermute | solution.py:39
  69.0 7.5 %shard_map.373 = (bf16[1024,768]{1,0:T(8,128)(2,1)S(1)}, bf16[1024,768]{1,0:T(8,128)(2,1)S(1)}, bf16[1024,768]{1,0:T(8,128)(2,1)S(1)}) custom-call(s32[5]{0:T(128)S(1)} %concatenate.113.at_ref, bf16[1024,768]{1,0:T(8,128)(2,1)S(1)} %bitcast.192, f32[1024,128]{1,0:T(8,128)S(1)} %get-tuple-element.378.cos_ref, f32[1024,128]{1,0:T(8,128)S(1)} %get-tuple-element.379.sin_ref, ...), custom_call_target="tpu_custom_call" | custom-call | flops 8800000000 | bytes 800000 | tf_op jit(solution)/shard_map/pallas_call | solution.py:176
  80.1 12.8 %shard_map.374 = (bf16[1024,768]{1,0:T(8,128)(2,1)}, f32[6,16,1024]{2,1,0:T(8,128)}) custom-call(s32[5]{0:T(128)S(1)} %concatenate.113.at_ref, bf16[1024,768]{1,0:T(8,128)(2,1)} %copy-done.70, bf16[1024,768]{1,0:T(8,128)(2,1)} %copy-done.71, bf16[1024,768]{1,0:T(8,128)(2,1)} %copy-done.72), custom_call_target="tpu_custom_call" | custom-call | flops 13200000000 | bytes 1200000 | tf_op jit(solution)/shard_map/pallas_call | solution.py:210
  100.0 7.6 %collective-permute-done.13 = bf16[2,128,384]{2,1,0:T(8,128)(2,1)S(1)} collective-permute-done((bf16[2,128,384]{2,1,0:T(8,128)(2,1)S(1)}, bf16[2,128,384]{2,1,0:T(8,128)(2,1)S(1)}, u32[]{:S(2)}, u32[]{:S(2)}) %collective-permute-start.13) | collective-permute-done | bytes 196640 | tf_op jit(solution)/shard_map/ppermute | solution.py:39
  110.2 13.0 %shard_map.375 = (bf16[1024,768]{1,0:T(8,128)(2,1)}, f32[6,16,1024]{2,1,0:T(8,128)}) custom-call(s32[5]{0:T(128)S(1)} %concatenate.113.at_ref, bf16[1024,768]{1,0:T(8,128)(2,1)} %copy-done.70, bf16[1024,768]{1,0:T(8,128)(2,1)} %copy-done.71, bf16[1024,768]{1,0:T(8,128)(2,1)} %copy-done.72, ...), custom_call_target="tpu_custom_call", output_to_operand_aliasing={{0}: (4, {}), {1}: (5, {})} | custom-call | flops 13200000000 | bytes 1200000 | tf_op jit(solution)/shard_map/pallas_call | solution.py:210
  130.4 14.2 %shard_map.376 = (f32[1024,768]{1,0:T(8,128)S(1)}, bf16[1024,768]{1,0:T(8,128)(2,1)S(1)}, bf16[1024,2048]{1,0:T(8,128)(2,1)S(1)}, bf16[1024,2048]{1,0:T(8,128)(2,1)S(1)}, bf16[1024,2048]{1,0:T(8,128)(2,1)S(1)}) custom-call(s32[5]{0:T(128)S(1)} %concatenate.113.at_ref, bf16[1024,768]{1,0:T(8,128)(2,1)S(1)} %copy-done.54, bf16[1024,768]{1,0:T(8,128)(2,1)S(1)} %bitcast.193, ...), custom_call_target="tpu_custom_call" | custom-call | flops 13200000000 | bytes 1200000 | tf_op jit(solution)/shard_map/pallas_call | solution.py:176
  160.7 8.8 %shard_map.377 = (f32[1024,768]{1,0:T(8,128)S(1)}, f32[1024,768]{1,0:T(8,128)}, bf16[1024,768]{1,0:T(8,128)(2,1)S(1)}) custom-call(s32[5]{0:T(128)S(1)} %concatenate.113.at_ref, bf16[1024,2048]{1,0:T(8,128)(2,1)S(1)} %get-tuple-element.168.z_ref.refs_5_, f32[1024,768]{1,0:T(8,128)S(1)} %get-tuple-element.169.r_ref, ...), custom_call_target="tpu_custom_call" | custom-call | flops 8800000000 | bytes 800000 | tf_op jit(solution)/shard_map/pallas_call | solution.py:176
  173.5 7.6 %collective-permute-done.29.refs_1_ = bf16[4,48,2432]{2,1,0:T(8,128)(2,1)} collective-permute-done((bf16[4,48,2432]{2,1,0:T(8,128)(2,1)}, bf16[4,48,2432]{2,1,0:T(8,128)(2,1)}, u32[]{:S(2)}, u32[]{:S(2)}) %collective-permute-start.29) | collective-permute-done | bytes 933920 | tf_op jit(solution)/shard_map/ppermute | solution.py:39
  185.8 7.5 %shard_map.378 = (bf16[1024,768]{1,0:T(8,128)(2,1)S(1)}, bf16[1024,768]{1,0:T(8,128)(2,1)S(1)}, bf16[1024,768]{1,0:T(8,128)(2,1)S(1)}) custom-call(s32[5]{0:T(128)S(1)} %concatenate.113.at_ref, bf16[1024,768]{1,0:T(8,128)(2,1)S(1)} %copy-done.10, f32[1024,128]{1,0:T(8,128)S(1)} %get-tuple-element.378.cos_ref, f32[1024,128]{1,0:T(8,128)S(1)} %get-tuple-element.379.sin_ref, ...), custom_call_target="tpu_custom_call" | custom-call | flops 8800000000 | bytes 800000 | tf_op jit(solution)/shard_map/pallas_call | solution.py:176
  198.8 12.6 %shard_map.379 = (bf16[1024,768]{1,0:T(8,128)(2,1)}, f32[6,16,1024]{2,1,0:T(8,128)}) custom-call(s32[5]{0:T(128)S(1)} %concatenate.113.at_ref, bf16[1024,768]{1,0:T(8,128)(2,1)} %copy-done.73, bf16[1024,768]{1,0:T(8,128)(2,1)} %copy-done.74, bf16[1024,768]{1,0:T(8,128)(2,1)} %copy-done.75), custom_call_target="tpu_custom_call" | custom-call | flops 13200000000 | bytes 1200000 | tf_op jit(solution)/shard_map/pallas_call | solution.py:210
  214.5 13.3 %shard_map.380 = (bf16[1024,768]{1,0:T(8,128)(2,1)}, f32[6,16,1024]{2,1,0:T(8,128)}) custom-call(s32[5]{0:T(128)S(1)} %concatenate.113.at_ref, bf16[1024,768]{1,0:T(8,128)(2,1)} %copy-done.73, bf16[1024,768]{1,0:T(8,128)(2,1)} %copy-done.74, bf16[1024,768]{1,0:T(8,128)(2,1)} %copy-done.75, ...), custom_call_target="tpu_custom_call", output_to_operand_aliasing={{0}: (4, {}), {1}: (5, {})} | custom-call | flops 13200000000 | bytes 1200000 | tf_op jit(solution)/shard_map/pallas_call | solution.py:210
  231.3 14.1 %shard_map.381 = (f32[1024,768]{1,0:T(8,128)S(1)}, bf16[1024,768]{1,0:T(8,128)(2,1)S(1)}, bf16[1024,2048]{1,0:T(8,128)(2,1)S(1)}, bf16[1024,2048]{1,0:T(8,128)(2,1)S(1)}, bf16[1024,2048]{1,0:T(8,128)(2,1)S(1)}) custom-call(s32[5]{0:T(128)S(1)} %concatenate.113.at_ref, bf16[1024,768]{1,0:T(8,128)(2,1)S(1)} %copy-done.57, f32[1024,768]{1,0:T(8,128)S(1)} %copy-done.7, ...), custom_call_target="tpu_custom_call" | custom-call | flops 13200000000 | bytes 1200000 | tf_op jit(solution)/shard_map/pallas_call | solution.py:176
  250.6 4.6 copy-done.63
  257.4 24.1 %shard_map.382 = (bf16[1024,2048]{1,0:T(8,128)(2,1)S(1)}, bf16[1024,2048]{1,0:T(8,128)(2,1)S(1)}, f32[1024,768]{1,0:T(8,128)S(1)}, bf16[1024,768]{1,0:T(8,128)(2...) custom-call(s32[5]{0:T(128)S(1)} %concatenate.113.at_ref, bf16[1024,768]{1,0:T(8,128)(2,1)S(1)} %bitcast.188, ...), custom_call_target="tpu_custom_call" | custom-call | flops 26400000000 | bytes 2400000 | tf_op jit(solution)/shard_map/pallas_call | solution.py:176
  282.6 6.7 %shard_map.383 = (bf16[768,2432]{1,0:T(8,128)(2,1)}, bf16[2048,384]{1,0:T(8,128)(2,1)S(1)}) custom-call(s32[1]{0:T(128)S(6)} %sub.66.half_ref, bf16[1024,768]{1,0:T(8,128)(2,1)S(1)} %copy-done.58, bf16[1024,768]{1,0:T(8,128)(2,1)S(1)} %get-tuple-element.195.refs_1_, bf16[1024,768]{1,0:T(8,128)(2,1)S(1)} %get-tuple-element.196.refs_2_, ...), custom_call_target="tpu_custom_call" | custom-call | flops 9900000256 | bytes 900000 | tf_op jit(solution)/shard_map/pallas_call | solution.py:176
  290.1 16.3 %shard_map.384 = (bf16[1024,768]{1,0:T(8,128)(2,1)}, bf16[1024,768]{1,0:T(8,128)(2,1)}, bf16[1024,768]{1,0:T(8,128)(2,1)}) custom-call(s32[5]{0:T(128)S(1)} %concatenate.113.at_ref, bf16[1024,768]{1,0:T(8,128)(2,1)} %copy-done.73, bf16[1024,768]{1,0:T(8,128)(2,1)} %copy-done.74, bf16[1024,768]{1,0:T(8,128)(2,1)} %copy-done.75, ...), custom_call_target="tpu_custom_call" | custom-call | flops 16499999744 | bytes 1500000 | tf_op jit(solution)/shard_map/pallas_call | solution.py:210
  306.5 8.6 %shard_map.385 = (bf16[768,2432]{1,0:T(8,128)(2,1)S(1)}, bf16[2048,384]{1,0:T(8,128)(2,1)S(1)}) custom-call(s32[1]{0:T(128)} %bitcast.3.half_ref, bf16[1024,768]{1,0:T(8,128)(2,1)S(1)} %copy-done.59, bf16[1024,768]{1,0:T(8,128)(2,1)S(1)} %copy-done.53, bf16[1024,768]{1,0:T(8,128)(2,1)S(1)} %copy-done.51, bf16[1024,2048]{1,0:T(8,128)(2,1)S(1)} %copy-done.31, ...), custom_call_target="tpu_custom_call" | custom-call | flops 9900000256 | bytes 900000 | tf_op jit(solution)/shard_map/pallas_call | solution.py:176
  318.6 16.0 %shard_map.386 = (bf16[1024,768]{1,0:T(8,128)(2,1)}, bf16[1024,768]{1,0:T(8,128)(2,1)}, bf16[1024,768]{1,0:T(8,128)(2,1)}) custom-call(s32[5]{0:T(128)S(1)} %concatenate.113.at_ref, bf16[1024,768]{1,0:T(8,128)(2,1)} %copy-done.73, bf16[1024,768]{1,0:T(8,128)(2,1)} %copy-done.74, ...), custom_call_target="tpu_custom_call", output_to_operand_aliasing={{0}: (9, {}), {1}: (10, {}), {2}: (11, {})} | custom-call | flops 16499999744 | bytes 1500000 | tf_op jit(solution)/shard_map/pallas_call | solution.py:210
  343.1 9.9 %shard_map.388 = (f32[1024,768]{1,0:T(8,128)S(1)}, bf16[1024,768]{1,0:T(8,128)(2,1)S(1)}, f32[8,768]{1,0:T(8,128)S(1)}, f32[8,768]{1,0:T(8,128)S(1)}) custom-call(s32[5]{0:T(128)S(1)} %concatenate.113.at_ref, bf16[1024,768]{1,0:T(8,128)(2,1)S(1)} %copy-done.15, bf16[1024,768]{1,0:T(8,128)(2,1)S(1)} %copy-done.17, bf16[1024,768]{1,0:T(8,128)(2,1)S(1)} %copy-done.19, ...), custom_call_target="tpu_custom_call" | custom-call | flops 8800000000 | bytes 800000 | tf_op jit(solution)/shard_map/pallas_call | solution.py:176
  360.5 25.0 %shard_map.390 = (bf16[1024,2048]{1,0:T(8,128)(2,1)S(1)}, bf16[1024,2048]{1,0:T(8,128)(2,1)S(1)}, f32[1024,768]{1,0:T(8,128)S(1)}, bf16[1024,768]{1,0:T(8,128)(2...) custom-call(s32[5]{0:T(128)S(1)} %concatenate.113.at_ref, f32[1024,768]{1,0:T(8,128)S(1)} %get-tuple-element.219.du_ref, ...), custom_call_target="tpu_custom_call" | custom-call | flops 26400000000 | bytes 2400000 | tf_op jit(solution)/shard_map/pallas_call | solution.py:176
  392.4 6.5 %shard_map.391 = (bf16[768,2432]{1,0:T(8,128)(2,1)}, bf16[2048,384]{1,0:T(8,128)(2,1)S(1)}) custom-call(s32[1]{0:T(128)S(6)} %sub.66.half_ref, bf16[1024,768]{1,0:T(8,128)(2,1)S(1)} %copy-done.55, bf16[1024,768]{1,0:T(8,128)(2,1)S(1)} %get-tuple-element.231.refs_1_, bf16[1024,768]{1,0:T(8,128)(2,1)S(1)} %copy-done.43, ...), custom_call_target="tpu_custom_call" | custom-call | flops 9900000256 | bytes 900000 | tf_op jit(solution)/shard_map/pallas_call | solution.py:176
  413.4 8.3 %shard_map.392 = f32[1024,768]{1,0:T(8,128)} custom-call(s32[5]{0:T(128)S(1)} %concatenate.113.at_ref, bf16[1024,2048]{1,0:T(8,128)(2,1)S(1)} %copy-done.25, f32[1024,768]{1,0:T(8,128)S(1)} %copy-done.37, bf16[4,128,384]{2,1,0:T(8,128)(2,1)} %copy-done.88, bf16[4,128,384]{2,1,0:T(8,128)(2,1)} %copy-done.102, bf16[4,128,384]{2,1,0:T(8,128)(2,1)} %copy-done.104, ...), custom_call_target="tpu_custom_call" | custom-call | flops 7699999744 | bytes 700000 | tf_op jit(solution)/shard_map/pallas_call | solution.py:176
  426.3 8.8 %shard_map.393 = (bf16[768,2432]{1,0:T(8,128)(2,1)S(1)}, bf16[2048,384]{1,0:T(8,128)(2,1)S(1)}) custom-call(s32[1]{0:T(128)} %bitcast.3.half_ref, bf16[1024,768]{1,0:T(8,128)(2,1)S(1)} %copy-done.56, bf16[1024,768]{1,0:T(8,128)(2,1)S(1)} %copy-done.49, bf16[1024,768]{1,0:T(8,128)(2,1)S(1)} %copy-done.44, bf16[1024,2048]{1,0:T(8,128)(2,1)S(1)} %copy-done.27, ...), custom_call_target="tpu_custom_call" | custom-call | flops 9900000256 | bytes 900000 | tf_op jit(solution)/shard_map/pallas_call | solution.py:176
  435.0 15.5 %shard_map.394 = (bf16[1024,768]{1,0:T(8,128)(2,1)}, bf16[1024,768]{1,0:T(8,128)(2,1)}, bf16[1024,768]{1,0:T(8,128)(2,1)}) custom-call(s32[5]{0:T(128)S(1)} %concatenate.113.at_ref, bf16[1024,768]{1,0:T(8,128)(2,1)} %copy-done.70, bf16[1024,768]{1,0:T(8,128)(2,1)} %copy-done.71, bf16[1024,768]{1,0:T(8,128)(2,1)} %copy-done.72, ...), custom_call_target="tpu_custom_call" | custom-call | flops 16499999744 | bytes 1500000 | tf_op jit(solution)/shard_map/pallas_call | solution.py:210
  458.5 15.7 %shard_map.395 = (bf16[1024,768]{1,0:T(8,128)(2,1)}, bf16[1024,768]{1,0:T(8,128)(2,1)}, bf16[1024,768]{1,0:T(8,128)(2,1)}) custom-call(s32[5]{0:T(128)S(1)} %concatenate.113.at_ref, bf16[1024,768]{1,0:T(8,128)(2,1)} %copy-done.70, bf16[1024,768]{1,0:T(8,128)(2,1)} %copy-done.71, ...), custom_call_target="tpu_custom_call", output_to_operand_aliasing={{0}: (9, {}), {1}: (10, {}), {2}: (11, {})} | custom-call | flops 16499999744 | bytes 1500000 | tf_op jit(solution)/shard_map/pallas_call | solution.py:210
  475.6 16.8 %collective-permute-done.57 = bf16[4,2,48,2432]{3,2,0,1:T(8,128)(2,1)S(1)} collective-permute-done((bf16[4,2,48,2432]{3,2,0,1:T(8,128)(2,1)S(1)}, bf16[4,2,48,2432]{3,2,0,1:T(8,128)(2,1)S(1)}, u32[]{:S(2)}, u32[]{:S(2)}) %collective-permute-start.57) | collective-permute-done | bytes 1867808 | tf_op jit(solution)/shard_map/ppermute | solution.py:39
  498.2 8.9 %shard_map.397 = f32[1024,768]{1,0:T(8,128)} custom-call(s32[5]{0:T(128)S(1)} %concatenate.113.at_ref, bf16[1024,768]{1,0:T(8,128)(2,1)S(1)} %copy-done.12, bf16[1024,768]{1,0:T(8,128)(2,1)S(1)} %copy-done.13, bf16[1024,768]{1,0:T(8,128)(2,1)S(1)} %copy-done.14, f32[1024,768]{1,0:T(8,128)S(1)} %copy-done.35, bf16[4,48,1280]{2,1,0:T(8,128)(2,1)} %pad_maximum_fusion.8.refs_0_, ...), custom_call_target="tpu_custom_call" | custom-call | flops 7699999744 | bytes 700000 | tf_op jit(solution)/shard_map/pallas_call | solution.py:176
  521.0 8.8 %collective-permute-done.66 = bf16[4,2,48,1152]{3,2,0,1:T(8,128)(2,1)S(1)} collective-permute-done((bf16[4,2,48,1152]{3,2,0,1:T(8,128)(2,1)S(1)}, bf16[4,2,48,1152]{3,2,0,1:T(8,128)(2,1)S(1)}, u32[]{:S(2)}, u32[]{:S(2)}) %collective-permute-start.66) | collective-permute-done | bytes 884768 | tf_op jit(solution)/shard_map/ppermute | solution.py:39
  536.6 5.8 collective-permute-done.75
  547.0 4.4 collective-permute-done.80
  (570 shorter events, 213.6 us)
Async XLA Ops:
  7.2 177.1 %all-gather.3.cloned.1.call-start = ((), (), s32[]{:S(2)}) async-start(), calls=%async_computation | async-start | bytes 3649536 | tf_op jit(solution)/shard_map/all_gather | solution.py:745
  45.6 23.3 %collective-permute-start.5 = (bf16[4,48,1280]{2,1,0:T(8,128)(2,1)}, bf16[4,48,1280]{2,1,0:T(8,128)(2,1)}, u32[]{:S(2)}, u32[]{:S(2)}) collective-permute-start(bf16[4,48,1280]{2,1,0:T(8,128)(2,1)} %pad_maximum_fusion.8.refs_0_), channel_id=1, source_target_pairs={{0,1},{1,0},{2,3},{3,2},{4,5},{5,4},{6,7},{7,6},{8,9},{9,8},{10,11... | collective-permute-start | bytes 1474568 | tf_op jit(solution)/shard_map/ppermute | solution.py:39
  45.6 23.4 %collective-permute-start.6 = (bf16[4,48,1280]{2,1,0:T(8,128)(2,1)}, bf16[4,48,1280]{2,1,0:T(8,128)(2,1)}, u32[]{:S(2)}, u32[]{:S(2)}) collective-permute-start(bf16[4,48,1280]{2,1,0:T(8,128)(2,1)} %collective-permute-done.2.refs_1_), channel_id=1, source_target_pairs={{0,1},{1,0},{2,3},{3,2},{4,5},{5,4},{6,7},{7,6},{8,9},{9,8},{10,11... | collective-permute-start | bytes 1474568 | tf_op jit(solution)/shard_map/ppermute | solution.py:39
  46.1 22.9 %collective-permute-start.7 = (bf16[4,48,1280]{2,1,0:T(8,128)(2,1)}, bf16[4,48,1280]{2,1,0:T(8,128)(2,1)}, u32[]{:S(2)}, u32[]{:S(2)}) collective-permute-start(bf16[4,48,1280]{2,1,0:T(8,128)(2,1)} %collective-permute-done.3.refs_2_), channel_id=1, source_target_pairs={{0,1},{1,0},{2,3},{3,2},{4,5},{5,4},{6,7},{7,6},{8,9},{9,8},{10,11... | collective-permute-start | bytes 1474568 | tf_op jit(solution)/shard_map/ppermute | solution.py:39
  66.4 26.5 %collective-permute-start.11 = (bf16[4,48,2432]{2,1,0:T(8,128)(2,1)}, bf16[4,48,2432]{2,1,0:T(8,128)(2,1)}, u32[]{:S(2)}, u32[]{:S(2)}) collective-permute-start(bf16[4,48,2432]{2,1,0:T(8,128)(2,1)} %pad_maximum_fusion.refs_0_), channel_id=1, source_target_pairs={{0,2},{1,5},{2,0},{3,7},{4,6},{5,1},{6,4},{7,3},{8,10},{9,13},{10,... | collective-permute-start | bytes 2801672 | tf_op jit(solution)/shard_map/ppermute | solution.py:39
  68.9 40.7 %collective-permute-start.14 = (bf16[4,48,2432]{2,1,0:T(8,128)(2,1)}, bf16[4,48,2432]{2,1,0:T(8,128)(2,1)}, u32[]{:S(2)}, u32[]{:S(2)}) collective-permute-start(bf16[4,48,2432]{2,1,0:T(8,128)(2,1)} %pad_maximum_fusion.refs_0_), channel_id=1, source_target_pairs={{0,4},{1,3},{2,6},{3,1},{4,0},{5,7},{6,2},{7,5},{8,12},{9,11},{10,... | collective-permute-start | bytes 2801672 | tf_op jit(solution)/shard_map/ppermute | solution.py:39
  99.9 23.2 %collective-permute-start.16 = (bf16[4,48,2432]{2,1,0:T(8,128)(2,1)}, bf16[4,48,2432]{2,1,0:T(8,128)(2,1)S(1)}, u32[]{:S(2)}, u32[]{:S(2)}) collective-permute-start(bf16[4,48,2432]{2,1,0:T(8,128)(2,1)} %pad_maximum_fusion.refs_0_), channel_id=1, source_target_pairs={{0,1},{1,0},{2,3},{3,2},{4,5},{5,4},{6,7},{7,6},{8,9},{9,8},{10,11... | collective-permute-start | bytes 2801672 | tf_op jit(solution)/shard_map/ppermute | solution.py:39
  107.7 40.8 %collective-permute-start.20 = (bf16[4,128,384]{2,1,0:T(8,128)(2,1)S(1)}, bf16[4,128,384]{2,1,0:T(8,128)(2,1)S(1)}, u32[]{:S(2)}, u32[]{:S(2)}) collective-permute-start(bf16[4,128,384]{2,1,0:T(8,128)(2,1)S(1)} %pad_maximum_fusion.13.refs_0_.refs_8_), channel_id=1, source_target_pairs={{0,2},{1,5},{2,0},{3,7},{4,6},{5,1},{6,4},{7,3},{8,10},{9,13},{10,... | collective-permute-start | bytes 1179656 | tf_op jit(solution)/shard_map/ppermute | solution.py:39
  123.2 28.0 %collective-permute-start.21 = (bf16[4,128,384]{2,1,0:T(8,128)(2,1)S(1)}, bf16[4,128,384]{2,1,0:T(8,128)(2,1)S(1)}, u32[]{:S(2)}, u32[]{:S(2)}) collective-permute-start(bf16[4,128,384]{2,1,0:T(8,128)(2,1)S(1)} %pad_maximum_fusion.13.refs_0_.refs_8_), channel_id=1, source_target_pairs={{0,4},{1,3},{2,6},{3,1},{4,0},{5,7},{6,2},{7,5},{8,12},{9,11},{10,... | collective-permute-start | bytes 1179656 | tf_op jit(solution)/shard_map/ppermute | solution.py:39
  124.6 26.9 %collective-permute-start.28 = (bf16[2,48,2432]{2,1,0:T(8,128)(2,1)S(1)}, bf16[2,48,2432]{2,1,0:T(8,128)(2,1)S(1)}, u32[]{:S(2)}, u32[]{:S(2)}) collective-permute-start(bf16[2,48,2432]{2,1,0:T(8,128)(2,1)S(1)} %pad_maximum_fusion.10), channel_id=1, source_target_pairs={{0,16},{1,17},{2,18},{3,19},{4,20},{5,21},{6,22},{7,23},{8,24},{9,... | collective-permute-start | bytes 1400840 | tf_op jit(solution)/shard_map/ppermute | solution.py:39
  157.5 23.6 %collective-permute-start.29 = (bf16[4,48,2432]{2,1,0:T(8,128)(2,1)}, bf16[4,48,2432]{2,1,0:T(8,128)(2,1)}, u32[]{:S(2)}, u32[]{:S(2)}) collective-permute-start(bf16[4,48,2432]{2,1,0:T(8,128)(2,1)} %pad_maximum_fusion.1.refs_0_), channel_id=1, source_target_pairs={{0,2},{1,5},{2,0},{3,7},{4,6},{5,1},{6,4},{7,3},{8,10},{9,13},{10,... | collective-permute-start | bytes 2801672 | tf_op jit(solution)/shard_map/ppermute | solution.py:39
  158.4 22.7 %collective-permute-start.34 = (bf16[4,48,2432]{2,1,0:T(8,128)(2,1)}, bf16[4,48,2432]{2,1,0:T(8,128)(2,1)}, u32[]{:S(2)}, u32[]{:S(2)}) collective-permute-start(bf16[4,48,2432]{2,1,0:T(8,128)(2,1)} %pad_maximum_fusion.1.refs_0_), channel_id=1, source_target_pairs={{0,4},{1,3},{2,6},{3,1},{4,0},{5,7},{6,2},{7,5},{8,12},{9,11},{10,... | collective-permute-start | bytes 2801672 | tf_op jit(solution)/shard_map/ppermute | solution.py:39
  173.5 41.0 %collective-permute-start.35 = (bf16[4,48,2432]{2,1,0:T(8,128)(2,1)}, bf16[4,48,2432]{2,1,0:T(8,128)(2,1)}, u32[]{:S(2)}, u32[]{:S(2)}) collective-permute-start(bf16[4,48,2432]{2,1,0:T(8,128)(2,1)} %pad_maximum_fusion.1.refs_0_), channel_id=1, source_target_pairs={{0,1},{1,0},{2,3},{3,2},{4,5},{5,4},{6,7},{7,6},{8,9},{9,8},{10,11... | collective-permute-start | bytes 2801672 | tf_op jit(solution)/shard_map/ppermute | solution.py:39
  181.1 46.7 %collective-permute-start.36 = (bf16[4,48,2432]{2,1,0:T(8,128)(2,1)}, bf16[4,48,2432]{2,1,0:T(8,128)(2,1)}, u32[]{:S(2)}, u32[]{:S(2)}) collective-permute-start(bf16[4,48,2432]{2,1,0:T(8,128)(2,1)} %collective-permute-done.29.refs_1_), channel_id=1, source_target_pairs={{0,1},{1,0},{2,3},{3,2},{4,5},{5,4},{6,7},{7,6},{8,9},{9,8},{10,11... | collective-permute-start | bytes 2801672 | tf_op jit(solution)/shard_map/ppermute | solution.py:39
  181.1 47.3 %collective-permute-start.37 = (bf16[4,48,2432]{2,1,0:T(8,128)(2,1)}, bf16[4,48,2432]{2,1,0:T(8,128)(2,1)}, u32[]{:S(2)}, u32[]{:S(2)}) collective-permute-start(bf16[4,48,2432]{2,1,0:T(8,128)(2,1)} %collective-permute-done.34.refs_2_), channel_id=1, source_target_pairs={{0,1},{1,0},{2,3},{3,2},{4,5},{5,4},{6,7},{7,6},{8,9},{9,8},{10,11... | collective-permute-start | bytes 2801672 | tf_op jit(solution)/shard_map/ppermute | solution.py:39
  227.8 21.7 %collective-permute-start.41 = (bf16[4,128,384]{2,1,0:T(8,128)(2,1)S(1)}, bf16[4,128,384]{2,1,0:T(8,128)(2,1)S(1)}, u32[]{:S(2)}, u32[]{:S(2)}) collective-permute-start(bf16[4,128,384]{2,1,0:T(8,128)(2,1)S(1)} %pad_maximum_fusion.14.refs_8_.refs_0_), channel_id=1, source_target_pairs={{0,1},{1,0},{2,3},{3,2},{4,5},{5,4},{6,7},{7,6},{8,9},{9,8},{10,11... | collective-permute-start | bytes 1179656 | tf_op jit(solution)/shard_map/ppermute | solution.py:39
  317.4 35.9 %collective-permute-start.48 = (bf16[4,2,48,2432]{3,2,0,1:T(8,128)(2,1)S(1)}, bf16[4,2,48,2432]{3,2,0,1:T(8,128)(2,1)S(1)}, u32[]{:S(2)}, u32[]{:S(2)}) collective-permute-start(bf16[4,2,48,2432]{3,2,0,1:T(8,128)(2,1)S(1)} %bitcast_select_fusion.2), channel_id=1, source_target_pairs={{0,4},{1,3},{2,6},{3,1},{4,0},{5,7},{6,2},{7,5},{8,12},{9,11},{10,... | collective-permute-start | bytes 5603336 | tf_op jit(solution)/shard_map/ppermute | solution.py:39
  353.2 35.3 %collective-permute-start.52 = (bf16[2,128,384]{2,1,0:T(8,128)(2,1)S(1)}, bf16[2,128,384]{2,1,0:T(8,128)(2,1)S(1)}, u32[]{:S(2)}, u32[]{:S(2)}) collective-permute-start(bf16[2,128,384]{2,1,0:T(8,128)(2,1)S(1)} %constant_dynamic-slice_fusion.23), channel_id=1, source_target_pairs={{0,16},{1,17},{2,18},{3,19},{4,20},{5,21},{6,22},{7,23},{8,24},{9,... | collective-permute-start | bytes 589832 | tf_op jit(solution)/shard_map/ppermute | solution.py:39
  355.1 33.5 %collective-permute-start.51 = (bf16[4,48,2432]{2,1,0:T(8,128)(2,1)}, bf16[4,48,2432]{2,1,0:T(8,128)(2,1)S(1)}, u32[]{:S(2)}, u32[]{:S(2)}) collective-permute-start(bf16[4,48,2432]{2,1,0:T(8,128)(2,1)} %dynamic-slice_bitcast_fusion.1), channel_id=1, source_target_pairs={{0,2},{1,5},{2,0},{3,7},{4,6},{5,1},{6,4},{7,3},{8,10},{9,13},{10,... | collective-permute-start | bytes 2801672 | tf_op jit(solution)/shard_map/ppermute | solution.py:39
  402.0 23.5 %collective-permute-start.55 = (bf16[768,2432]{1,0:T(8,128)(2,1)}, bf16[768,2432]{1,0:T(8,128)(2,1)}, u32[]{:S(2)}, u32[]{:S(2)}) collective-permute-start(bf16[768,2432]{1,0:T(8,128)(2,1)} %get-tuple-element.235), channel_id=1, source_target_pairs={{0,1},{1,0},{2,3},{3,2},{4,5},{5,4},{6,7},{7,6},{8,9},{9,8},{10,11... | collective-permute-start | bytes 11206664 | tf_op jit(solution)/shard_map/ppermute | solution.py:39
  408.7 47.3 %collective-permute-start.83 = (f32[4,768]{1,0:T(4,128)S(1)}, f32[4,768]{1,0:T(4,128)S(1)}, u32[]{:S(2)}, u32[]{:S(2)}) collective-permute-start(f32[4,768]{1,0:T(4,128)S(1)} %pad_maximum_fusion.34), channel_id=1, source_target_pairs={{0,1},{1,0},{2,3},{3,2},{4,5},{5,4},{6,7},{7,6},{8,9},{9,8},{10,11... | collective-permute-start | bytes 36872 | tf_op jit(solution)/shard_map/ppermute | solution.py:39
  421.7 29.3 %collective-permute-start.59 = (bf16[2,48,2432]{2,1,0:T(8,128)(2,1)S(1)}, bf16[2,48,2432]{2,1,0:T(8,128)(2,1)S(1)}, u32[]{:S(2)}, u32[]{:S(2)}) collective-permute-start(bf16[2,48,2432]{2,1,0:T(8,128)(2,1)S(1)} %copy-done.86), channel_id=1, source_target_pairs={{0,16},{1,17},{2,18},{3,19},{4,20},{5,21},{6,22},{7,23},{8,24},{9,... | collective-permute-start | bytes 1400840 | tf_op jit(solution)/shard_map/ppermute | solution.py:39
  422.9 27.7 %collective-permute-start.60 = (bf16[128,384]{1,0:T(8,128)(2,1)S(1)}, bf16[128,384]{1,0:T(8,128)(2,1)S(1)}, u32[]{:S(2)}, u32[]{:S(2)}) collective-permute-start(bf16[128,384]{1,0:T(8,128)(2,1)S(1)} %fusion.11), channel_id=1, source_target_pairs={{0,2},{1,3},{2,0},{3,1},{4,6},{5,7},{6,4},{7,5},{8,10},{9,11},{10,... | collective-permute-start | bytes 294920 | tf_op jit(solution)/shard_map/ppermute | solution.py:39
  424.4 28.3 %collective-permute-start.58 = (bf16[4,48,1152]{2,1,0:T(8,128)(2,1)S(1)}, bf16[4,48,1152]{2,1,0:T(8,128)(2,1)S(1)}, u32[]{:S(2)}, u32[]{:S(2)}) collective-permute-start(bf16[4,48,1152]{2,1,0:T(8,128)(2,1)S(1)} %dynamic-slice_bitcast_fusion.3), channel_id=1, source_target_pairs={{0,2},{1,5},{2,0},{3,7},{4,6},{5,1},{6,4},{7,3},{8,10},{9,13},{10,... | collective-permute-start | bytes 1327112 | tf_op jit(solution)/shard_map/ppermute | solution.py:39
  452.9 21.4 %collective-permute-start.62 = (bf16[2,48,1152]{2,1,0:T(8,128)(2,1)S(1)}, bf16[2,48,1152]{2,1,0:T(8,128)(2,1)S(1)}, u32[]{:S(2)}, u32[]{:S(2)}) collective-permute-start(bf16[2,48,1152]{2,1,0:T(8,128)(2,1)S(1)} %constant_dynamic-slice_fusion.13), channel_id=1, source_target_pairs={{0,16},{1,17},{2,18},{3,19},{4,20},{5,21},{6,22},{7,23},{8,24},{9,... | collective-permute-start | bytes 663560 | tf_op jit(solution)/shard_map/ppermute | solution.py:39
  455.9 60.6 %collective-permute-start.68 = (bf16[48,2432]{1,0:T(8,128)(2,1)S(1)}, bf16[48,2432]{1,0:T(8,128)(2,1)S(1)}, u32[]{:S(2)}, u32[]{:S(2)}) collective-permute-start(bf16[48,2432]{1,0:T(8,128)(2,1)S(1)} %dynamic-slice_bitcast_fusion.7), channel_id=1, source_target_pairs={{0,8},{1,9},{2,10},{3,11},{4,12},{5,13},{6,14},{7,15},{8,0},{9,1},... | collective-permute-start | bytes 700424 | tf_op jit(solution)/shard_map/ppermute | solution.py:39
  455.9 61.9 %collective-permute-start.67 = (bf16[256,384]{1,0:T(8,128)(2,1)S(1)}, bf16[256,384]{1,0:T(8,128)(2,1)S(1)}, u32[]{:S(2)}, u32[]{:S(2)}) collective-permute-start(bf16[256,384]{1,0:T(8,128)(2,1)S(1)} %pad_maximum_fusion.30), channel_id=1, source_target_pairs={{0,1},{1,0},{2,3},{3,2},{4,5},{5,4},{6,7},{7,6},{8,9},{9,8},{10,11... | collective-permute-start | bytes 589832 | tf_op jit(solution)/shard_map/ppermute | solution.py:39
  457.0 35.4 %collective-permute-start.57 = (bf16[4,2,48,2432]{3,2,0,1:T(8,128)(2,1)S(1)}, bf16[4,2,48,2432]{3,2,0,1:T(8,128)(2,1)S(1)}, u32[]{:S(2)}, u32[]{:S(2)}) collective-permute-start(bf16[4,2,48,2432]{3,2,0,1:T(8,128)(2,1)S(1)} %bitcast_select_fusion), channel_id=1, source_target_pairs={{0,4},{1,3},{2,6},{3,1},{4,0},{5,7},{6,2},{7,5},{8,12},{9,11},{10,... | collective-permute-start | bytes 5603336 | tf_op jit(solution)/shard_map/ppermute | solution.py:39
  474.8 32.4 %collective-permute-start.64 = (bf16[4,128,384]{2,1,0:T(8,128)(2,1)S(1)}, bf16[4,128,384]{2,1,0:T(8,128)(2,1)S(1)}, u32[]{:S(2)}, u32[]{:S(2)}) collective-permute-start(bf16[4,128,384]{2,1,0:T(8,128)(2,1)S(1)} %dynamic-slice_bitcast_fusion.4), channel_id=1, source_target_pairs={{0,2},{1,5},{2,0},{3,7},{4,6},{5,1},{6,4},{7,3},{8,10},{9,13},{10,... | collective-permute-start | bytes 1179656 | tf_op jit(solution)/shard_map/ppermute | solution.py:39
  510.5 25.9 %collective-permute-start.79 = (bf16[2,128,384]{2,1,0:T(8,128)(2,1)S(1)}, bf16[2,128,384]{2,1,0:T(8,128)(2,1)S(1)}, u32[]{:S(2)}, u32[]{:S(2)}) collective-permute-start(bf16[2,128,384]{2,1,0:T(8,128)(2,1)S(1)} %constant_dynamic-slice_fusion.7), channel_id=1, source_target_pairs={{0,16},{1,17},{2,18},{3,19},{4,20},{5,21},{6,22},{7,23},{8,24},{9,... | collective-permute-start | bytes 589832 | tf_op jit(solution)/shard_map/ppermute | solution.py:39
  513.6 28.8 %collective-permute-start.75 = (bf16[2,48,2432]{2,1,0:T(8,128)(2,1)S(1)}, bf16[2,48,2432]{2,1,0:T(8,128)(2,1)S(1)}, u32[]{:S(2)}, u32[]{:S(2)}) collective-permute-start(bf16[2,48,2432]{2,1,0:T(8,128)(2,1)S(1)} %constant_dynamic-slice_fusion.8), channel_id=1, source_target_pairs={{0,16},{1,17},{2,18},{3,19},{4,20},{5,21},{6,22},{7,23},{8,24},{9,... | collective-permute-start | bytes 1400840 | tf_op jit(solution)/shard_map/ppermute | solution.py:39
  532.2 27.0 %collective-permute-start.91 = (bf16[96,2432]{1,0:T(8,128)(2,1)S(1)}, bf16[96,2432]{1,0:T(8,128)(2,1)S(1)}, u32[]{:S(2)}, u32[]{:S(2)}) collective-permute-start(bf16[96,2432]{1,0:T(8,128)(2,1)S(1)} %pad_maximum_fusion.12), channel_id=1, source_target_pairs={{0,1},{1,0},{2,3},{3,2},{4,5},{5,4},{6,7},{7,6},{8,9},{9,8},{10,11... | collective-permute-start | bytes 1400840 | tf_op jit(solution)/shard_map/ppermute | solution.py:39
  (179 other events, 2116.0 us)
Sparse Core Ops, SparseCore 0:
  69.0 75.8 all-gather.2
